TPU v7x, 512 devices: a whole 4x4x16 slice. The times are simulated.
512 devices in a mesh: cells: 16 (over y, z_lo), row: 4 (over z_hi), col: 8 (over x, core).
Axes of the slice: x: 4, y: 4, z: 16 (z_hi: 4, z_lo: 4; z = z_hi * 4 + z_lo), core: 2. Of those that a mesh axis runs over, the one named last changes fastest.
Arguments:
- snapshots: bfloat16 [2048, 131072], P('row', ('cells', 'col')), may hold values from -8 to 8
- snapshot_order: int32 [2048], replicated, may hold values from 0 to 2047, each once
Outputs:
- gram: float32 [2048, 2048], P('row', ('cells', 'col'))
All inputs are finite; a program needn't handle non-finite values.
Results may differ from a plain program's by a relative error of at most 0.0003.
Values may be sent and summed in bfloat16 or wider, within the bound.
No kernel may reach another device: no remote copies, remote signals or barrier semaphores. Data moves between devices by JAX's collectives and lax.ppermute only.
A program may use at most 64 MiB of HBM per device.

v0:
```python
import jax
import jax.numpy as jnp
from jax import lax
from jax.sharding import PartitionSpec as P


def local(snapshots, snapshot_order):
    everyone = lax.all_gather(snapshots, "row", axis=0, tiled=True)
    ordered = jnp.take(everyone, snapshot_order, axis=0)
    panel = ordered.shape[0] // lax.axis_size("row")
    own = lax.dynamic_slice_in_dim(ordered, lax.axis_index("row") * panel, panel, 0)
    groups = lax.axis_size(("cells", "col"))
    factor = 1.0 / (snapshots.shape[1] * groups)
    width = ordered.shape[0] // groups
    partial_value = (
        jnp.einsum("ic,jc->ij", own, ordered, preferred_element_type=jnp.float32) * factor
    )
    summed = lax.psum(partial_value, ("cells", "col"))
    return lax.dynamic_slice_in_dim(summed, lax.axis_index(("cells", "col")) * width, width, 1)


def solution(mesh):
    placed = (P("row", ("cells", "col")), P())
    return jax.shard_map(
        local, mesh=mesh, in_specs=placed, out_specs=P("row", ("cells", "col")), check_vma=False
    )
```

profile of v0, /device:TPU:6, one launch (start us, length us, event | category | flops | bytes accessed | tf_op | source)
XLA Modules:
  0.0 1508.0 jit_solution(6270238159481145694)
XLA Ops:
  6.5 0.0 all-gather.2.cloned.1.call-start
  6.5 0.7 all-gather.2.cloned.1.call-update
  7.3 0.0 all-reduce.2.cloned.1.call-start
  7.3 0.7 compare_and_fusion
  8.0 0.7 fusion.1
  8.7 168.1 %all-gather.2.cloned.1.call-done = bf16[2048,1024]{1,0:T(8,128)(2,1)} async-done(((bf16[512,1024]{1,0:T(8,128)(2,1)}), bf16[2048,1024]{1,0:T(8,128)(2,1)}) %all-gather.2.cloned.1.call-update) | async-done | bytes 4194320 | tf_op jit(solution)/shard_map/all_gather | solution.py:8
  176.8 13.8 gather_fusion
  190.6 2.5 broadcast_select_fusion
  193.1 4.4 convolution_multiply_fusion
  197.5 0.0 all-reduce.2.cloned.1.call-update
  197.5 1302.2 %all-reduce.2.cloned.1.call-done = f32[512,2048]{0,1:T(8,128)} async-done(((f32[512,2048]{0,1:T(8,128)}), f32[512,2048]{0,1:T(8,128)}) %all-reduce.2.cloned.1.call-update) | async-done | bytes 4194320 | tf_op jit(solution)/shard_map/psum | solution.py:18
  1499.8 1.4 constant_dynamic-slice_fusion
Async XLA Ops:
  6.5 170.3 %all-gather.2.cloned.1.call-start = ((), (), s32[]{:S(2)}) async-start(), calls=%async_computation | async-start | bytes 5242880 | tf_op jit(solution)/shard_map/all_gather | solution.py:8
  7.3 1492.5 %all-reduce.2.cloned.1.call-start = ((), (), s32[]{:S(2)}) async-start(), calls=%async_computation.1 | async-start | bytes 8388608 | tf_op jit(solution)/shard_map/psum | solution.py:18
Sparse Core Ops, SparseCore 0:
  9.5 167.3 all-gather.1
  197.6 1302.0 all-reduce.1
where the time goes:
time: 1530 us; the launch traced here: 1510 us
  waiting for transfers between devices  1470 us (96%)
    psum x1, waiting for transfers between devices, local(): summed = lax.psum(partial_value, ('cells', 'col'))  1300 us
    all_gather x1, waiting for transfers between devices, local(): everyone = lax.all_gather(snapshots, 'row', axis=0, tiled=True)  168 us
  transfers between devices with their start and end apart: 2, of which 2 were waited for; matrix products, arithmetic and copies ran while one was open for 0% of the time, Pallas kernels for 0%

commit v1 on v0

v1 whole, which is shorter than its diff:
```python
import jax
import jax.numpy as jnp
from jax import lax
from jax.sharding import Mesh, PartitionSpec as P


def shift(value, axis, by):
    n = lax.axis_size(axis)
    return lax.ppermute(value, axis, [(i, (i + by) % n) for i in range(n)])


def local(snapshots, snapshot_order):
    held, cells = snapshots.shape
    rows = lax.axis_size("row")
    total = held * rows
    devices = lax.axis_size(("y", "zl", "row", "x", "core"))
    factor = 1.0 / (cells * (devices // rows))
    part = cells // rows
    split = snapshots.reshape(held, rows, part).transpose(1, 0, 2)
    mine = lax.all_to_all(split, "row", 0, 0, tiled=False).reshape(total, part)
    pick = (snapshot_order[:, None] == lax.iota(jnp.int32, total)[None, :]).astype(jnp.bfloat16)
    mine = jnp.dot(pick, mine, preferred_element_type=jnp.float32).astype(jnp.bfloat16)
    own = [mine] + [shift(mine, "x", by) for by in (1, 3, 2)]
    pieces = own + [shift(p, "core", 1) for p in own]
    everything = jnp.concatenate(pieces, axis=1)
    sub = lax.axis_size("x") * lax.axis_size("core")
    width = total // (lax.axis_size(("y", "zl", "x", "core")))
    at = lax.axis_index(("x", "core"))
    chosen = everything.reshape(total // (sub * width), sub, width, everything.shape[1])
    chosen = lax.dynamic_index_in_dim(chosen, at, 1, keepdims=False).reshape(total // sub, -1)
    value = lax.dot_general(
        chosen, everything, (((1,), (1,)), ((), ())), preferred_element_type=jnp.float32
    )
    for axis in ("y", "zl"):
        n = lax.axis_size(axis)
        value = value.reshape(n, value.shape[0] // n, total)
        value = lax.all_to_all(value, axis, 0, 0, tiled=False).sum(0)
    value = value.reshape(width, rows, held).transpose(1, 0, 2)
    value = lax.all_to_all(value, "row", 0, 0, tiled=False).sum(0)
    return value.T * factor


def solution(mesh):
    fine = Mesh(mesh.devices.reshape(4, 4, 4, 4, 2), ("y", "zl", "row", "x", "core"))
    columns = ("y", "zl", "x", "core")
    return jax.shard_map(
        local, mesh=fine, in_specs=(P("row", columns), P()), out_specs=P("row", columns), check_vma=False
    )
```

time: 1530 us -> 229 us (0.15); the launches traced: 1510 us -> 228 us
  waiting for transfers between devices: 1470 us -> 39.2 us
  blocking collectives: 0 us -> 133 us
  starting transfers between devices: 0.04 us -> 17.3 us
    psum x1 -> x0, waiting for transfers between devices: 1300 us -> none  [local(): summed = lax.psum(partial_value, ('cells', 'col'))]
    all_gather x1 -> x0, waiting for transfers between devices: 168 us -> none  [local(): everyone = lax.all_gather(snapshots, 'row', axis=0, tiled=True)]
    all_to_all x0 -> x4, blocking collectives: none -> 133 us  [the longest x1 64.6 us: local(): mine = lax.all_to_all(split, 'row', 0, 0, tiled=False).reshape(total, part)]
    ppermute x0 -> x7, waiting for transfers between devices: none -> 39.2 us  [shift(): return lax.ppermute(value, axis, [(i, (i + by) % n) for i in range(n)])]
    ppermute x0 -> x7, starting transfers between devices: none -> 17.3 us  [shift(): return lax.ppermute(value, axis, [(i, (i + by) % n) for i in range(n)])]
  transfers between devices with their start and end apart: 2 -> 7, of which waited for: 2 -> 2; matrix products, arithmetic and copies ran while one was open for 0% -> 4% of each run, Pallas kernels for 0% -> 0%
where the time goes in v1:
time: 229 us; the launch traced here: 228 us
  blocking collectives  133 us (58%)
  waiting for transfers between devices  39.2 us (17%)
  local copies, waits for them, and re-layouts  25.8 us (11%)
  starting transfers between devices  17.3 us (8%)
  matrix products  11.5 us (5%)
    all_to_all x1, blocking collectives, local(): mine = lax.all_to_all(split, 'row', 0, 0, tiled=False).reshape(total, part)  64.6 us
    all_to_all x2, blocking collectives, local(): value = lax.all_to_all(value, axis, 0, 0, tiled=False).sum(0)  50.6 us
    ppermute x7, waiting for transfers between devices, shift(): return lax.ppermute(value, axis, [(i, (i + by) % n) for i in range(n)])  39.2 us
    all_to_all x1, blocking collectives, local(): value = lax.all_to_all(value, 'row', 0, 0, tiled=False).sum(0)  17.7 us
    ppermute x7, starting transfers between devices, shift(): return lax.ppermute(value, axis, [(i, (i + by) % n) for i in range(n)])  17.3 us
    concatenate x2, local copies, waits for them, and re-layouts, local(): everything = jnp.concatenate(pieces, axis=1)  13.4 us
    unnamed x7, local copies, waits for them, and re-layouts  10.4 us
    dot_general x1, matrix products, local(): jnp.dot(pick, mine, preferred_element_type=jnp.float32).astype(jnp.bfloat16)  5.81 us
  transfers between devices with their start and end apart: 7, of which 2 were waited for; matrix products, arithmetic and copies ran while one was open for 4% of the time, Pallas kernels for 0%

profile of v1, /device:TPU:6, one launch (start us, length us, event | category | flops | bytes accessed | tf_op | source)
XLA Modules:
  0.0 227.7 jit_solution(4267221176050127653)
XLA Ops:
  0.0 1.5 copy.20
  1.5 64.6 %all_to_all.20 = bf16[4,512,256]{1,2,0:T(8,128)(2,1)S(1)} all-to-all(bf16[4,512,256]{1,2,0:T(8,128)(2,1)S(1)} %bitcast.16), channel_id=1, replica_groups=mesh['y'=4,'zl'=4,'row'=4,'x'=4,'core'=2] {'row'}, dimensions={0} | all-to-all | bytes 2097152 | tf_op jit(solution)/shard_map/all_to_all | solution.py:20
  66.6 5.8 %constant_dynamic-update-slice_fusion.7 = (bf16[2048,2048]{0,1:T(8,128)(2,1)}, bf16[2048,256]{0,1:T(8,128)(2,1)}) fusion(bf16[2048,256]{1,0:T(8,128)(2,1)S(1)} %bitcast.19, s32[2048]{0:T(1024)} %param.3), kind=kOutput, calls=%fused_computation.14 | convolution fusion | flops 2152202240 | bytes 3153920 | tf_op jit(solution)/shard_map/dot_general | solution.py:22
  72.4 2.4 %collective-permute-start = (bf16[2048,256]{0,1:T(8,128)(2,1)}, bf16[2048,256]{0,1:T(8,128)(2,1)S(1)}, u32[]{:S(2)}, u32[]{:S(2)}) collective-permute-start(bf16[2048,256]{0,1:T(8,128)(2,1)} %get-tuple-element.6), channel_id=1, source_target_pairs={{0,2},{2,4},{4,6},{6,0},{1,3},{3,5},{5,7},{7,1},{8,10},{10,12},{12... | collective-permute-start | bytes 3145736 | tf_op jit(solution)/shard_map/ppermute | solution.py:9
  74.8 3.5 %collective-permute-start.1 = (bf16[2048,256]{0,1:T(8,128)(2,1)}, bf16[2048,256]{0,1:T(8,128)(2,1)S(1)}, u32[]{:S(2)}, u32[]{:S(2)}) collective-permute-start(bf16[2048,256]{0,1:T(8,128)(2,1)} %get-tuple-element.6), channel_id=1, source_target_pairs={{0,6},{2,0},{4,2},{6,4},{1,7},{3,1},{5,3},{7,5},{8,14},{10,8},{12,... | collective-permute-start | bytes 3145736 | tf_op jit(solution)/shard_map/ppermute | solution.py:9
  78.3 3.3 %collective-permute-start.2 = (bf16[2048,256]{0,1:T(8,128)(2,1)}, bf16[2048,256]{0,1:T(8,128)(2,1)S(1)}, u32[]{:S(2)}, u32[]{:S(2)}) collective-permute-start(bf16[2048,256]{0,1:T(8,128)(2,1)} %get-tuple-element.6), channel_id=1, source_target_pairs={{0,4},{2,6},{4,0},{6,2},{1,5},{3,7},{5,1},{7,3},{8,12},{10,14},{12... | collective-permute-start | bytes 3145736 | tf_op jit(solution)/shard_map/ppermute | solution.py:9
  81.6 1.9 collective-permute-start.3
  83.5 17.1 %collective-permute-done = bf16[2048,256]{0,1:T(8,128)(2,1)S(1)} collective-permute-done((bf16[2048,256]{0,1:T(8,128)(2,1)}, bf16[2048,256]{0,1:T(8,128)(2,1)S(1)}, u32[]{:S(2)}, u32[]{:S(2)}) %collective-permute-start) | collective-permute-done | bytes 1048608 | tf_op jit(solution)/shard_map/ppermute | solution.py:9
  100.6 1.9 collective-permute-start.4
  102.5 22.1 %collective-permute-done.1 = bf16[2048,256]{0,1:T(8,128)(2,1)S(1)} collective-permute-done((bf16[2048,256]{0,1:T(8,128)(2,1)}, bf16[2048,256]{0,1:T(8,128)(2,1)S(1)}, u32[]{:S(2)}, u32[]{:S(2)}) %collective-permute-start.1) | collective-permute-done | bytes 1048608 | tf_op jit(solution)/shard_map/ppermute | solution.py:9
  124.6 1.9 collective-permute-start.5
  126.5 1.1 constant_dynamic-update-slice_fusion.6
  127.6 2.4 %collective-permute-start.6 = (bf16[2048,256]{0,1:T(8,128)(2,1)S(1)}, bf16[2048,256]{0,1:T(8,128)(2,1)S(1)}, u32[]{:S(2)}, u32[]{:S(2)}) collective-permute-start(bf16[2048,256]{0,1:T(8,128)(2,1)S(1)} %collective-permute-done.2), channel_id=1, source_target_pairs={{0,1},{1,0},{2,3},{3,2},{4,5},{5,4},{6,7},{7,6},{8,9},{9,8},{10,11... | collective-permute-start | bytes 3145736 | tf_op jit(solution)/shard_map/ppermute | solution.py:9
  130.1 1.1 constant_dynamic-update-slice_fusion.5
  131.1 1.1 constant_dynamic-update-slice_fusion.4
  132.2 2.3 %constant_dynamic-update-slice_fusion.3 = bf16[2048,2048]{0,1:T(8,128)(2,1)} fusion(bf16[2048,2048]{0,1:T(8,128)(2,1)} %constant_dynamic-update-slice_fusion.4, bf16[2048,256]{0,1:T(8,128)(2,1)} %collective-permute-done.3), kind=kLoop, calls=%fused_computation.10 | loop fusion | bytes 2097152
  134.5 2.4 %constant_dynamic-update-slice_fusion.2 = bf16[2048,2048]{0,1:T(8,128)(2,1)} fusion(bf16[2048,2048]{0,1:T(8,128)(2,1)} %constant_dynamic-update-slice_fusion.3, bf16[2048,256]{0,1:T(8,128)(2,1)} %collective-permute-done.4), kind=kLoop, calls=%fused_computation.9 | loop fusion | bytes 2097152
  136.8 1.1 constant_dynamic-update-slice_fusion.1
  138.9 12.3 %copy.22 = bf16[2048,2048]{1,0:T(8,128)(2,1)} copy(bf16[2048,2048]{0,1:T(8,128)(2,1)} %constant_dynamic-update-slice_fusion) | data formatting | bytes 16777216 | tf_op jit(solution)/shard_map/concatenate | solution.py:25
  151.3 1.3 constant_dynamic-slice_fusion
  152.6 5.7 %fusion.1 = f32[4,64,2048]{2,1,0:T(8,128)S(1)} fusion(bf16[4,64,2048]{2,1,0:T(8,128)(2,1)S(1)} %bitcast.18, bf16[2048,2048]{0,1:T(8,128)(2,1)} %constant_dynamic-update-slice_fusion), kind=kOutput, calls=%fused_computation.2 | convolution fusion | flops 2147483648 | bytes 11534336 | tf_op jit(solution)/shard_map/dot_general | solution.py:31
  158.3 30.8 %all_to_all.21 = f32[4,64,2048]{2,1,0:T(8,128)S(1)} all-to-all(f32[4,64,2048]{2,1,0:T(8,128)S(1)} %fusion.1), channel_id=1, replica_groups=mesh['y'=4,'zl'=4,'row'=4,'x'=4,'core'=2] {'y'}, dimensions={0} | all-to-all | bytes 4194304 | tf_op jit(solution)/shard_map/all_to_all | solution.py:37
  189.3 19.8 %all_to_all.22 = f32[4,16,2048]{2,1,0:T(8,128)S(1)} all-to-all(f32[4,16,2048]{2,1,0:T(8,128)S(1)} %bitcast.17), channel_id=1, replica_groups=mesh['y'=4,'zl'=4,'row'=4,'x'=4,'core'=2] {'zl'}, dimensions={0} | all-to-all | bytes 1048576 | tf_op jit(solution)/shard_map/all_to_all | solution.py:37
  209.3 17.7 %all_to_all.23 = f32[4,16,512]{2,1,0:T(8,128)S(1)} all-to-all(f32[4,16,512]{2,1,0:T(8,128)S(1)} %copy.24), channel_id=1, replica_groups=mesh['y'=4,'zl'=4,'row'=4,'x'=4,'core'=2] {'row'}, dimensions={0} | all-to-all | bytes 262144 | tf_op jit(solution)/shard_map/all_to_all | solution.py:39
  (13 shorter events, 2.5 us)
Async XLA Ops:
  72.4 28.2 %collective-permute-start = (bf16[2048,256]{0,1:T(8,128)(2,1)}, bf16[2048,256]{0,1:T(8,128)(2,1)S(1)}, u32[]{:S(2)}, u32[]{:S(2)}) collective-permute-start(bf16[2048,256]{0,1:T(8,128)(2,1)} %get-tuple-element.6), channel_id=1, source_target_pairs={{0,2},{2,4},{4,6},{6,0},{1,3},{3,5},{5,7},{7,1},{8,10},{10,12},{12... | collective-permute-start | bytes 3145736 | tf_op jit(solution)/shard_map/ppermute | solution.py:9
  74.8 49.8 %collective-permute-start.1 = (bf16[2048,256]{0,1:T(8,128)(2,1)}, bf16[2048,256]{0,1:T(8,128)(2,1)S(1)}, u32[]{:S(2)}, u32[]{:S(2)}) collective-permute-start(bf16[2048,256]{0,1:T(8,128)(2,1)} %get-tuple-element.6), channel_id=1, source_target_pairs={{0,6},{2,0},{4,2},{6,4},{1,7},{3,1},{5,3},{7,5},{8,14},{10,8},{12,... | collective-permute-start | bytes 3145736 | tf_op jit(solution)/shard_map/ppermute | solution.py:9
  78.3 49.4 %collective-permute-start.2 = (bf16[2048,256]{0,1:T(8,128)(2,1)}, bf16[2048,256]{0,1:T(8,128)(2,1)S(1)}, u32[]{:S(2)}, u32[]{:S(2)}) collective-permute-start(bf16[2048,256]{0,1:T(8,128)(2,1)} %get-tuple-element.6), channel_id=1, source_target_pairs={{0,4},{2,6},{4,0},{6,2},{1,5},{3,7},{5,1},{7,3},{8,12},{10,14},{12... | collective-permute-start | bytes 3145736 | tf_op jit(solution)/shard_map/ppermute | solution.py:9
  81.6 50.6 %collective-permute-start.3 = (bf16[2048,256]{0,1:T(8,128)(2,1)}, bf16[2048,256]{0,1:T(8,128)(2,1)}, u32[]{:S(2)}, u32[]{:S(2)}) collective-permute-start(bf16[2048,256]{0,1:T(8,128)(2,1)} %get-tuple-element.6), channel_id=1, source_target_pairs={{0,1},{1,0},{2,3},{3,2},{4,5},{5,4},{6,7},{7,6},{8,9},{9,8},{10,11... | collective-permute-start | bytes 3145736 | tf_op jit(solution)/shard_map/ppermute | solution.py:9
  100.6 33.9 %collective-permute-start.4 = (bf16[2048,256]{0,1:T(8,128)(2,1)S(1)}, bf16[2048,256]{0,1:T(8,128)(2,1)}, u32[]{:S(2)}, u32[]{:S(2)}) collective-permute-start(bf16[2048,256]{0,1:T(8,128)(2,1)S(1)} %collective-permute-done), channel_id=1, source_target_pairs={{0,1},{1,0},{2,3},{3,2},{4,5},{5,4},{6,7},{7,6},{8,9},{9,8},{10,11... | collective-permute-start | bytes 3145736 | tf_op jit(solution)/shard_map/ppermute | solution.py:9
  124.6 12.2 %collective-permute-start.5 = (bf16[2048,256]{0,1:T(8,128)(2,1)S(1)}, bf16[2048,256]{0,1:T(8,128)(2,1)S(1)}, u32[]{:S(2)}, u32[]{:S(2)}) collective-permute-start(bf16[2048,256]{0,1:T(8,128)(2,1)S(1)} %collective-permute-done.1), channel_id=1, source_target_pairs={{0,1},{1,0},{2,3},{3,2},{4,5},{5,4},{6,7},{7,6},{8,9},{9,8},{10,11... | collective-permute-start | bytes 3145736 | tf_op jit(solution)/shard_map/ppermute | solution.py:9
  127.6 10.3 %collective-permute-start.6 = (bf16[2048,256]{0,1:T(8,128)(2,1)S(1)}, bf16[2048,256]{0,1:T(8,128)(2,1)S(1)}, u32[]{:S(2)}, u32[]{:S(2)}) collective-permute-start(bf16[2048,256]{0,1:T(8,128)(2,1)S(1)} %collective-permute-done.2), channel_id=1, source_target_pairs={{0,1},{1,0},{2,3},{3,2},{4,5},{5,4},{6,7},{7,6},{8,9},{9,8},{10,11... | collective-permute-start | bytes 3145736 | tf_op jit(solution)/shard_map/ppermute | solution.py:9

commit v2 on v0

v2 whole, which is shorter than its diff:
```python
import functools

import jax
import jax.numpy as jnp
from jax import lax
from jax.experimental import pallas as pl
from jax.experimental.pallas import tpu as pltpu
from jax.sharding import Mesh, PartitionSpec as P

Y, ZL, ROW, X, CORE = 4, 4, 4, 4, 2
CHUNKS = 2
VMEM_BYTES = 40 * 1024 * 1024
STEPS = (1, 3, 2)


def shift(value, axis, by):
    n = lax.axis_size(axis)
    return lax.ppermute(value, axis, [(i, (i + by) % n) for i in range(n)])


def params():
    return pltpu.CompilerParams(vmem_limit_bytes=VMEM_BYTES)


def split_kernel(place, source, *outs):
    row = place[0]
    width = outs[0].shape[1]
    for chunk in range(CHUNKS):
        for k in range(ROW):
            start = lax.rem(row + k, ROW) * (width * CHUNKS) + chunk * width
            outs[chunk * ROW + k][...] = source[:, pl.ds(pl.multiple_of(start, width), width)]


def split(place, snapshots):
    held, cells = snapshots.shape
    width = cells // (ROW * CHUNKS)
    return pl.pallas_call(
        split_kernel,
        out_shape=[jax.ShapeDtypeStruct((held, width), snapshots.dtype)] * (CHUNKS * ROW),
        in_specs=[pl.BlockSpec(memory_space=pltpu.SMEM), pl.BlockSpec(memory_space=pltpu.VMEM)],
        out_specs=[pl.BlockSpec(memory_space=pltpu.VMEM)] * (CHUNKS * ROW),
        compiler_params=params(),
        name="split_cells",
    )(place, snapshots)


def order_kernel(index, *refs):
    pieces, out = refs[:-1], refs[-1]
    block = 256
    held = pieces[0].shape[0]
    for at in range(0, out.shape[0], block):
        wanted = index[at : at + block, :]
        value = None
        for k, piece in enumerate(pieces):
            row = lax.broadcasted_iota(jnp.int32, (block, held), 1) + k * held
            pick = jnp.where(wanted == row, 1.0, 0.0).astype(jnp.bfloat16)
            term = jnp.dot(pick, piece[...], preferred_element_type=jnp.float32)
            value = term if value is None else value + term
        out[at : at + block, :] = value.astype(out.dtype)


def in_order(index, pieces):
    total = index.shape[0]
    width = pieces[0].shape[1]
    return pl.pallas_call(
        order_kernel,
        out_shape=jax.ShapeDtypeStruct((total, width), pieces[0].dtype),
        in_specs=[pl.BlockSpec(memory_space=pltpu.VMEM)] * (1 + len(pieces)),
        out_specs=pl.BlockSpec(memory_space=pltpu.VMEM),
        compiler_params=params(),
        cost_estimate=pl.CostEstimate(
            flops=2 * total * total * width, bytes_accessed=4 * total * width, transcendentals=0
        ),
        name="rows_in_order",
    )(index, *pieces)


D_ORDER = (2, 1, 3, 0)


def panel_kernel(count, place, *refs):
    pieces, outs, chosen = refs[:count], refs[count:-1], refs[-1]
    y, zl, row, x, core = (place[i] for i in (1, 2, 0, 3, 4))
    width = pieces[0].shape[1]
    total = pieces[0].shape[0]
    unit = total // (Y * ZL * X * CORE)
    step = pl.program_id(0)

    @pl.when(step == 0)
    def _():
        for part in range(CORE):
            to_core = lax.rem(core + 1 - part, CORE)
            for d_at, d in enumerate(D_ORDER):
                for k in range(ZL):
                    to_y, to_zl = lax.rem(y + d, Y), lax.rem(zl + k, ZL)
                    start = (((to_y * ZL + to_zl) * X + x) * CORE + to_core) * unit
                    at = ((part * Y + d_at) * ZL + k) * unit
                    for p, piece in enumerate(pieces):
                        chosen[at : at + unit, p * width : (p + 1) * width] = piece[
                            pl.ds(pl.multiple_of(start, unit), unit), :
                        ]

    columns = outs[0].shape[1]
    per_row = total // ROW // columns
    start = lax.rem(row + step // per_row, ROW) * (total // ROW) + lax.rem(step, per_row) * columns
    rows = pl.ds(pl.multiple_of(start, columns), columns)
    right = jnp.concatenate([piece[rows, :] for piece in pieces], axis=1)
    value = lax.dot_general(
        chosen[...], right, (((1,), (1,)), ((), ())), preferred_element_type=jnp.float32
    )
    at = 0
    for out in outs:
        out[...] = value[at : at + out.shape[0], :]
        at += out.shape[0]


def panel(place, pieces):
    total, width = pieces[0].shape
    columns = 256
    height = total // (Y * X * CORE)
    heights = [height, 2 * height, height] * CORE
    depth = width * len(pieces)
    return pl.pallas_call(
        functools.partial(panel_kernel, len(pieces)),
        grid=(total // columns,),
        out_shape=[jax.ShapeDtypeStruct((h, total), jnp.float32) for h in heights],
        in_specs=[pl.BlockSpec(memory_space=pltpu.SMEM)]
        + [pl.BlockSpec(memory_space=pltpu.VMEM)] * len(pieces),
        out_specs=[pl.BlockSpec((h, columns), lambda i: (0, i)) for h in heights],
        scratch_shapes=[pltpu.VMEM((total // X, depth), pieces[0].dtype)],
        compiler_params=params(),
        cost_estimate=pl.CostEstimate(
            flops=2 * total * (total // X) * depth,
            bytes_accessed=2 * total * depth + 4 * total * (total // X),
            transcendentals=0,
        ),
        name="gram_panel",
    )(place, *pieces)


def local(snapshots, snapshot_order):
    held, cells = snapshots.shape
    total = held * ROW
    factor = 1.0 / (cells * Y * ZL * X * CORE)
    row = lax.axis_index("row")
    place = jnp.stack([row] + [lax.axis_index(a) for a in ("y", "zl", "x", "core")])
    index = lax.rem(row - snapshot_order // held + ROW, ROW) * held + snapshot_order % held
    index = index.reshape(total, 1)
    parts = split(place, snapshots)
    pieces = []
    for chunk in range(CHUNKS):
        sent = parts[chunk * ROW : (chunk + 1) * ROW]
        got = {k: shift(sent[k], "row", k) for k in STEPS}
        mine = in_order(index, [sent[0]] + [got[k] for k in (1, 2, 3)])
        pieces += [mine] + [shift(mine, "x", by) for by in STEPS]
    far, near, own, keep_far, keep_near, keep_own = panel(place, pieces)
    height = far.shape[0]
    far = keep_far + shift(far, "core", 1)
    near = keep_near + shift(near, "core", 1)
    own = keep_own + shift(own, "core", 1)
    value = (
        own
        + shift(near[:height], "y", 1)
        + shift(near[height:], "y", 3)
        + shift(far, "y", 2)
    )
    unit = height // ZL
    value = value[:unit] + sum(shift(value[k * unit : (k + 1) * unit], "zl", k) for k in STEPS)
    value = value[:, :held] + sum(
        shift(value[:, k * held : (k + 1) * held], "row", k) for k in STEPS
    )
    return value.T * factor


def solution(mesh):
    fine = Mesh(mesh.devices.reshape(Y, ZL, ROW, X, CORE), ("y", "zl", "row", "x", "core"))
    columns = ("y", "zl", "x", "core")
    return jax.shard_map(
        local, mesh=fine, in_specs=(P("row", columns), P()), out_specs=P("row", columns), check_vma=False
    )
```

time: 1530 us -> 198 us (0.13); the launches traced: 1510 us -> 195 us
  waiting for transfers between devices: 1470 us -> 64.3 us
  starting transfers between devices: 0.04 us -> 117 us
    psum x1 -> x0, waiting for transfers between devices: 1300 us -> none  [local(): summed = lax.psum(partial_value, ('cells', 'col'))]
    all_gather x1 -> x0, waiting for transfers between devices: 168 us -> none  [local(): everyone = lax.all_gather(snapshots, 'row', axis=0, tiled=True)]
    ppermute x0 -> x24, starting transfers between devices: none -> 117 us  [shift(): return lax.ppermute(value, axis, [(i, (i + by) % n) for i in range(n)])]
    ppermute x0 -> x24, waiting for transfers between devices: none -> 64.3 us  [shift(): return lax.ppermute(value, axis, [(i, (i + by) % n) for i in range(n)])]
  transfers between devices with their start and end apart: 2 -> 24, of which waited for: 2 -> 11; matrix products, arithmetic and copies ran while one was open for 0% -> 0% of each run, Pallas kernels for 0% -> 1%
where the time goes in v2:
time: 198 us; the launch traced here: 195 us
  starting transfers between devices  117 us (59%)
  waiting for transfers between devices  64.3 us (32%)
  Pallas kernels  11 us (6%)
    ppermute x24, starting transfers between devices, shift(): return lax.ppermute(value, axis, [(i, (i + by) % n) for i in range(n)])  117 us
    ppermute x24, waiting for transfers between devices, shift(): return lax.ppermute(value, axis, [(i, (i + by) % n) for i in range(n)])  64.3 us
    pallas_call x1, Pallas kernels, panel(): pl.pallas_call(functools.partial(panel_kernel, len(pieces)), grid=(total...  5.42 us
    pallas_call x2, Pallas kernels, in_order(): pl.pallas_call(order_kernel, out_shape=jax.ShapeDtypeStruct((total, width...  4.81 us
  transfers between devices with their start and end apart: 24, of which 11 were waited for; matrix products, arithmetic and copies ran while one was open for 0% of the time, Pallas kernels for 1%

profile of v2, /device:TPU:6, one launch (start us, length us, event | category | flops | bytes accessed | tf_op | source)
XLA Modules:
  0.0 195.4 jit_solution(1122059175874633343)
XLA Ops:
  2.1 9.1 %collective-permute-start.6 = (bf16[512,128]{1,0:T(8,128)(2,1)S(1)}, bf16[512,128]{1,0:T(8,128)(2,1)S(1)}, u32[]{:S(2)}, u32[]{:S(2)}) collective-permute-start(bf16[512,128]{1,0:T(8,128)(2,1)S(1)} %get-tuple-element.24), channel_id=1, source_target_pairs={{0,8},{8,16},{16,24},{24,0},{1,9},{9,17},{17,25},{25,1},{2,10},{10... | collective-permute-start | bytes 393224 | tf_op jit(solution)/shard_map/ppermute | solution.py:18
  11.2 10.9 %collective-permute-start.7 = (bf16[512,128]{1,0:T(8,128)(2,1)S(1)}, bf16[512,128]{1,0:T(8,128)(2,1)S(1)}, u32[]{:S(2)}, u32[]{:S(2)}) collective-permute-start(bf16[512,128]{1,0:T(8,128)(2,1)S(1)} %get-tuple-element.25), channel_id=1, source_target_pairs={{0,16},{8,24},{16,0},{24,8},{1,17},{9,25},{17,1},{25,9},{2,18},{10... | collective-permute-start | bytes 393224 | tf_op jit(solution)/shard_map/ppermute | solution.py:18
  22.2 5.5 %collective-permute-start.8 = (bf16[512,128]{1,0:T(8,128)(2,1)S(1)}, bf16[512,128]{1,0:T(8,128)(2,1)S(1)}, u32[]{:S(2)}, u32[]{:S(2)}) collective-permute-start(bf16[512,128]{1,0:T(8,128)(2,1)S(1)} %get-tuple-element.26), channel_id=1, source_target_pairs={{0,24},{8,0},{16,8},{24,16},{1,25},{9,1},{17,9},{25,17},{2,26},{10... | collective-permute-start | bytes 393224 | tf_op jit(solution)/shard_map/ppermute | solution.py:18
  28.1 11.7 %collective-permute-done.7.refs_2_ = bf16[512,128]{1,0:T(8,128)(2,1)S(1)} collective-permute-done((bf16[512,128]{1,0:T(8,128)(2,1)S(1)}, bf16[512,128]{1,0:T(8,128)(2,1)S(1)}, u32[]{:S(2)}, u32[]{:S(2)}) %collective-permute-start.7) | collective-permute-done | bytes 131104 | tf_op jit(solution)/shard_map/ppermute | solution.py:18
  39.8 5.9 %collective-permute-done.8.refs_3_ = bf16[512,128]{1,0:T(8,128)(2,1)S(1)} collective-permute-done((bf16[512,128]{1,0:T(8,128)(2,1)S(1)}, bf16[512,128]{1,0:T(8,128)(2,1)S(1)}, u32[]{:S(2)}, u32[]{:S(2)}) %collective-permute-start.8) | collective-permute-done | bytes 131104 | tf_op jit(solution)/shard_map/ppermute | solution.py:18
  55.2 10.7 %collective-permute-start.1 = (bf16[512,128]{1,0:T(8,128)(2,1)S(1)}, bf16[512,128]{1,0:T(8,128)(2,1)S(1)}, u32[]{:S(2)}, u32[]{:S(2)}) collective-permute-start(bf16[512,128]{1,0:T(8,128)(2,1)S(1)} %get-tuple-element.21), channel_id=1, source_target_pairs={{0,16},{8,24},{16,0},{24,8},{1,17},{9,25},{17,1},{25,9},{2,18},{10... | collective-permute-start | bytes 393224 | tf_op jit(solution)/shard_map/ppermute | solution.py:18
  65.8 5.5 %collective-permute-start.2 = (bf16[512,128]{1,0:T(8,128)(2,1)S(1)}, bf16[512,128]{1,0:T(8,128)(2,1)S(1)}, u32[]{:S(2)}, u32[]{:S(2)}) collective-permute-start(bf16[512,128]{1,0:T(8,128)(2,1)S(1)} %get-tuple-element.22), channel_id=1, source_target_pairs={{0,24},{8,0},{16,8},{24,16},{1,25},{9,1},{17,9},{25,17},{2,26},{10... | collective-permute-start | bytes 393224 | tf_op jit(solution)/shard_map/ppermute | solution.py:18
  73.3 5.1 %collective-permute-start.9 = (bf16[2048,128]{1,0:T(8,128)(2,1)S(1)}, bf16[2048,128]{1,0:T(8,128)(2,1)S(1)}, u32[]{:S(2)}, u32[]{:S(2)}) collective-permute-start(bf16[2048,128]{1,0:T(8,128)(2,1)S(1)} %rows_in_order.3.refs_4_), channel_id=1, source_target_pairs={{0,2},{2,4},{4,6},{6,0},{1,3},{3,5},{5,7},{7,1},{8,10},{10,12},{12... | collective-permute-start | bytes 1572872 | tf_op jit(solution)/shard_map/ppermute | solution.py:18
  81.9 4.0 %collective-permute-start.5 = (bf16[2048,128]{1,0:T(8,128)(2,1)S(1)}, bf16[2048,128]{1,0:T(8,128)(2,1)S(1)}, u32[]{:S(2)}, u32[]{:S(2)}) collective-permute-start(bf16[2048,128]{1,0:T(8,128)(2,1)S(1)} %rows_in_order.2.refs_0_), channel_id=1, source_target_pairs={{0,4},{2,6},{4,0},{6,2},{1,5},{3,7},{5,1},{7,3},{8,12},{10,14},{12... | collective-permute-start | bytes 1572872 | tf_op jit(solution)/shard_map/ppermute | solution.py:18
  88.7 4.3 %collective-permute-start.3 = (bf16[2048,128]{1,0:T(8,128)(2,1)S(1)}, bf16[2048,128]{1,0:T(8,128)(2,1)S(1)}, u32[]{:S(2)}, u32[]{:S(2)}) collective-permute-start(bf16[2048,128]{1,0:T(8,128)(2,1)S(1)} %rows_in_order.2.refs_0_), channel_id=1, source_target_pairs={{0,2},{2,4},{4,6},{6,0},{1,3},{3,5},{5,7},{7,1},{8,10},{10,12},{12... | collective-permute-start | bytes 1572872 | tf_op jit(solution)/shard_map/ppermute | solution.py:18
  93.0 7.9 %collective-permute-done.9.refs_5_ = bf16[2048,128]{1,0:T(8,128)(2,1)S(1)} collective-permute-done((bf16[2048,128]{1,0:T(8,128)(2,1)S(1)}, bf16[2048,128]{1,0:T(8,128)(2,1)S(1)}, u32[]{:S(2)}, u32[]{:S(2)}) %collective-permute-start.9) | collective-permute-done | bytes 524320 | tf_op jit(solution)/shard_map/ppermute | solution.py:18
  100.9 9.4 %collective-permute-done.4.refs_2_ = bf16[2048,128]{1,0:T(8,128)(2,1)S(1)} collective-permute-done((bf16[2048,128]{1,0:T(8,128)(2,1)S(1)}, bf16[2048,128]{1,0:T(8,128)(2,1)S(1)}, u32[]{:S(2)}, u32[]{:S(2)}) %collective-permute-start.4) | collective-permute-done | bytes 524320 | tf_op jit(solution)/shard_map/ppermute | solution.py:18
  110.9 5.4 %gram_panel.1 = (f32[64,2048]{1,0:T(8,128)S(1)}, f32[128,2048]{1,0:T(8,128)S(1)}, f32[64,2048]{1,0:T(8,128)S(1)}, f32[64,2048]{1,0:T(8,128)S(1)}, f32[128,2048]{1,0:T(8,128)S(1)}, /*index=5*/f32[64,2048]{1,0:T(8,128)S(1)}) custom-call(s32[5]{0:T(128)S(1)} %stack.23.place, bf16[2048,128]{1,0:T(8,128)(2,1)S(1)} %rows_in_order.2.refs_0_, ...), custom_call_target="tpu_custom_call" | custom-call | flops 2147483648 | bytes 8388608 | tf_op jit(solution)/shard_map/gram_panel/pallas_call | solution.py:123
  122.6 5.1 %collective-permute-start.17 = (f32[64,2048]{1,0:T(8,128)S(1)}, f32[64,2048]{1,0:T(8,128)S(1)}, u32[]{:S(2)}, u32[]{:S(2)}) collective-permute-start(f32[64,2048]{1,0:T(8,128)S(1)} %add.56), channel_id=1, source_target_pairs={{0,256},{128,384},{256,0},{384,128},{1,257},{129,385},{257,1},{385... | collective-permute-start | bytes 1572872 | tf_op jit(solution)/shard_map/ppermute | solution.py:18
  130.6 4.5 %collective-permute-start.15 = (f32[64,2048]{1,0:T(8,128)S(1)}, f32[64,2048]{1,0:T(8,128)S(1)}, u32[]{:S(2)}, u32[]{:S(2)}) collective-permute-start(f32[64,2048]{1,0:T(8,128)S(1)} %get-tuple-element.34), channel_id=1, source_target_pairs={{0,384},{128,0},{256,128},{384,256},{1,385},{129,1},{257,129},{385... | collective-permute-start | bytes 1572872 | tf_op jit(solution)/shard_map/ppermute | solution.py:18
  135.1 5.7 %collective-permute-done.17 = f32[64,2048]{1,0:T(8,128)S(1)} collective-permute-done((f32[64,2048]{1,0:T(8,128)S(1)}, f32[64,2048]{1,0:T(8,128)S(1)}, u32[]{:S(2)}, u32[]{:S(2)}) %collective-permute-start.17) | collective-permute-done | bytes 524320 | tf_op jit(solution)/shard_map/ppermute | solution.py:18
  140.8 10.8 %collective-permute-done.14 = f32[64,2048]{1,0:T(8,128)S(1)} collective-permute-done((f32[64,2048]{1,0:T(8,128)S(1)}, f32[64,2048]{1,0:T(8,128)S(1)}, u32[]{:S(2)}, u32[]{:S(2)}) %collective-permute-start.14) | collective-permute-done | bytes 524320 | tf_op jit(solution)/shard_map/ppermute | solution.py:18
  154.1 4.9 %collective-permute-start.20 = (f32[16,2048]{1,0:T(8,128)S(1)}, f32[16,2048]{1,0:T(8,128)S(1)}, u32[]{:S(2)}, u32[]{:S(2)}) collective-permute-start(f32[16,2048]{1,0:T(8,128)S(1)} %get-tuple-element.36), channel_id=1, source_target_pairs={{0,64},{32,96},{64,0},{96,32},{1,65},{33,97},{65,1},{97,33},{2,66}... | collective-permute-start | bytes 393224 | tf_op jit(solution)/shard_map/ppermute | solution.py:18
  159.0 3.9 %collective-permute-start.18 = (f32[16,2048]{1,0:T(8,128)S(1)}, f32[16,2048]{1,0:T(8,128)S(1)}, u32[]{:S(2)}, u32[]{:S(2)}) collective-permute-start(f32[16,2048]{1,0:T(8,128)S(1)} %get-tuple-element.37), channel_id=1, source_target_pairs={{0,32},{32,64},{64,96},{96,0},{1,33},{33,65},{65,97},{97,1},{2,34}... | collective-permute-start | bytes 393224 | tf_op jit(solution)/shard_map/ppermute | solution.py:18
  163.0 5.9 %collective-permute-done.20 = f32[16,2048]{1,0:T(8,128)S(1)} collective-permute-done((f32[16,2048]{1,0:T(8,128)S(1)}, f32[16,2048]{1,0:T(8,128)S(1)}, u32[]{:S(2)}, u32[]{:S(2)}) %collective-permute-start.20) | collective-permute-done | bytes 131104 | tf_op jit(solution)/shard_map/ppermute | solution.py:18
  168.9 6.4 %collective-permute-start.22 = (f32[16,512]{1,0:T(8,128)S(1)}, f32[16,512]{1,0:T(8,128)S(1)}, u32[]{:S(2)}, u32[]{:S(2)}) collective-permute-start(f32[16,512]{1,0:T(8,128)S(1)} %get-tuple-element.38), channel_id=1, source_target_pairs={{0,24},{8,0},{16,8},{24,16},{1,25},{9,1},{17,9},{25,17},{2,26},{10... | collective-permute-start | bytes 98312 | tf_op jit(solution)/shard_map/ppermute | solution.py:18
  175.3 9.2 %collective-permute-start.23 = (f32[16,512]{1,0:T(8,128)S(1)}, f32[16,512]{1,0:T(8,128)S(1)}, u32[]{:S(2)}, u32[]{:S(2)}) collective-permute-start(f32[16,512]{1,0:T(8,128)S(1)} %get-tuple-element.39), channel_id=1, source_target_pairs={{0,16},{8,24},{16,0},{24,8},{1,17},{9,25},{17,1},{25,9},{2,18},{10... | collective-permute-start | bytes 98312 | tf_op jit(solution)/shard_map/ppermute | solution.py:18
  184.5 5.3 %collective-permute-start.21 = (f32[16,512]{1,0:T(8,128)S(1)}, f32[16,512]{1,0:T(8,128)S(1)}, u32[]{:S(2)}, u32[]{:S(2)}) collective-permute-start(f32[16,512]{1,0:T(8,128)S(1)} %get-tuple-element.40), channel_id=1, source_target_pairs={{0,8},{8,16},{16,24},{24,0},{1,9},{9,17},{17,25},{25,1},{2,10},{10... | collective-permute-start | bytes 98312 | tf_op jit(solution)/shard_map/ppermute | solution.py:18
  189.8 5.0 %collective-permute-done.21 = f32[16,512]{1,0:T(8,128)S(1)} collective-permute-done((f32[16,512]{1,0:T(8,128)S(1)}, f32[16,512]{1,0:T(8,128)S(1)}, u32[]{:S(2)}, u32[]{:S(2)}) %collective-permute-start.21) | collective-permute-done | bytes 32800 | tf_op jit(solution)/shard_map/ppermute | solution.py:18
  (43 shorter events, 33.0 us)
Async XLA Ops:
  2.1 25.9 %collective-permute-start.6 = (bf16[512,128]{1,0:T(8,128)(2,1)S(1)}, bf16[512,128]{1,0:T(8,128)(2,1)S(1)}, u32[]{:S(2)}, u32[]{:S(2)}) collective-permute-start(bf16[512,128]{1,0:T(8,128)(2,1)S(1)} %get-tuple-element.24), channel_id=1, source_target_pairs={{0,8},{8,16},{16,24},{24,0},{1,9},{9,17},{17,25},{25,1},{2,10},{10... | collective-permute-start | bytes 393224 | tf_op jit(solution)/shard_map/ppermute | solution.py:18
  11.2 28.5 %collective-permute-start.7 = (bf16[512,128]{1,0:T(8,128)(2,1)S(1)}, bf16[512,128]{1,0:T(8,128)(2,1)S(1)}, u32[]{:S(2)}, u32[]{:S(2)}) collective-permute-start(bf16[512,128]{1,0:T(8,128)(2,1)S(1)} %get-tuple-element.25), channel_id=1, source_target_pairs={{0,16},{8,24},{16,0},{24,8},{1,17},{9,25},{17,1},{25,9},{2,18},{10... | collective-permute-start | bytes 393224 | tf_op jit(solution)/shard_map/ppermute | solution.py:18
  22.2 23.4 %collective-permute-start.8 = (bf16[512,128]{1,0:T(8,128)(2,1)S(1)}, bf16[512,128]{1,0:T(8,128)(2,1)S(1)}, u32[]{:S(2)}, u32[]{:S(2)}) collective-permute-start(bf16[512,128]{1,0:T(8,128)(2,1)S(1)} %get-tuple-element.26), channel_id=1, source_target_pairs={{0,24},{8,0},{16,8},{24,16},{1,25},{9,1},{17,9},{25,17},{2,26},{10... | collective-permute-start | bytes 393224 | tf_op jit(solution)/shard_map/ppermute | solution.py:18
  48.0 40.6 %collective-permute-start.11 = (bf16[2048,128]{1,0:T(8,128)(2,1)S(1)}, bf16[2048,128]{1,0:T(8,128)(2,1)S(1)}, u32[]{:S(2)}, u32[]{:S(2)}) collective-permute-start(bf16[2048,128]{1,0:T(8,128)(2,1)S(1)} %rows_in_order.3.refs_4_), channel_id=1, source_target_pairs={{0,4},{2,6},{4,0},{6,2},{1,5},{3,7},{5,1},{7,3},{8,12},{10,14},{12... | collective-permute-start | bytes 1572872 | tf_op jit(solution)/shard_map/ppermute | solution.py:18
  51.3 22.0 %collective-permute-start = (bf16[512,128]{1,0:T(8,128)(2,1)S(1)}, bf16[512,128]{1,0:T(8,128)(2,1)S(1)}, u32[]{:S(2)}, u32[]{:S(2)}) collective-permute-start(bf16[512,128]{1,0:T(8,128)(2,1)S(1)} %get-tuple-element.20), channel_id=1, source_target_pairs={{0,8},{8,16},{16,24},{24,0},{1,9},{9,17},{17,25},{25,1},{2,10},{10... | collective-permute-start | bytes 393224 | tf_op jit(solution)/shard_map/ppermute | solution.py:18
  55.2 23.3 %collective-permute-start.1 = (bf16[512,128]{1,0:T(8,128)(2,1)S(1)}, bf16[512,128]{1,0:T(8,128)(2,1)S(1)}, u32[]{:S(2)}, u32[]{:S(2)}) collective-permute-start(bf16[512,128]{1,0:T(8,128)(2,1)S(1)} %get-tuple-element.21), channel_id=1, source_target_pairs={{0,16},{8,24},{16,0},{24,8},{1,17},{9,25},{17,1},{25,9},{2,18},{10... | collective-permute-start | bytes 393224 | tf_op jit(solution)/shard_map/ppermute | solution.py:18
  65.8 13.6 %collective-permute-start.2 = (bf16[512,128]{1,0:T(8,128)(2,1)S(1)}, bf16[512,128]{1,0:T(8,128)(2,1)S(1)}, u32[]{:S(2)}, u32[]{:S(2)}) collective-permute-start(bf16[512,128]{1,0:T(8,128)(2,1)S(1)} %get-tuple-element.22), channel_id=1, source_target_pairs={{0,24},{8,0},{16,8},{24,16},{1,25},{9,1},{17,9},{25,17},{2,26},{10... | collective-permute-start | bytes 393224 | tf_op jit(solution)/shard_map/ppermute | solution.py:18
  71.4 21.6 %collective-permute-start.10 = (bf16[2048,128]{1,0:T(8,128)(2,1)S(1)}, bf16[2048,128]{1,0:T(8,128)(2,1)S(1)}, u32[]{:S(2)}, u32[]{:S(2)}) collective-permute-start(bf16[2048,128]{1,0:T(8,128)(2,1)S(1)} %rows_in_order.3.refs_4_), channel_id=1, source_target_pairs={{0,6},{2,0},{4,2},{6,4},{1,7},{3,1},{5,3},{7,5},{8,14},{10,8},{12,... | collective-permute-start | bytes 1572872 | tf_op jit(solution)/shard_map/ppermute | solution.py:18
  73.3 27.6 %collective-permute-start.9 = (bf16[2048,128]{1,0:T(8,128)(2,1)S(1)}, bf16[2048,128]{1,0:T(8,128)(2,1)S(1)}, u32[]{:S(2)}, u32[]{:S(2)}) collective-permute-start(bf16[2048,128]{1,0:T(8,128)(2,1)S(1)} %rows_in_order.3.refs_4_), channel_id=1, source_target_pairs={{0,2},{2,4},{4,6},{6,0},{1,3},{3,5},{5,7},{7,1},{8,10},{10,12},{12... | collective-permute-start | bytes 1572872 | tf_op jit(solution)/shard_map/ppermute | solution.py:18
  81.9 19.0 %collective-permute-start.5 = (bf16[2048,128]{1,0:T(8,128)(2,1)S(1)}, bf16[2048,128]{1,0:T(8,128)(2,1)S(1)}, u32[]{:S(2)}, u32[]{:S(2)}) collective-permute-start(bf16[2048,128]{1,0:T(8,128)(2,1)S(1)} %rows_in_order.2.refs_0_), channel_id=1, source_target_pairs={{0,4},{2,6},{4,0},{6,2},{1,5},{3,7},{5,1},{7,3},{8,12},{10,14},{12... | collective-permute-start | bytes 1572872 | tf_op jit(solution)/shard_map/ppermute | solution.py:18
  85.9 24.4 %collective-permute-start.4 = (bf16[2048,128]{1,0:T(8,128)(2,1)S(1)}, bf16[2048,128]{1,0:T(8,128)(2,1)S(1)}, u32[]{:S(2)}, u32[]{:S(2)}) collective-permute-start(bf16[2048,128]{1,0:T(8,128)(2,1)S(1)} %rows_in_order.2.refs_0_), channel_id=1, source_target_pairs={{0,6},{2,0},{4,2},{6,4},{1,7},{3,1},{5,3},{7,5},{8,14},{10,8},{12,... | collective-permute-start | bytes 1572872 | tf_op jit(solution)/shard_map/ppermute | solution.py:18
  88.7 22.2 %collective-permute-start.3 = (bf16[2048,128]{1,0:T(8,128)(2,1)S(1)}, bf16[2048,128]{1,0:T(8,128)(2,1)S(1)}, u32[]{:S(2)}, u32[]{:S(2)}) collective-permute-start(bf16[2048,128]{1,0:T(8,128)(2,1)S(1)} %rows_in_order.2.refs_0_), channel_id=1, source_target_pairs={{0,2},{2,4},{4,6},{6,0},{1,3},{3,5},{5,7},{7,1},{8,10},{10,12},{12... | collective-permute-start | bytes 1572872 | tf_op jit(solution)/shard_map/ppermute | solution.py:18
  116.3 11.5 %collective-permute-start.13 = (f32[128,2048]{1,0:T(8,128)S(1)}, f32[128,2048]{1,0:T(8,128)S(1)}, u32[]{:S(2)}, u32[]{:S(2)}) collective-permute-start(f32[128,2048]{1,0:T(8,128)S(1)} %get-tuple-element.30), channel_id=1, source_target_pairs={{0,1},{1,0},{2,3},{3,2},{4,5},{5,4},{6,7},{7,6},{8,9},{9,8},{10,11... | collective-permute-start | bytes 3145736 | tf_op jit(solution)/shard_map/ppermute | solution.py:18
  118.2 4.3 %collective-permute-start.16 = (f32[64,2048]{1,0:T(8,128)S(1)}, f32[64,2048]{1,0:T(8,128)S(1)}, u32[]{:S(2)}, u32[]{:S(2)}) collective-permute-start(f32[64,2048]{1,0:T(8,128)S(1)} %get-tuple-element.32), channel_id=1, source_target_pairs={{0,1},{1,0},{2,3},{3,2},{4,5},{5,4},{6,7},{7,6},{8,9},{9,8},{10,11... | collective-permute-start | bytes 1572872 | tf_op jit(solution)/shard_map/ppermute | solution.py:18
  120.6 14.4 %collective-permute-start.12 = (f32[64,2048]{1,0:T(8,128)S(1)}, f32[64,2048]{1,0:T(8,128)S(1)}, u32[]{:S(2)}, u32[]{:S(2)}) collective-permute-start(f32[64,2048]{1,0:T(8,128)S(1)} %get-tuple-element.28), channel_id=1, source_target_pairs={{0,1},{1,0},{2,3},{3,2},{4,5},{5,4},{6,7},{7,6},{8,9},{9,8},{10,11... | collective-permute-start | bytes 1572872 | tf_op jit(solution)/shard_map/ppermute | solution.py:18
  122.6 18.2 %collective-permute-start.17 = (f32[64,2048]{1,0:T(8,128)S(1)}, f32[64,2048]{1,0:T(8,128)S(1)}, u32[]{:S(2)}, u32[]{:S(2)}) collective-permute-start(f32[64,2048]{1,0:T(8,128)S(1)} %add.56), channel_id=1, source_target_pairs={{0,256},{128,384},{256,0},{384,128},{1,257},{129,385},{257,1},{385... | collective-permute-start | bytes 1572872 | tf_op jit(solution)/shard_map/ppermute | solution.py:18
  128.0 23.6 %collective-permute-start.14 = (f32[64,2048]{1,0:T(8,128)S(1)}, f32[64,2048]{1,0:T(8,128)S(1)}, u32[]{:S(2)}, u32[]{:S(2)}) collective-permute-start(f32[64,2048]{1,0:T(8,128)S(1)} %get-tuple-element.33), channel_id=1, source_target_pairs={{0,128},{128,256},{256,384},{384,0},{1,129},{129,257},{257,385},{3... | collective-permute-start | bytes 1572872 | tf_op jit(solution)/shard_map/ppermute | solution.py:18
  130.6 21.4 %collective-permute-start.15 = (f32[64,2048]{1,0:T(8,128)S(1)}, f32[64,2048]{1,0:T(8,128)S(1)}, u32[]{:S(2)}, u32[]{:S(2)}) collective-permute-start(f32[64,2048]{1,0:T(8,128)S(1)} %get-tuple-element.34), channel_id=1, source_target_pairs={{0,384},{128,0},{256,128},{384,256},{1,385},{129,1},{257,129},{385... | collective-permute-start | bytes 1572872 | tf_op jit(solution)/shard_map/ppermute | solution.py:18
  152.2 10.8 %collective-permute-start.19 = (f32[16,2048]{1,0:T(8,128)S(1)}, f32[16,2048]{1,0:T(8,128)S(1)}, u32[]{:S(2)}, u32[]{:S(2)}) collective-permute-start(f32[16,2048]{1,0:T(8,128)S(1)} %get-tuple-element.35), channel_id=1, source_target_pairs={{0,96},{32,0},{64,32},{96,64},{1,97},{33,1},{65,33},{97,65},{2,98}... | collective-permute-start | bytes 393224 | tf_op jit(solution)/shard_map/ppermute | solution.py:18
  154.1 14.8 %collective-permute-start.20 = (f32[16,2048]{1,0:T(8,128)S(1)}, f32[16,2048]{1,0:T(8,128)S(1)}, u32[]{:S(2)}, u32[]{:S(2)}) collective-permute-start(f32[16,2048]{1,0:T(8,128)S(1)} %get-tuple-element.36), channel_id=1, source_target_pairs={{0,64},{32,96},{64,0},{96,32},{1,65},{33,97},{65,1},{97,33},{2,66}... | collective-permute-start | bytes 393224 | tf_op jit(solution)/shard_map/ppermute | solution.py:18
  159.0 9.9 %collective-permute-start.18 = (f32[16,2048]{1,0:T(8,128)S(1)}, f32[16,2048]{1,0:T(8,128)S(1)}, u32[]{:S(2)}, u32[]{:S(2)}) collective-permute-start(f32[16,2048]{1,0:T(8,128)S(1)} %get-tuple-element.37), channel_id=1, source_target_pairs={{0,32},{32,64},{64,96},{96,0},{1,33},{33,65},{65,97},{97,1},{2,34}... | collective-permute-start | bytes 393224 | tf_op jit(solution)/shard_map/ppermute | solution.py:18
  168.9 20.8 %collective-permute-start.22 = (f32[16,512]{1,0:T(8,128)S(1)}, f32[16,512]{1,0:T(8,128)S(1)}, u32[]{:S(2)}, u32[]{:S(2)}) collective-permute-start(f32[16,512]{1,0:T(8,128)S(1)} %get-tuple-element.38), channel_id=1, source_target_pairs={{0,24},{8,0},{16,8},{24,16},{1,25},{9,1},{17,9},{25,17},{2,26},{10... | collective-permute-start | bytes 98312 | tf_op jit(solution)/shard_map/ppermute | solution.py:18
  175.3 14.5 %collective-permute-start.23 = (f32[16,512]{1,0:T(8,128)S(1)}, f32[16,512]{1,0:T(8,128)S(1)}, u32[]{:S(2)}, u32[]{:S(2)}) collective-permute-start(f32[16,512]{1,0:T(8,128)S(1)} %get-tuple-element.39), channel_id=1, source_target_pairs={{0,16},{8,24},{16,0},{24,8},{1,17},{9,25},{17,1},{25,9},{2,18},{10... | collective-permute-start | bytes 98312 | tf_op jit(solution)/shard_map/ppermute | solution.py:18
  184.5 10.3 %collective-permute-start.21 = (f32[16,512]{1,0:T(8,128)S(1)}, f32[16,512]{1,0:T(8,128)S(1)}, u32[]{:S(2)}, u32[]{:S(2)}) collective-permute-start(f32[16,512]{1,0:T(8,128)S(1)} %get-tuple-element.40), channel_id=1, source_target_pairs={{0,8},{8,16},{16,24},{24,0},{1,9},{9,17},{17,25},{25,1},{2,10},{10... | collective-permute-start | bytes 98312 | tf_op jit(solution)/shard_map/ppermute | solution.py:18
  (2 other events, 27.6 us)

commit v3 on v0

v3 whole, which is shorter than its diff:
```python
import jax
import jax.numpy as jnp
from jax import lax
from jax.experimental import pallas as pl
from jax.experimental.pallas import tpu as pltpu
from jax.sharding import Mesh, PartitionSpec as P

Y, ZL, ROW, X, CORE = 4, 4, 4, 4, 2
VMEM_BYTES = 40 * 1024 * 1024
FULL = pl.BlockSpec(memory_space=pltpu.VMEM)
SCALARS = pl.BlockSpec(memory_space=pltpu.SMEM)


def params():
    return pltpu.CompilerParams(vmem_limit_bytes=VMEM_BYTES)


def both_ways(value, axis, by):
    n = lax.axis_size(axis)
    pairs = [(i * CORE + c, (i + (by if c == 0 else -by)) % n * CORE + c) for i in range(n) for c in range(CORE)]
    return lax.ppermute(value, (axis, "core"), pairs)


def split_kernel(place, source, *outs):
    row, core = place[0], place[1]
    width = outs[0].shape[1]
    for out, step in zip(outs, (0, 1 + 2 * core, 3 + 2 * core, 2)):
        start = lax.rem(row + step, ROW) * width
        out[...] = source[:, pl.ds(pl.multiple_of(start, width), width)]


STEPS = (1, 3, 2)


def split(place, snapshots):
    held, cells = snapshots.shape
    width = cells // ROW
    return pl.pallas_call(
        split_kernel,
        out_shape=[jax.ShapeDtypeStruct((held, width), snapshots.dtype)] * ROW,
        in_specs=[SCALARS, FULL],
        out_specs=[FULL] * ROW,
        compiler_params=params(),
        name="split_cells",
    )(place, snapshots)


def panel_kernel(place, wanted, *refs):
    pieces, (far, near, rows, chosen) = refs[:ROW], refs[ROW:]
    _, held, width = pieces[0].shape
    total, depth = rows.shape
    step = pl.program_id(0)

    @pl.when(step == 0)
    def _():
        row, core = place[0], place[1]
        for m, back in enumerate((0, 3 + 2 * core, 1 + 2 * core, 2)):
            at = pl.ds(pl.multiple_of(lax.rem(row + back, ROW) * held, held), held)
            for s in range(X):
                rows[at, s * width : (s + 1) * width] = pieces[m][s]
        block = 256
        for at in range(0, wanted.shape[0], block):
            number = lax.broadcasted_iota(jnp.int32, (block, total), 1)
            pick = jnp.where(wanted[at : at + block, :] == number, 1.0, 0.0).astype(jnp.bfloat16)
            for s in range(0, depth, width):
                chosen[at : at + block, s : s + width] = jnp.dot(
                    pick, rows[:, s : s + width], preferred_element_type=jnp.float32
                ).astype(jnp.bfloat16)

    lanes = far.shape[1]
    right = rows[pl.ds(pl.multiple_of(step * lanes, lanes), lanes), :]
    half = far.shape[0]
    for part, out in enumerate((far, near)):
        out[...] = lax.dot_general(
            chosen[part * half : (part + 1) * half, :],
            right,
            (((1,), (1,)), ((), ())),
            preferred_element_type=jnp.float32,
        )


def panel(place, wanted, pieces):
    _, held, width = pieces[0].shape
    total, depth, lanes = held * ROW, width * X, 512
    count = wanted.shape[0]
    half = count // CORE
    return pl.pallas_call(
        panel_kernel,
        grid=(total // lanes,),
        out_shape=[jax.ShapeDtypeStruct((half, total), jnp.float32)] * CORE,
        in_specs=[SCALARS] + [FULL] * (1 + len(pieces)),
        out_specs=[pl.BlockSpec((half, lanes), lambda i: (0, i))] * CORE,
        scratch_shapes=[
            pltpu.VMEM((total, depth), jnp.bfloat16),
            pltpu.VMEM((count, depth), jnp.bfloat16),
        ],
        compiler_params=params(),
        cost_estimate=pl.CostEstimate(
            flops=4 * count * total * depth,
            bytes_accessed=2 * total * depth + 4 * count * total,
            transcendentals=0,
        ),
        name="gram_panel",
    )(place, wanted, *pieces)


def arrange_kernel(order, value, out):
    whole = (value[0] + value[1]) + (value[2] + value[3])
    high = whole.astype(jnp.bfloat16)
    rest = whole - high.astype(jnp.float32)
    middle = rest.astype(jnp.bfloat16)
    low = (rest - middle.astype(jnp.float32)).astype(jnp.bfloat16)
    parts = jnp.concatenate([high, middle, low], axis=0)
    count, total = whole.shape
    _, unit, held = out.shape
    block = 256
    for at in range(0, total, block):
        number = lax.broadcasted_iota(jnp.int32, (total, block), 0)
        pick = jnp.where(order[:, at : at + block] == number, 1.0, 0.0).astype(jnp.bfloat16)
        moved = jnp.dot(parts, pick, preferred_element_type=jnp.float32)
        moved = (moved[:count] + moved[count : 2 * count]) + moved[2 * count :]
        row, lane = at // held, at % held
        for zl in range(ZL):
            out[row * ZL + zl, :, lane : lane + block] = moved[zl * unit : (zl + 1) * unit]


def arrange(order, value):
    _, count, total = value.shape
    return pl.pallas_call(
        arrange_kernel,
        out_shape=jax.ShapeDtypeStruct((ROW * ZL, count // ZL, total // ROW), jnp.float32),
        in_specs=[FULL, FULL],
        out_specs=FULL,
        compiler_params=params(),
        cost_estimate=pl.CostEstimate(
            flops=6 * count * total * total, bytes_accessed=20 * count * total, transcendentals=0
        ),
        name="arrange_rows",
    )(order, value)


def local(snapshots, snapshot_order):
    held, cells = snapshots.shape
    total = held * ROW
    factor = 1.0 / (cells * Y * ZL * X * CORE)
    core = lax.axis_index("core")
    place = jnp.stack([lax.axis_index("row"), core])
    order = snapshot_order.reshape(1, total)
    mine = snapshot_order.reshape(Y, ZL, X, CORE, -1)
    mine = lax.dynamic_index_in_dim(mine, lax.axis_index("x"), 2, keepdims=False)
    mine = mine.transpose(2, 0, 1, 3)
    wanted = jnp.where(core == 0, mine[::-1], mine).reshape(total // X, 1)
    own, *sent = split(place, snapshots)
    got = [both_ways(value, "row", by) for value, by in zip(sent, STEPS)]
    pieces = [lax.all_gather(own, "x")]
    for value in got:
        if len(pieces) > 1:
            value, _ = lax.optimization_barrier((value, pieces[-1]))
        copies = jnp.broadcast_to(value[None], (X,) + value.shape)
        pieces.append(lax.all_to_all(copies, "x", 0, 0, tiled=False))
    far, near = panel(place, wanted, pieces)
    near = near + lax.ppermute(far, "core", [(0, 1), (1, 0)])
    value = lax.all_to_all(near.reshape(Y, -1, total), "y", 0, 0, tiled=False)
    value = arrange(order, value)
    value = lax.all_to_all(value, ("row", "zl"), 0, 0, tiled=False)
    return value.sum(0).T * factor


def solution(mesh):
    fine = Mesh(mesh.devices.reshape(Y, ZL, ROW, X, CORE), ("y", "zl", "row", "x", "core"))
    columns = ("y", "zl", "x", "core")
    return jax.shard_map(
        local, mesh=fine, in_specs=(P("row", columns), P()), out_specs=P("row", columns), check_vma=False
    )
```

time: 1530 us -> 207 us (0.14); the launches traced: 1510 us -> 205 us
  waiting for transfers between devices: 1470 us -> 56.1 us
  blocking collectives: 0 us -> 67.1 us
  starting transfers between devices: 0.04 us -> 51.1 us
    psum x1 -> x0, waiting for transfers between devices: 1300 us -> none  [local(): summed = lax.psum(partial_value, ('cells', 'col'))]
    all_gather x1, waiting for transfers between devices: 168 us -> 0.02 us  [local(): pieces = [lax.all_gather(own, 'x')]]
    all_to_all x0 -> x2, blocking collectives: none -> 67.1 us  [the longest x1 36.3 us: local(): value = lax.all_to_all(value, ('row', 'zl'), 0, 0, tiled=False)]
    ppermute x0 -> x4, waiting for transfers between devices: none -> 42.3 us  [the longest x3 38.2 us: both_ways(): return lax.ppermute(value, (axis, 'core'), pairs)]
    ppermute x0 -> x4, starting transfers between devices: none -> 36.7 us  [the longest x3 34.8 us: both_ways(): return lax.ppermute(value, (axis, 'core'), pairs)]
  transfers between devices with their start and end apart: 2 -> 8, of which waited for: 2 -> 5; matrix products, arithmetic and copies ran while one was open for 0% -> 1% of each run, Pallas kernels for 0% -> 0%
where the time goes in v3:
time: 207 us; the launch traced here: 205 us
  blocking collectives  67.1 us (32%)
  waiting for transfers between devices  56.1 us (27%)
  starting transfers between devices  51.1 us (25%)
  between operations  13.5 us (7%)
  Pallas kernels  9.87 us (5%)
  local copies, waits for them, and re-layouts  5.98 us (3%)
    ppermute x3, waiting for transfers between devices, both_ways(): return lax.ppermute(value, (axis, 'core'), pairs)  38.2 us
    all_to_all x1, blocking collectives, local(): value = lax.all_to_all(value, ('row', 'zl'), 0, 0, tiled=False)  36.3 us
    ppermute x3, starting transfers between devices, both_ways(): return lax.ppermute(value, (axis, 'core'), pairs)  34.8 us
    all_to_all x1, blocking collectives, local(): value = lax.all_to_all(near.reshape(Y, -1, total), 'y', 0, 0, tiled=False)  30.9 us
    all_to_all x3, starting transfers between devices, local(): pieces.append(lax.all_to_all(copies, 'x', 0, 0, tiled=False))  14.4 us
    all_to_all x3, waiting for transfers between devices, local(): pieces.append(lax.all_to_all(copies, 'x', 0, 0, tiled=False))  13.1 us
    pallas_call x1, Pallas kernels, panel(): pl.pallas_call(panel_kernel, grid=(total // lanes,), out_shape=[jax.Shape...  6.65 us
  transfers between devices with their start and end apart: 8, of which 5 were waited for; matrix products, arithmetic and copies ran while one was open for 1% of the time, Pallas kernels for 0%

profile of v3, /device:TPU:6, one launch (start us, length us, event | category | flops | bytes accessed | tf_op | source)
XLA Modules:
  0.0 204.7 jit_solution(10941528665799979930)
XLA Ops:
  6.6 1.2 copy-done
  7.8 1.4 split_cells.1
  9.2 9.1 %collective-permute-start = (bf16[512,256]{1,0:T(8,128)(2,1)S(1)}, bf16[512,256]{1,0:T(8,128)(2,1)S(1)}, u32[]{:S(2)}, u32[]{:S(2)}) collective-permute-start(bf16[512,256]{1,0:T(8,128)(2,1)S(1)} %get-tuple-element.14), channel_id=1, source_target_pairs={{0,8},{1,25},{8,16},{9,1},{16,24},{17,9},{24,0},{25,17},{2,10},{3,... | collective-permute-start | bytes 786440 | tf_op jit(solution)/shard_map/ppermute | solution.py:21
  18.3 8.3 %collective-permute-done = bf16[512,256]{1,0:T(8,128)(2,1)S(1)} collective-permute-done((bf16[512,256]{1,0:T(8,128)(2,1)S(1)}, bf16[512,256]{1,0:T(8,128)(2,1)S(1)}, u32[]{:S(2)}, u32[]{:S(2)}) %collective-permute-start) | collective-permute-done | bytes 262176 | tf_op jit(solution)/shard_map/ppermute | solution.py:21
  26.6 1.0 broadcast_in_dim.6
  27.6 4.8 %all-to-all-start = ((bf16[4,512,256]{2,1,0:T(8,128)(2,1)}), bf16[4,512,256]{2,1,0:T(8,128)(2,1)S(1)}, u32[]{:S(2)}, u32[]{:S(2)}) async-start(bf16[4,512,256]{2,1,0:T(8,128)(2,1)} %broadcast_in_dim.6), calls=%async_computation | async-start | bytes 2097152 | tf_op jit(solution)/shard_map/all_to_all | solution.py:160
  32.4 10.7 %collective-permute-start.1 = (bf16[512,256]{1,0:T(8,128)(2,1)S(1)}, bf16[512,256]{1,0:T(8,128)(2,1)S(1)}, u32[]{:S(2)}, u32[]{:S(2)}) collective-permute-start(bf16[512,256]{1,0:T(8,128)(2,1)S(1)} %get-tuple-element.15), channel_id=1, source_target_pairs={{0,24},{1,9},{8,0},{9,17},{16,8},{17,25},{24,16},{25,1},{2,26},{3,... | collective-permute-start | bytes 786440 | tf_op jit(solution)/shard_map/ppermute | solution.py:21
  43.1 10.7 %collective-permute-done.1 = bf16[512,256]{1,0:T(8,128)(2,1)S(1)} collective-permute-done((bf16[512,256]{1,0:T(8,128)(2,1)S(1)}, bf16[512,256]{1,0:T(8,128)(2,1)S(1)}, u32[]{:S(2)}, u32[]{:S(2)}) %collective-permute-start.1) | collective-permute-done | bytes 262176 | tf_op jit(solution)/shard_map/ppermute | solution.py:21
  53.8 1.1 broadcast_in_dim.7
  54.9 4.8 %all-to-all-start.1 = ((bf16[4,512,256]{2,1,0:T(8,128)(2,1)}), bf16[4,512,256]{2,1,0:T(8,128)(2,1)S(1)}, u32[]{:S(2)}, u32[]{:S(2)}) async-start(bf16[4,512,256]{2,1,0:T(8,128)(2,1)} %broadcast_in_dim.7), calls=%async_computation.1 | async-start | bytes 2097152 | tf_op jit(solution)/shard_map/all_to_all | solution.py:160
  59.7 0.7 all-gather.3.cloned.1.call-update
  60.4 15.0 %collective-permute-start.2 = (bf16[512,256]{1,0:T(8,128)(2,1)S(1)}, bf16[512,256]{1,0:T(8,128)(2,1)S(1)}, u32[]{:S(2)}, u32[]{:S(2)}) collective-permute-start(bf16[512,256]{1,0:T(8,128)(2,1)S(1)} %get-tuple-element.17), channel_id=1, source_target_pairs={{0,16},{1,17},{8,24},{9,25},{16,0},{17,1},{24,8},{25,9},{2,18},{3,... | collective-permute-start | bytes 786440 | tf_op jit(solution)/shard_map/ppermute | solution.py:21
  75.4 19.2 %collective-permute-done.2 = bf16[512,256]{1,0:T(8,128)(2,1)S(1)} collective-permute-done((bf16[512,256]{1,0:T(8,128)(2,1)S(1)}, bf16[512,256]{1,0:T(8,128)(2,1)S(1)}, u32[]{:S(2)}, u32[]{:S(2)}) %collective-permute-start.2) | collective-permute-done | bytes 262176 | tf_op jit(solution)/shard_map/ppermute | solution.py:21
  94.6 1.1 broadcast_in_dim.8
  95.7 4.8 %all-to-all-start.2 = ((bf16[4,512,256]{2,1,0:T(8,128)(2,1)}), bf16[4,512,256]{2,1,0:T(8,128)(2,1)S(1)}, u32[]{:S(2)}, u32[]{:S(2)}) async-start(bf16[4,512,256]{2,1,0:T(8,128)(2,1)} %broadcast_in_dim.8), calls=%async_computation.2 | async-start | bytes 2097152 | tf_op jit(solution)/shard_map/all_to_all | solution.py:160
  100.9 13.1 %all-to-all-done.2.refs_3_ = bf16[4,512,256]{2,1,0:T(8,128)(2,1)S(1)} async-done(((bf16[4,512,256]{2,1,0:T(8,128)(2,1)}), bf16[4,512,256]{2,1,0:T(8,128)(2,1)S(1)}, u32[]{:S(2)}, u32[]{:S(2)}) %all-to-all-start.2) | async-done | bytes 1048608 | tf_op jit(solution)/shard_map/all_to_all | solution.py:160
  114.0 1.2 copy-done.2
  115.2 6.7 %gram_panel.1 = (f32[256,2048]{1,0:T(8,128)S(1)}, f32[256,2048]{1,0:T(8,128)S(1)}) custom-call(s32[2]{0:T(128)S(1)} %pad_add_fusion.place, s32[512,1]{1,0:T(8,128)S(1)} %reshape.20.wanted, bf16[4,512,256]{2,1,0:T(8,128)(2,1)S(1)} %bitcast.14, bf16[4,512,256]{2,1,0:T(8,128)(2,1)S(1)} %all-to-all-done.refs_1_, ...), custom_call_target="tpu_custom_call" | custom-call | flops 4294967296 | bytes 8388608 | tf_op jit(solution)/shard_map/gram_panel/pallas_call | solution.py:87
  121.9 1.9 collective-permute-start.3
  123.8 4.1 %collective-permute-done.3 = f32[256,2048]{1,0:T(8,128)S(1)} collective-permute-done((f32[256,2048]{1,0:T(8,128)S(1)}, f32[256,2048]{1,0:T(8,128)S(1)}, u32[]{:S(2)}, u32[]{:S(2)}) %collective-permute-start.3) | collective-permute-done | bytes 2097184 | tf_op jit(solution)/shard_map/ppermute | solution.py:162
  128.2 30.9 %all_to_all.25.value = f32[4,64,2048]{2,1,0:T(8,128)S(1)} all-to-all(f32[4,64,2048]{2,1,0:T(8,128)S(1)} %bitcast.15), channel_id=1, replica_groups=mesh['y'=4,'zl'=4,'row'=4,'x'=4,'core'=2] {'y'}, dimensions={0} | all-to-all | bytes 4194304 | tf_op jit(solution)/shard_map/all_to_all | solution.py:163
  159.1 1.8 arrange_rows.1
  161.0 36.3 %all_to_all.26 = f32[16,16,512]{2,1,0:T(8,128)S(1)} all-to-all(f32[16,16,512]{2,1,0:T(8,128)S(1)} %arrange_rows.1), channel_id=1, replica_groups=mesh['y'=4,'zl'=4,'row'=4,'x'=4,'core'=2] {'row','zl'}, dimensions={0} | all-to-all | bytes 1048576 | tf_op jit(solution)/shard_map/all_to_all | solution.py:165
  197.3 0.6 multiply_bitcast_fusion
  (17 shorter events, 0.8 us)
Async XLA Ops:
  6.6 1.2 copy-start
  9.2 17.4 %collective-permute-start = (bf16[512,256]{1,0:T(8,128)(2,1)S(1)}, bf16[512,256]{1,0:T(8,128)(2,1)S(1)}, u32[]{:S(2)}, u32[]{:S(2)}) collective-permute-start(bf16[512,256]{1,0:T(8,128)(2,1)S(1)} %get-tuple-element.14), channel_id=1, source_target_pairs={{0,8},{1,25},{8,16},{9,1},{16,24},{17,9},{24,0},{25,17},{2,10},{3,... | collective-permute-start | bytes 786440 | tf_op jit(solution)/shard_map/ppermute | solution.py:21
  27.6 26.2 %all-to-all-start = ((bf16[4,512,256]{2,1,0:T(8,128)(2,1)}), bf16[4,512,256]{2,1,0:T(8,128)(2,1)S(1)}, u32[]{:S(2)}, u32[]{:S(2)}) async-start(bf16[4,512,256]{2,1,0:T(8,128)(2,1)} %broadcast_in_dim.6), calls=%async_computation | async-start | bytes 2097152 | tf_op jit(solution)/shard_map/all_to_all | solution.py:160
  32.4 21.4 %collective-permute-start.1 = (bf16[512,256]{1,0:T(8,128)(2,1)S(1)}, bf16[512,256]{1,0:T(8,128)(2,1)S(1)}, u32[]{:S(2)}, u32[]{:S(2)}) collective-permute-start(bf16[512,256]{1,0:T(8,128)(2,1)S(1)} %get-tuple-element.15), channel_id=1, source_target_pairs={{0,24},{1,9},{8,0},{9,17},{16,8},{17,25},{24,16},{25,1},{2,26},{3,... | collective-permute-start | bytes 786440 | tf_op jit(solution)/shard_map/ppermute | solution.py:21
  54.9 39.7 %all-to-all-start.1 = ((bf16[4,512,256]{2,1,0:T(8,128)(2,1)}), bf16[4,512,256]{2,1,0:T(8,128)(2,1)S(1)}, u32[]{:S(2)}, u32[]{:S(2)}) async-start(bf16[4,512,256]{2,1,0:T(8,128)(2,1)} %broadcast_in_dim.7), calls=%async_computation.1 | async-start | bytes 2097152 | tf_op jit(solution)/shard_map/all_to_all | solution.py:160
  59.7 40.8 %copy-start.1 = (s32[2048]{0:T(1024)S(1)}, s32[2048]{0:T(1024)}, u32[]{:S(2)}) copy-start(s32[2048]{0:T(1024)} %param.3) | copy-start | bytes 24580
  59.7 41.2 %all-gather.3.cloned.1.call-start = ((), (), s32[]{:S(2)}) async-start(), calls=%async_computation.5 | async-start | bytes 1310720 | tf_op jit(solution)/shard_map/all_gather | solution.py:155
  60.4 34.2 %collective-permute-start.2 = (bf16[512,256]{1,0:T(8,128)(2,1)S(1)}, bf16[512,256]{1,0:T(8,128)(2,1)S(1)}, u32[]{:S(2)}, u32[]{:S(2)}) collective-permute-start(bf16[512,256]{1,0:T(8,128)(2,1)S(1)} %get-tuple-element.17), channel_id=1, source_target_pairs={{0,16},{1,17},{8,24},{9,25},{16,0},{17,1},{24,8},{25,9},{2,18},{3,... | collective-permute-start | bytes 786440 | tf_op jit(solution)/shard_map/ppermute | solution.py:21
  95.7 18.3 %all-to-all-start.2 = ((bf16[4,512,256]{2,1,0:T(8,128)(2,1)}), bf16[4,512,256]{2,1,0:T(8,128)(2,1)S(1)}, u32[]{:S(2)}, u32[]{:S(2)}) async-start(bf16[4,512,256]{2,1,0:T(8,128)(2,1)} %broadcast_in_dim.8), calls=%async_computation.2 | async-start | bytes 2097152 | tf_op jit(solution)/shard_map/all_to_all | solution.py:160
  114.0 1.2 copy-start.2
  121.9 6.1 %collective-permute-start.3 = (f32[256,2048]{1,0:T(8,128)S(1)}, f32[256,2048]{1,0:T(8,128)S(1)}, u32[]{:S(2)}, u32[]{:S(2)}) collective-permute-start(f32[256,2048]{1,0:T(8,128)S(1)} %get-tuple-element.20), channel_id=1, source_target_pairs={{0,1},{1,0},{2,3},{3,2},{4,5},{5,4},{6,7},{7,6},{8,9},{9,8},{10,11... | collective-permute-start | bytes 6291464 | tf_op jit(solution)/shard_map/ppermute | solution.py:162
Sparse Core Ops, SparseCore 0:
  62.6 34.0 all-gather.2

commit v4 on v3

v4 whole, which is shorter than its diff:
```python
import jax
import jax.numpy as jnp
from jax import lax
from jax.experimental import pallas as pl
from jax.experimental.pallas import tpu as pltpu
from jax.sharding import Mesh, PartitionSpec as P

Y, ZL, ROW, X, CORE = 4, 4, 4, 4, 2
VMEM_BYTES = 40 * 1024 * 1024
FULL = pl.BlockSpec(memory_space=pltpu.VMEM)
SCALARS = pl.BlockSpec(memory_space=pltpu.SMEM)


def params():
    return pltpu.CompilerParams(vmem_limit_bytes=VMEM_BYTES)


def both_ways(value, axis, by):
    n = lax.axis_size(axis)
    pairs = [(i * CORE + c, (i + (by if c == 0 else -by)) % n * CORE + c) for i in range(n) for c in range(CORE)]
    return lax.ppermute(value, (axis, "core"), pairs)


def split_kernel(place, source, *outs):
    row, core = place[0], place[1]
    width = outs[0].shape[1]
    for out, step in zip(outs, (0, 1 + 2 * core, 3 + 2 * core, 2)):
        start = lax.rem(row + step, ROW) * width
        out[...] = source[:, pl.ds(pl.multiple_of(start, width), width)]


STEPS = (1, 3, 2)


def split(place, snapshots):
    held, cells = snapshots.shape
    width = cells // ROW
    return pl.pallas_call(
        split_kernel,
        out_shape=[jax.ShapeDtypeStruct((held, width), snapshots.dtype)] * ROW,
        in_specs=[SCALARS, FULL],
        out_specs=[FULL] * ROW,
        compiler_params=params(),
        name="split_cells",
    )(place, snapshots)


def slots(place):
    x, core = place[2], place[1]
    return [lax.rem(x + back, X) for back in (0, 3 + 2 * core, 1 + 2 * core, 2)]


def rows_of(m, at, count, order, own, opposite, pairs):
    if m in (0, 3):
        ref = own if m == 0 else opposite
        return [ref[slot, at : at + count, :] for slot in order]
    at += (m - 1) * own.shape[1]
    return [ref[at : at + count, :] for ref in pairs]


BLOCK = 256


def multiply(left, out, blocks, order, own, opposite, pairs):
    held = own.shape[1]
    for to, m in enumerate(blocks):
        for at in range(0, held, BLOCK):
            right = jnp.concatenate(rows_of(m, at, BLOCK, order, own, opposite, pairs), axis=1)
            out[:, to * held + at : to * held + at + BLOCK] = lax.dot_general(
                left, right, (((1,), (1,)), ((), ())), preferred_element_type=jnp.float32
            )


def far_kernel(place, wanted, own, opposite, p0, p1, p2, p3, far, chosen):
    pairs = (p0, p1, p2, p3)
    order = slots(place)
    held = own.shape[1]
    values = []
    for at in range(0, wanted.shape[0], BLOCK):
        parts = [None] * X
        for m in range(ROW):
            number = lax.broadcasted_iota(jnp.int32, (BLOCK, held), 1) + m * held
            pick = jnp.where(wanted[at : at + BLOCK, :] == number, 1.0, 0.0).astype(jnp.bfloat16)
            for s, rows in enumerate(rows_of(m, 0, held, order, own, opposite, pairs)):
                term = jnp.dot(pick, rows, preferred_element_type=jnp.float32)
                parts[s] = term if parts[s] is None else parts[s] + term
        values.append(jnp.concatenate(parts, axis=1).astype(jnp.bfloat16))
    chosen[...] = values[1]
    multiply(values[0], far, (0, 2, 1, 3), order, own, opposite, pairs)


def near_kernel(place, chosen, own, opposite, p0, p1, p2, p3, near):
    multiply(chosen[...], near, (0, 1, 2, 3), slots(place), own, opposite, (p0, p1, p2, p3))


def panels(place, wanted, own, opposite, pairs):
    _, held, width = own.shape
    total, depth, half = held * ROW, width * X, wanted.shape[0] // CORE
    panel = jax.ShapeDtypeStruct((half, total), jnp.float32)
    cost = pl.CostEstimate(
        flops=2 * half * total * depth, bytes_accessed=2 * total * depth + 4 * half * total, transcendentals=0
    )
    far, chosen = pl.pallas_call(
        far_kernel,
        out_shape=[panel, jax.ShapeDtypeStruct((half, depth), own.dtype)],
        in_specs=[SCALARS] + [FULL] * (3 + X),
        out_specs=[FULL] * 2,
        compiler_params=params(),
        cost_estimate=cost,
        name="far_panel",
    )(place, wanted, own, opposite, *pairs)
    near = pl.pallas_call(
        near_kernel,
        out_shape=panel,
        in_specs=[SCALARS] + [FULL] * (3 + X),
        out_specs=FULL,
        compiler_params=params(),
        cost_estimate=cost,
        name="near_panel",
    )(place, chosen, own, opposite, *pairs)
    return far, near


def arrange_kernel(order, value, out):
    whole = (value[0] + value[1]) + (value[2] + value[3])
    high = whole.astype(jnp.bfloat16)
    rest = whole - high.astype(jnp.float32)
    middle = rest.astype(jnp.bfloat16)
    low = (rest - middle.astype(jnp.float32)).astype(jnp.bfloat16)
    parts = jnp.concatenate([high, middle, low], axis=0)
    count, total = whole.shape
    _, unit, held = out.shape
    block = 256
    for at in range(0, total, block):
        number = lax.broadcasted_iota(jnp.int32, (total, block), 0)
        pick = jnp.where(order[:, at : at + block] == number, 1.0, 0.0).astype(jnp.bfloat16)
        moved = jnp.dot(parts, pick, preferred_element_type=jnp.float32)
        moved = (moved[:count] + moved[count : 2 * count]) + moved[2 * count :]
        row, lane = at // held, at % held
        for zl in range(ZL):
            out[row * ZL + zl, :, lane : lane + block] = moved[zl * unit : (zl + 1) * unit]


def arrange(order, value):
    _, count, total = value.shape
    return pl.pallas_call(
        arrange_kernel,
        out_shape=jax.ShapeDtypeStruct((ROW * ZL, count // ZL, total // ROW), jnp.float32),
        in_specs=[FULL, FULL],
        out_specs=FULL,
        compiler_params=params(),
        cost_estimate=pl.CostEstimate(
            flops=6 * count * total * total, bytes_accessed=20 * count * total, transcendentals=0
        ),
        name="arrange_rows",
    )(order, value)


def share(value):
    copies = jnp.broadcast_to(value[None], (X,) + value.shape)
    return lax.all_to_all(copies, "x", 0, 0, tiled=False)


def local(snapshots, snapshot_order):
    held, cells = snapshots.shape
    total = held * ROW
    factor = 1.0 / (cells * Y * ZL * X * CORE)
    core = lax.axis_index("core")
    row = lax.axis_index("row")
    place = jnp.stack([row, core, lax.axis_index("x")])
    away = lax.rem(snapshot_order // held - row + ROW, ROW)
    first = jnp.where(core == 0, ROW - 1, 1)
    piece = jnp.where(away == 0, 0, jnp.where(away == 2, 3, jnp.where(away == first, 1, 2)))
    index = piece * held + snapshot_order % held
    mine = index.reshape(Y, ZL, X, CORE, -1)
    mine = lax.dynamic_index_in_dim(mine, lax.axis_index("x"), 2, keepdims=False)
    mine = mine.transpose(2, 0, 1, 3)
    wanted = jnp.where(core == 0, mine[::-1], mine).reshape(total // X, 1)
    own, *sent = split(place, snapshots)
    near_a, near_b, opposite = [both_ways(value, "row", by) for value, by in zip(sent, STEPS)]
    own = lax.all_gather(own, "x")
    pair = jnp.concatenate([near_a, near_b], axis=0)
    pairs = [pair] + [both_ways(pair, "x", by) for by in STEPS]
    opposite = share(opposite)
    far, near = panels(place, wanted, own, opposite, pairs)
    near = near + lax.ppermute(far, "core", [(0, 1), (1, 0)])
    value = lax.all_to_all(near.reshape(Y, -1, total), "y", 0, 0, tiled=False)
    value = arrange(index.reshape(1, total), value)
    value = lax.all_to_all(value, ("row", "zl"), 0, 0, tiled=False)
    return value.sum(0).T * factor


def solution(mesh):
    fine = Mesh(mesh.devices.reshape(Y, ZL, ROW, X, CORE), ("y", "zl", "row", "x", "core"))
    columns = ("y", "zl", "x", "core")
    return jax.shard_map(
        local, mesh=fine, in_specs=(P("row", columns), P()), out_specs=P("row", columns), check_vma=False
    )
```

time: 207 us -> 190 us (0.918)
  starting transfers between devices: 51.1 us -> 42.6 us
  waiting for transfers between devices: 56.1 us -> 50.4 us
  local copies, waits for them, and re-layouts: 5.98 us -> 3.91 us
    all_to_all x3 -> x1, waiting for transfers between devices: 13.1 us -> 0.01 us  [share(): return lax.all_to_all(copies, 'x', 0, 0, tiled=False)]
    ppermute x3 -> x6, waiting for transfers between devices: 38.2 us -> 48.2 us  [both_ways(): return lax.ppermute(value, (axis, 'core'), pairs)]
    all_to_all x3 -> x1, starting transfers between devices: 14.4 us -> 4.77 us  [share(): return lax.all_to_all(copies, 'x', 0, 0, tiled=False)]
    broadcast_in_dim x3 -> x1, local copies, waits for them, and re-layouts: 3.17 us -> 1.07 us  [share(): copies = jnp.broadcast_to(value[None], (X,) + value.shape)]
    ppermute x3 -> x6, starting transfers between devices: 34.8 us -> 35.8 us  [both_ways(): return lax.ppermute(value, (axis, 'core'), pairs)]
    pallas_call x1 -> x2, Pallas kernels: 6.65 us -> 5.84 us  [the longest x1 4.01 us: panels(): pl.pallas_call(far_kernel, out_shape=[panel, jax.ShapeDtypeStruct((half,...]
  transfers between devices with their start and end apart: 8 -> 9, of which waited for: 5 -> 5; matrix products, arithmetic and copies ran while one was open for 1% -> 1% of each run, Pallas kernels for 0% -> 1%
where the time goes in v4:
time: 190 us; the launch traced here: 188 us
  blocking collectives  67.1 us (35%)
  waiting for transfers between devices  50.4 us (27%)
  starting transfers between devices  42.6 us (22%)
  between operations  13.6 us (7%)
  Pallas kernels  9.06 us (5%)
  local copies, waits for them, and re-layouts  3.91 us (2%)
    ppermute x6, waiting for transfers between devices, both_ways(): return lax.ppermute(value, (axis, 'core'), pairs)  48.2 us
    all_to_all x1, blocking collectives, local(): value = lax.all_to_all(value, ('row', 'zl'), 0, 0, tiled=False)  36.2 us
    ppermute x6, starting transfers between devices, both_ways(): return lax.ppermute(value, (axis, 'core'), pairs)  35.8 us
    all_to_all x1, blocking collectives, local(): value = lax.all_to_all(near.reshape(Y, -1, total), 'y', 0, 0, tiled=False)  30.9 us
    all_to_all x1, starting transfers between devices, share(): return lax.all_to_all(copies, 'x', 0, 0, tiled=False)  4.77 us
    pallas_call x1, Pallas kernels, panels(): pl.pallas_call(far_kernel, out_shape=[panel, jax.ShapeDtypeStruct((half,...  4.01 us
  transfers between devices with their start and end apart: 9, of which 5 were waited for; matrix products, arithmetic and copies ran while one was open for 1% of the time, Pallas kernels for 1%

profile of v4, /device:TPU:6, one launch (start us, length us, event | category | flops | bytes accessed | tf_op | source)
XLA Modules:
  0.0 187.7 jit_solution(14621262144940853207)
XLA Ops:
  6.6 1.2 copy-done.1
  7.8 1.4 split_cells.1
  9.3 15.7 %collective-permute-start = (bf16[512,256]{1,0:T(8,128)(2,1)S(1)}, bf16[512,256]{1,0:T(8,128)(2,1)S(1)}, u32[]{:S(2)}, u32[]{:S(2)}) collective-permute-start(bf16[512,256]{1,0:T(8,128)(2,1)S(1)} %get-tuple-element.12), channel_id=1, source_target_pairs={{0,16},{1,17},{8,24},{9,25},{16,0},{17,1},{24,8},{25,9},{2,18},{3,... | collective-permute-start | bytes 786440 | tf_op jit(solution)/shard_map/ppermute | solution.py:21
  25.0 4.3 %collective-permute-start.1 = (bf16[512,256]{1,0:T(8,128)(2,1)S(1)}, bf16[512,256]{1,0:T(8,128)(2,1)S(1)}, u32[]{:S(2)}, u32[]{:S(2)}) collective-permute-start(bf16[512,256]{1,0:T(8,128)(2,1)S(1)} %get-tuple-element.13), channel_id=1, source_target_pairs={{0,8},{1,25},{8,16},{9,1},{16,24},{17,9},{24,0},{25,17},{2,10},{3,... | collective-permute-start | bytes 786440 | tf_op jit(solution)/shard_map/ppermute | solution.py:21
  29.3 5.5 %collective-permute-start.2 = (bf16[512,256]{1,0:T(8,128)(2,1)S(1)}, bf16[512,256]{1,0:T(8,128)(2,1)S(1)}, u32[]{:S(2)}, u32[]{:S(2)}) collective-permute-start(bf16[512,256]{1,0:T(8,128)(2,1)S(1)} %get-tuple-element.14), channel_id=1, source_target_pairs={{0,24},{1,9},{8,0},{9,17},{16,8},{17,25},{24,16},{25,1},{2,26},{3,... | collective-permute-start | bytes 786440 | tf_op jit(solution)/shard_map/ppermute | solution.py:21
  34.8 1.1 broadcast_in_dim.9
  35.9 4.8 %all-to-all-start = ((bf16[4,512,256]{2,1,0:T(8,128)(2,1)}), bf16[4,512,256]{2,1,0:T(8,128)(2,1)S(1)}, u32[]{:S(2)}, u32[]{:S(2)}) async-start(bf16[4,512,256]{2,1,0:T(8,128)(2,1)} %broadcast_in_dim.9), calls=%async_computation | async-start | bytes 2097152 | tf_op jit(solution)/shard_map/all_to_all | solution.py:161
  40.6 7.0 %collective-permute-done.1 = bf16[512,256]{1,0:T(8,128)(2,1)S(1)} collective-permute-done((bf16[512,256]{1,0:T(8,128)(2,1)S(1)}, bf16[512,256]{1,0:T(8,128)(2,1)S(1)}, u32[]{:S(2)}, u32[]{:S(2)}) %collective-permute-start.1) | collective-permute-done | bytes 262176 | tf_op jit(solution)/shard_map/ppermute | solution.py:21
  47.6 23.7 %collective-permute-done.2 = bf16[512,256]{1,0:T(8,128)(2,1)S(1)} collective-permute-done((bf16[512,256]{1,0:T(8,128)(2,1)S(1)}, bf16[512,256]{1,0:T(8,128)(2,1)S(1)}, u32[]{:S(2)}, u32[]{:S(2)}) %collective-permute-start.2) | collective-permute-done | bytes 262176 | tf_op jit(solution)/shard_map/ppermute | solution.py:21
  71.4 3.3 %collective-permute-start.5 = (bf16[1024,256]{1,0:T(8,128)(2,1)S(1)}, bf16[1024,256]{1,0:T(8,128)(2,1)S(1)}, u32[]{:S(2)}, u32[]{:S(2)}) collective-permute-start(bf16[1024,256]{1,0:T(8,128)(2,1)S(1)} %constant_dynamic-update-slice_fusion.p0), channel_id=1, source_target_pairs={{0,4},{1,5},{2,6},{3,7},{4,0},{5,1},{6,2},{7,3},{8,12},{9,13},{10,... | collective-permute-start | bytes 1572872 | tf_op jit(solution)/shard_map/ppermute | solution.py:21
  74.7 1.9 %collective-permute-start.4 = (bf16[1024,256]{1,0:T(8,128)(2,1)S(1)}, bf16[1024,256]{1,0:T(8,128)(2,1)S(1)}, u32[]{:S(2)}, u32[]{:S(2)}) collective-permute-start(bf16[1024,256]{1,0:T(8,128)(2,1)S(1)} %constant_dynamic-update-slice_fusion.p0), channel_id=1, source_target_pairs={{0,6},{1,3},{2,0},{3,5},{4,2},{5,7},{6,4},{7,1},{8,14},{9,11},{10,... | collective-permute-start | bytes 1572872 | tf_op jit(solution)/shard_map/ppermute | solution.py:21
  76.6 5.1 %collective-permute-start.3 = (bf16[1024,256]{1,0:T(8,128)(2,1)S(1)}, bf16[1024,256]{1,0:T(8,128)(2,1)S(1)}, u32[]{:S(2)}, u32[]{:S(2)}) collective-permute-start(bf16[1024,256]{1,0:T(8,128)(2,1)S(1)} %constant_dynamic-update-slice_fusion.p0), channel_id=1, source_target_pairs={{0,2},{1,7},{2,4},{3,1},{4,6},{5,3},{6,0},{7,5},{8,10},{9,15},{10,... | collective-permute-start | bytes 1572872 | tf_op jit(solution)/shard_map/ppermute | solution.py:21
  82.2 7.4 %collective-permute-done.5.p3 = bf16[1024,256]{1,0:T(8,128)(2,1)S(1)} collective-permute-done((bf16[1024,256]{1,0:T(8,128)(2,1)S(1)}, bf16[1024,256]{1,0:T(8,128)(2,1)S(1)}, u32[]{:S(2)}, u32[]{:S(2)}) %collective-permute-start.5) | collective-permute-done | bytes 524320 | tf_op jit(solution)/shard_map/ppermute | solution.py:21
  89.6 10.0 %collective-permute-done.4.p2 = bf16[1024,256]{1,0:T(8,128)(2,1)S(1)} collective-permute-done((bf16[1024,256]{1,0:T(8,128)(2,1)S(1)}, bf16[1024,256]{1,0:T(8,128)(2,1)S(1)}, u32[]{:S(2)}, u32[]{:S(2)}) %collective-permute-start.4) | collective-permute-done | bytes 524320 | tf_op jit(solution)/shard_map/ppermute | solution.py:21
  99.7 1.2 copy-done
  100.9 4.0 %far_panel.1 = (f32[256,2048]{1,0:T(8,128)S(1)}, bf16[256,1024]{1,0:T(8,128)(2,1)S(1)}) custom-call(s32[3]{0:T(128)S(1)} %pad_add_fusion.place, s32[512,1]{1,0:T(8,128)S(1)} %reshape.18.wanted, bf16[4,512,256]{2,1,0:T(8,128)(2,1)S(1)} %bitcast.14, bf16[4,512,256]{2,1,0:T(8,128)(2,1)S(1)} %all-to-all-done.opposite, ...), custom_call_target="tpu_custom_call" | custom-call | flops 1073741824 | bytes 6291456 | tf_op jit(solution)/shard_map/far_panel/pallas_call | solution.py:103
  104.9 2.0 %collective-permute-start.6 = (f32[256,2048]{1,0:T(8,128)S(1)}, f32[256,2048]{1,0:T(8,128)S(1)}, u32[]{:S(2)}, u32[]{:S(2)}) collective-permute-start(f32[256,2048]{1,0:T(8,128)S(1)} %get-tuple-element.16), channel_id=1, source_target_pairs={{0,1},{1,0},{2,3},{3,2},{4,5},{5,4},{6,7},{7,6},{8,9},{9,8},{10,11... | collective-permute-start | bytes 6291464 | tf_op jit(solution)/shard_map/ppermute | solution.py:186
  107.0 1.8 near_panel.1
  108.8 2.2 %collective-permute-done.6 = f32[256,2048]{1,0:T(8,128)S(1)} collective-permute-done((f32[256,2048]{1,0:T(8,128)S(1)}, f32[256,2048]{1,0:T(8,128)S(1)}, u32[]{:S(2)}, u32[]{:S(2)}) %collective-permute-start.6) | collective-permute-done | bytes 2097184 | tf_op jit(solution)/shard_map/ppermute | solution.py:186
  111.0 0.3 add.24
  111.3 30.9 %all_to_all.15.value = f32[4,64,2048]{2,1,0:T(8,128)S(1)} all-to-all(f32[4,64,2048]{2,1,0:T(8,128)S(1)} %bitcast.17), channel_id=1, replica_groups=mesh['y'=4,'zl'=4,'row'=4,'x'=4,'core'=2] {'y'}, dimensions={0} | all-to-all | bytes 4194304 | tf_op jit(solution)/shard_map/all_to_all | solution.py:187
  142.2 1.8 arrange_rows.1
  144.1 36.2 %all_to_all.16 = f32[16,16,512]{2,1,0:T(8,128)S(1)} all-to-all(f32[16,16,512]{2,1,0:T(8,128)S(1)} %arrange_rows.1), channel_id=1, replica_groups=mesh['y'=4,'zl'=4,'row'=4,'x'=4,'core'=2] {'row','zl'}, dimensions={0} | all-to-all | bytes 1048576 | tf_op jit(solution)/shard_map/all_to_all | solution.py:189
  180.2 0.6 multiply_bitcast_fusion
  (21 shorter events, 0.6 us)
Async XLA Ops:
  6.5 93.2 %all-gather.3.cloned.1.call-start = ((), (), s32[]{:S(2)}) async-start(), calls=%async_computation.3 | async-start | bytes 1310720 | tf_op jit(solution)/shard_map/all_gather | solution.py:181
  6.6 1.2 copy-start.1
  9.3 25.5 %collective-permute-start = (bf16[512,256]{1,0:T(8,128)(2,1)S(1)}, bf16[512,256]{1,0:T(8,128)(2,1)S(1)}, u32[]{:S(2)}, u32[]{:S(2)}) collective-permute-start(bf16[512,256]{1,0:T(8,128)(2,1)S(1)} %get-tuple-element.12), channel_id=1, source_target_pairs={{0,16},{1,17},{8,24},{9,25},{16,0},{17,1},{24,8},{25,9},{2,18},{3,... | collective-permute-start | bytes 786440 | tf_op jit(solution)/shard_map/ppermute | solution.py:21
  25.0 22.6 %collective-permute-start.1 = (bf16[512,256]{1,0:T(8,128)(2,1)S(1)}, bf16[512,256]{1,0:T(8,128)(2,1)S(1)}, u32[]{:S(2)}, u32[]{:S(2)}) collective-permute-start(bf16[512,256]{1,0:T(8,128)(2,1)S(1)} %get-tuple-element.13), channel_id=1, source_target_pairs={{0,8},{1,25},{8,16},{9,1},{16,24},{17,9},{24,0},{25,17},{2,10},{3,... | collective-permute-start | bytes 786440 | tf_op jit(solution)/shard_map/ppermute | solution.py:21
  29.3 42.1 %collective-permute-start.2 = (bf16[512,256]{1,0:T(8,128)(2,1)S(1)}, bf16[512,256]{1,0:T(8,128)(2,1)S(1)}, u32[]{:S(2)}, u32[]{:S(2)}) collective-permute-start(bf16[512,256]{1,0:T(8,128)(2,1)S(1)} %get-tuple-element.14), channel_id=1, source_target_pairs={{0,24},{1,9},{8,0},{9,17},{16,8},{17,25},{24,16},{25,1},{2,26},{3,... | collective-permute-start | bytes 786440 | tf_op jit(solution)/shard_map/ppermute | solution.py:21
  34.8 47.0 %copy-start.2 = (s32[2048]{0:T(1024)S(1)}, s32[2048]{0:T(1024)}, u32[]{:S(2)}) copy-start(s32[2048]{0:T(1024)} %param.3) | copy-start | bytes 24580
  35.9 63.8 %all-to-all-start = ((bf16[4,512,256]{2,1,0:T(8,128)(2,1)}), bf16[4,512,256]{2,1,0:T(8,128)(2,1)S(1)}, u32[]{:S(2)}, u32[]{:S(2)}) async-start(bf16[4,512,256]{2,1,0:T(8,128)(2,1)} %broadcast_in_dim.9), calls=%async_computation | async-start | bytes 2097152 | tf_op jit(solution)/shard_map/all_to_all | solution.py:161
  71.4 18.2 %collective-permute-start.5 = (bf16[1024,256]{1,0:T(8,128)(2,1)S(1)}, bf16[1024,256]{1,0:T(8,128)(2,1)S(1)}, u32[]{:S(2)}, u32[]{:S(2)}) collective-permute-start(bf16[1024,256]{1,0:T(8,128)(2,1)S(1)} %constant_dynamic-update-slice_fusion.p0), channel_id=1, source_target_pairs={{0,4},{1,5},{2,6},{3,7},{4,0},{5,1},{6,2},{7,3},{8,12},{9,13},{10,... | collective-permute-start | bytes 1572872 | tf_op jit(solution)/shard_map/ppermute | solution.py:21
  74.7 25.0 %collective-permute-start.4 = (bf16[1024,256]{1,0:T(8,128)(2,1)S(1)}, bf16[1024,256]{1,0:T(8,128)(2,1)S(1)}, u32[]{:S(2)}, u32[]{:S(2)}) collective-permute-start(bf16[1024,256]{1,0:T(8,128)(2,1)S(1)} %constant_dynamic-update-slice_fusion.p0), channel_id=1, source_target_pairs={{0,6},{1,3},{2,0},{3,5},{4,2},{5,7},{6,4},{7,1},{8,14},{9,11},{10,... | collective-permute-start | bytes 1572872 | tf_op jit(solution)/shard_map/ppermute | solution.py:21
  76.6 23.0 %collective-permute-start.3 = (bf16[1024,256]{1,0:T(8,128)(2,1)S(1)}, bf16[1024,256]{1,0:T(8,128)(2,1)S(1)}, u32[]{:S(2)}, u32[]{:S(2)}) collective-permute-start(bf16[1024,256]{1,0:T(8,128)(2,1)S(1)} %constant_dynamic-update-slice_fusion.p0), channel_id=1, source_target_pairs={{0,2},{1,7},{2,4},{3,1},{4,6},{5,3},{6,0},{7,5},{8,10},{9,15},{10,... | collective-permute-start | bytes 1572872 | tf_op jit(solution)/shard_map/ppermute | solution.py:21
  99.7 1.2 copy-start
  104.9 6.1 %collective-permute-start.6 = (f32[256,2048]{1,0:T(8,128)S(1)}, f32[256,2048]{1,0:T(8,128)S(1)}, u32[]{:S(2)}, u32[]{:S(2)}) collective-permute-start(f32[256,2048]{1,0:T(8,128)S(1)} %get-tuple-element.16), channel_id=1, source_target_pairs={{0,1},{1,0},{2,3},{3,2},{4,5},{5,4},{6,7},{7,6},{8,9},{9,8},{10,11... | collective-permute-start | bytes 6291464 | tf_op jit(solution)/shard_map/ppermute | solution.py:186
Sparse Core Ops, SparseCore 0:
  9.5 37.0 all-gather.2

commit v5 on v4

--- a/solution.py
+++ b/solution.py
@@ -1,3 +1,5 @@
+import functools
+
 import jax
 import jax.numpy as jnp
 from jax import lax
@@ -50,74 +52,75 @@
     return [lax.rem(x + back, X) for back in (0, 3 + 2 * core, 1 + 2 * core, 2)]
 
 
-def rows_of(m, at, count, order, own, opposite, pairs):
-    if m in (0, 3):
-        ref = own if m == 0 else opposite
-        return [ref[slot, at : at + count, :] for slot in order]
-    at += (m - 1) * own.shape[1]
-    return [ref[at : at + count, :] for ref in pairs]
+def rows_of(source, at, count, order, arrays):
+    kind, which, start = source
+    at += start
+    if kind == "by_x":
+        return [arrays[which][slot, at : at + count, :] for slot in order]
+    if kind == "stack":
+        return [arrays[which][s, at : at + count, :] for s in range(X)]
+    return [arrays[i][at : at + count, :] for i in which]
 
 
 BLOCK = 256
 
 
-def multiply(left, out, blocks, order, own, opposite, pairs):
-    held = own.shape[1]
-    for to, m in enumerate(blocks):
+def multiply(left, out, sources, held, order, arrays):
+    for to, source in enumerate(sources):
         for at in range(0, held, BLOCK):
-            right = jnp.concatenate(rows_of(m, at, BLOCK, order, own, opposite, pairs), axis=1)
+            right = jnp.concatenate(rows_of(source, at, BLOCK, order, arrays), axis=1)
             out[:, to * held + at : to * held + at + BLOCK] = lax.dot_general(
                 left, right, (((1,), (1,)), ((), ())), preferred_element_type=jnp.float32
             )
 
 
-def far_kernel(place, wanted, own, opposite, p0, p1, p2, p3, far, chosen):
-    pairs = (p0, p1, p2, p3)
+def far_kernel(sources, held, place, wanted, *refs):
+    arrays, (far, chosen) = refs[:-2], refs[-2:]
     order = slots(place)
-    held = own.shape[1]
     values = []
     for at in range(0, wanted.shape[0], BLOCK):
         parts = [None] * X
-        for m in range(ROW):
+        for m, source in enumerate(sources):
             number = lax.broadcasted_iota(jnp.int32, (BLOCK, held), 1) + m * held
             pick = jnp.where(wanted[at : at + BLOCK, :] == number, 1.0, 0.0).astype(jnp.bfloat16)
-            for s, rows in enumerate(rows_of(m, 0, held, order, own, opposite, pairs)):
+            for s, rows in enumerate(rows_of(source, 0, held, order, arrays)):
                 term = jnp.dot(pick, rows, preferred_element_type=jnp.float32)
                 parts[s] = term if parts[s] is None else parts[s] + term
         values.append(jnp.concatenate(parts, axis=1).astype(jnp.bfloat16))
     chosen[...] = values[1]
-    multiply(values[0], far, (0, 2, 1, 3), order, own, opposite, pairs)
-
-
-def near_kernel(place, chosen, own, opposite, p0, p1, p2, p3, near):
-    multiply(chosen[...], near, (0, 1, 2, 3), slots(place), own, opposite, (p0, p1, p2, p3))
-
-
-def panels(place, wanted, own, opposite, pairs):
-    _, held, width = own.shape
+    multiply(values[0], far, [sources[m] for m in (0, 2, 1, 3)], held, order, arrays)
+
+
+def near_kernel(sources, held, place, chosen, *refs):
+    arrays, near = refs[:-1], refs[-1]
+    multiply(chosen[...], near, sources, held, slots(place), arrays)
+
+
+def panels(place, wanted, held, sources, arrays):
+    width = arrays[0].shape[-1]
     total, depth, half = held * ROW, width * X, wanted.shape[0] // CORE
     panel = jax.ShapeDtypeStruct((half, total), jnp.float32)
     cost = pl.CostEstimate(
         flops=2 * half * total * depth, bytes_accessed=2 * total * depth + 4 * half * total, transcendentals=0
     )
     far, chosen = pl.pallas_call(
-        far_kernel,
-        out_shape=[panel, jax.ShapeDtypeStruct((half, depth), own.dtype)],
-        in_specs=[SCALARS] + [FULL] * (3 + X),
+        functools.partial(far_kernel, sources, held),
+        out_shape=[panel, jax.ShapeDtypeStruct((half, depth), arrays[0].dtype)],
+        in_specs=[SCALARS] + [FULL] * (1 + len(arrays)),
         out_specs=[FULL] * 2,
         compiler_params=params(),
         cost_estimate=cost,
         name="far_panel",
-    )(place, wanted, own, opposite, *pairs)
+    )(place, wanted, *arrays)
     near = pl.pallas_call(
-        near_kernel,
+        functools.partial(near_kernel, sources, held),
         out_shape=panel,
-        in_specs=[SCALARS] + [FULL] * (3 + X),
+        in_specs=[SCALARS] + [FULL] * (1 + len(arrays)),
         out_specs=FULL,
         compiler_params=params(),
         cost_estimate=cost,
         name="near_panel",
-    )(place, chosen, own, opposite, *pairs)
+    )(place, chosen, *arrays)
     return far, near
 
 
@@ -178,11 +181,11 @@
     wanted = jnp.where(core == 0, mine[::-1], mine).reshape(total // X, 1)
     own, *sent = split(place, snapshots)
     near_a, near_b, opposite = [both_ways(value, "row", by) for value, by in zip(sent, STEPS)]
-    own = lax.all_gather(own, "x")
-    pair = jnp.concatenate([near_a, near_b], axis=0)
-    pairs = [pair] + [both_ways(pair, "x", by) for by in STEPS]
-    opposite = share(opposite)
-    far, near = panels(place, wanted, own, opposite, pairs)
+    group = jnp.concatenate([own, near_a, near_b], axis=0)
+    group = [group] + [both_ways(group, "x", by) for by in STEPS]
+    arrays = group + [opposite] + [both_ways(opposite, "x", by) for by in STEPS]
+    sources = [(None, (0, 1, 2, 3), m * held) for m in range(3)] + [(None, (4, 5, 6, 7), 0)]
+    far, near = panels(place, wanted, held, sources, arrays)
     near = near + lax.ppermute(far, "core", [(0, 1), (1, 0)])
     value = lax.all_to_all(near.reshape(Y, -1, total), "y", 0, 0, tiled=False)
     value = arrange(index.reshape(1, total), value)

time: 190 us -> 194 us (1.021)
  between operations: 13.6 us -> 0.23 us
  waiting for transfers between devices: 50.4 us -> 63.3 us
  starting transfers between devices: 42.6 us -> 47.8 us
    ppermute x6 -> x9, waiting for transfers between devices: 48.2 us -> 61.6 us  [both_ways(): return lax.ppermute(value, (axis, 'core'), pairs)]
    ppermute x6 -> x9, starting transfers between devices: 35.8 us -> 45.9 us  [both_ways(): return lax.ppermute(value, (axis, 'core'), pairs)]
    all_to_all x1 -> x0, starting transfers between devices: 4.77 us -> none  [share(): return lax.all_to_all(copies, 'x', 0, 0, tiled=False)]
  transfers between devices with their start and end apart: 9 -> 10, of which waited for: 5 -> 4; matrix products, arithmetic and copies ran while one was open for 1% -> 1% of each run, Pallas kernels for 1% -> 1%
where the time goes in v5:
time: 194 us; the launch traced here: 192 us
  blocking collectives  66.3 us (34%)
  waiting for transfers between devices  63.3 us (33%)
  starting transfers between devices  47.8 us (25%)
  Pallas kernels  9.49 us (5%)
  local copies, waits for them, and re-layouts  3.31 us (2%)
    ppermute x9, waiting for transfers between devices, both_ways(): return lax.ppermute(value, (axis, 'core'), pairs)  61.6 us
    ppermute x9, starting transfers between devices, both_ways(): return lax.ppermute(value, (axis, 'core'), pairs)  45.9 us
    all_to_all x1, blocking collectives, local(): value = lax.all_to_all(value, ('row', 'zl'), 0, 0, tiled=False)  35.4 us
    all_to_all x1, blocking collectives, local(): value = lax.all_to_all(near.reshape(Y, -1, total), 'y', 0, 0, tiled=False)  30.9 us
    pallas_call x1, Pallas kernels, panels(): pl.pallas_call(functools.partial(far_kernel, sources, held), out_shape=[p...  4.58 us
  transfers between devices with their start and end apart: 10, of which 4 were waited for; matrix products, arithmetic and copies ran while one was open for 1% of the time, Pallas kernels for 1%

profile of v5, /device:TPU:6, one launch (start us, length us, event | category | flops | bytes accessed | tf_op | source)
XLA Modules:
  0.0 191.5 jit_solution(10035919999391026118)
XLA Ops:
  0.1 1.2 copy-done.1
  1.3 0.7 split_cells.1
  2.0 9.1 %collective-permute-start = (bf16[512,256]{1,0:T(8,128)(2,1)S(1)}, bf16[512,256]{1,0:T(8,128)(2,1)S(1)}, u32[]{:S(2)}, u32[]{:S(2)}) collective-permute-start(bf16[512,256]{1,0:T(8,128)(2,1)S(1)} %get-tuple-element.12), channel_id=1, source_target_pairs={{0,8},{1,25},{8,16},{9,1},{16,24},{17,9},{24,0},{25,17},{2,10},{3,... | collective-permute-start | bytes 786440 | tf_op jit(solution)/shard_map/ppermute | solution.py:23
  11.1 5.6 %collective-permute-start.1 = (bf16[512,256]{1,0:T(8,128)(2,1)S(1)}, bf16[512,256]{1,0:T(8,128)(2,1)S(1)}, u32[]{:S(2)}, u32[]{:S(2)}) collective-permute-start(bf16[512,256]{1,0:T(8,128)(2,1)S(1)} %get-tuple-element.13), channel_id=1, source_target_pairs={{0,24},{1,9},{8,0},{9,17},{16,8},{17,25},{24,16},{25,1},{2,26},{3,... | collective-permute-start | bytes 786440 | tf_op jit(solution)/shard_map/ppermute | solution.py:23
  16.7 10.8 %collective-permute-start.5 = (bf16[512,256]{1,0:T(8,128)(2,1)S(1)}, bf16[512,256]{1,0:T(8,128)(2,1)S(1)}, u32[]{:S(2)}, u32[]{:S(2)}) collective-permute-start(bf16[512,256]{1,0:T(8,128)(2,1)S(1)} %get-tuple-element.14), channel_id=1, source_target_pairs={{0,16},{1,17},{8,24},{9,25},{16,0},{17,1},{24,8},{25,9},{2,18},{3,... | collective-permute-start | bytes 786440 | tf_op jit(solution)/shard_map/ppermute | solution.py:23
  27.6 29.5 %collective-permute-done.1 = bf16[512,256]{1,0:T(8,128)(2,1)S(1)} collective-permute-done((bf16[512,256]{1,0:T(8,128)(2,1)S(1)}, bf16[512,256]{1,0:T(8,128)(2,1)S(1)}, u32[]{:S(2)}, u32[]{:S(2)}) %collective-permute-start.1) | collective-permute-done | bytes 262176 | tf_op jit(solution)/shard_map/ppermute | solution.py:23
  57.1 3.3 %collective-permute-start.4 = (bf16[1536,256]{1,0:T(8,128)(2,1)S(1)}, bf16[1536,256]{1,0:T(8,128)(2,1)S(1)}, u32[]{:S(2)}, u32[]{:S(2)}) collective-permute-start(bf16[1536,256]{1,0:T(8,128)(2,1)S(1)} %constant_dynamic-update-slice_fusion.refs_0_), channel_id=1, source_target_pairs={{0,4},{1,5},{2,6},{3,7},{4,0},{5,1},{6,2},{7,3},{8,12},{9,13},{10,... | collective-permute-start | bytes 2359304 | tf_op jit(solution)/shard_map/ppermute | solution.py:23
  60.4 1.9 %collective-permute-start.3 = (bf16[1536,256]{1,0:T(8,128)(2,1)S(1)}, bf16[1536,256]{1,0:T(8,128)(2,1)S(1)}, u32[]{:S(2)}, u32[]{:S(2)}) collective-permute-start(bf16[1536,256]{1,0:T(8,128)(2,1)S(1)} %constant_dynamic-update-slice_fusion.refs_0_), channel_id=1, source_target_pairs={{0,6},{1,3},{2,0},{3,5},{4,2},{5,7},{6,4},{7,1},{8,14},{9,11},{10,... | collective-permute-start | bytes 2359304 | tf_op jit(solution)/shard_map/ppermute | solution.py:23
  62.3 5.1 %collective-permute-start.2 = (bf16[1536,256]{1,0:T(8,128)(2,1)S(1)}, bf16[1536,256]{1,0:T(8,128)(2,1)S(1)}, u32[]{:S(2)}, u32[]{:S(2)}) collective-permute-start(bf16[1536,256]{1,0:T(8,128)(2,1)S(1)} %constant_dynamic-update-slice_fusion.refs_0_), channel_id=1, source_target_pairs={{0,2},{1,7},{2,4},{3,1},{4,6},{5,3},{6,0},{7,5},{8,10},{9,15},{10,... | collective-permute-start | bytes 2359304 | tf_op jit(solution)/shard_map/ppermute | solution.py:23
  67.5 2.8 %collective-permute-start.8 = (bf16[512,256]{1,0:T(8,128)(2,1)S(1)}, bf16[512,256]{1,0:T(8,128)(2,1)}, u32[]{:S(2)}, u32[]{:S(2)}) collective-permute-start(bf16[512,256]{1,0:T(8,128)(2,1)S(1)} %collective-permute-done.5.refs_4_), channel_id=1, source_target_pairs={{0,4},{1,5},{2,6},{3,7},{4,0},{5,1},{6,2},{7,3},{8,12},{9,13},{10,... | collective-permute-start | bytes 786440 | tf_op jit(solution)/shard_map/ppermute | solution.py:23
  70.5 2.7 %collective-permute-start.7 = (bf16[512,256]{1,0:T(8,128)(2,1)S(1)}, bf16[512,256]{1,0:T(8,128)(2,1)}, u32[]{:S(2)}, u32[]{:S(2)}) collective-permute-start(bf16[512,256]{1,0:T(8,128)(2,1)S(1)} %collective-permute-done.5.refs_4_), channel_id=1, source_target_pairs={{0,6},{1,3},{2,0},{3,5},{4,2},{5,7},{6,4},{7,1},{8,14},{9,11},{10,... | collective-permute-start | bytes 786440 | tf_op jit(solution)/shard_map/ppermute | solution.py:23
  73.3 28.2 %collective-permute-done.8.refs_7_ = bf16[512,256]{1,0:T(8,128)(2,1)} collective-permute-done((bf16[512,256]{1,0:T(8,128)(2,1)S(1)}, bf16[512,256]{1,0:T(8,128)(2,1)}, u32[]{:S(2)}, u32[]{:S(2)}) %collective-permute-start.8) | collective-permute-done | bytes 262176 | tf_op jit(solution)/shard_map/ppermute | solution.py:23
  101.5 4.5 %collective-permute-start.6 = (bf16[512,256]{1,0:T(8,128)(2,1)S(1)}, bf16[512,256]{1,0:T(8,128)(2,1)}, u32[]{:S(2)}, u32[]{:S(2)}) collective-permute-start(bf16[512,256]{1,0:T(8,128)(2,1)S(1)} %collective-permute-done.5.refs_4_), channel_id=1, source_target_pairs={{0,2},{1,7},{2,4},{3,1},{4,6},{5,3},{6,0},{7,5},{8,10},{9,15},{10,... | collective-permute-start | bytes 786440 | tf_op jit(solution)/shard_map/ppermute | solution.py:23
  106.1 0.9 reshape.16.wanted
  107.0 3.8 %collective-permute-done.6.refs_5_ = bf16[512,256]{1,0:T(8,128)(2,1)} collective-permute-done((bf16[512,256]{1,0:T(8,128)(2,1)S(1)}, bf16[512,256]{1,0:T(8,128)(2,1)}, u32[]{:S(2)}, u32[]{:S(2)}) %collective-permute-start.6) | collective-permute-done | bytes 262176 | tf_op jit(solution)/shard_map/ppermute | solution.py:23
  110.8 0.9 copy-done
  111.8 4.6 %far_panel.1 = (f32[256,2048]{1,0:T(8,128)S(1)}, bf16[256,1024]{1,0:T(8,128)(2,1)S(1)}) custom-call(s32[3]{0:T(128)S(1)} %pad_add_fusion.place, s32[512,1]{1,0:T(8,128)S(1)} %copy-done, bf16[1536,256]{1,0:T(8,128)(2,1)S(1)} %constant_dynamic-update-slice_fusion.refs_0_, bf16[1536,256]{1,0:T(8,128)(2,1)S(1)} %collective-permute-done.2.refs_1_, ...), custom_call_target="tpu_custom_call" | custom-call | flops 1073741824 | bytes 6291456 | tf_op jit(solution)/shard_map/far_panel/pallas_call | solution.py:106
  116.4 1.9 %collective-permute-start.9 = (f32[256,2048]{1,0:T(8,128)S(1)}, f32[256,2048]{1,0:T(8,128)S(1)}, u32[]{:S(2)}, u32[]{:S(2)}) collective-permute-start(f32[256,2048]{1,0:T(8,128)S(1)} %get-tuple-element.16), channel_id=1, source_target_pairs={{0,1},{1,0},{2,3},{3,2},{4,5},{5,4},{6,7},{7,6},{8,9},{9,8},{10,11... | collective-permute-start | bytes 6291464 | tf_op jit(solution)/shard_map/ppermute | solution.py:189
  118.3 2.4 %near_panel.1 = f32[256,2048]{1,0:T(8,128)S(1)} custom-call(s32[3]{0:T(128)S(1)} %pad_add_fusion.place, bf16[256,1024]{1,0:T(8,128)(2,1)S(1)} %get-tuple-element.15.chosen, bf16[1536,256]{1,0:T(8,128)(2,1)S(1)} %constant_dynamic-update-slice_fusion.refs_0_, bf16[1536,256]{1,0:T(8,128)(2,1)S(1)} %collective-permute-done.2.refs_1_, ...), custom_call_target="tpu_custom_call" | custom-call | flops 1073741824 | bytes 6291456 | tf_op jit(solution)/shard_map/near_panel/pallas_call | solution.py:115
  120.7 1.7 collective-permute-done.9
  122.7 30.9 %all_to_all.10.value = f32[4,64,2048]{2,1,0:T(8,128)S(1)} all-to-all(f32[4,64,2048]{2,1,0:T(8,128)S(1)} %bitcast.14), channel_id=1, replica_groups=mesh['y'=4,'zl'=4,'row'=4,'x'=4,'core'=2] {'y'}, dimensions={0} | all-to-all | bytes 4194304 | tf_op jit(solution)/shard_map/all_to_all | solution.py:190
  153.6 1.8 arrange_rows.1
  155.5 35.4 %all_to_all.11 = f32[16,16,512]{2,1,0:T(8,128)S(1)} all-to-all(f32[16,16,512]{2,1,0:T(8,128)S(1)} %arrange_rows.1), channel_id=1, replica_groups=mesh['y'=4,'zl'=4,'row'=4,'x'=4,'core'=2] {'row','zl'}, dimensions={0} | all-to-all | bytes 1048576 | tf_op jit(solution)/shard_map/all_to_all | solution.py:192
  190.9 0.6 multiply_bitcast_fusion
  (22 shorter events, 0.7 us)
Async XLA Ops:
  0.0 70.3 %copy-start.2 = (s32[2048]{0:T(1024)S(1)}, s32[2048]{0:T(1024)}, u32[]{:S(2)}) copy-start(s32[2048]{0:T(1024)} %param.3) | copy-start | bytes 24580
  0.1 1.2 copy-start.1
  2.0 25.5 %collective-permute-start = (bf16[512,256]{1,0:T(8,128)(2,1)S(1)}, bf16[512,256]{1,0:T(8,128)(2,1)S(1)}, u32[]{:S(2)}, u32[]{:S(2)}) collective-permute-start(bf16[512,256]{1,0:T(8,128)(2,1)S(1)} %get-tuple-element.12), channel_id=1, source_target_pairs={{0,8},{1,25},{8,16},{9,1},{16,24},{17,9},{24,0},{25,17},{2,10},{3,... | collective-permute-start | bytes 786440 | tf_op jit(solution)/shard_map/ppermute | solution.py:23
  11.1 46.0 %collective-permute-start.1 = (bf16[512,256]{1,0:T(8,128)(2,1)S(1)}, bf16[512,256]{1,0:T(8,128)(2,1)S(1)}, u32[]{:S(2)}, u32[]{:S(2)}) collective-permute-start(bf16[512,256]{1,0:T(8,128)(2,1)S(1)} %get-tuple-element.13), channel_id=1, source_target_pairs={{0,24},{1,9},{8,0},{9,17},{16,8},{17,25},{24,16},{25,1},{2,26},{3,... | collective-permute-start | bytes 786440 | tf_op jit(solution)/shard_map/ppermute | solution.py:23
  16.7 50.8 %collective-permute-start.5 = (bf16[512,256]{1,0:T(8,128)(2,1)S(1)}, bf16[512,256]{1,0:T(8,128)(2,1)S(1)}, u32[]{:S(2)}, u32[]{:S(2)}) collective-permute-start(bf16[512,256]{1,0:T(8,128)(2,1)S(1)} %get-tuple-element.14), channel_id=1, source_target_pairs={{0,16},{1,17},{8,24},{9,25},{16,0},{17,1},{24,8},{25,9},{2,18},{3,... | collective-permute-start | bytes 786440 | tf_op jit(solution)/shard_map/ppermute | solution.py:23
  57.1 53.7 %collective-permute-start.4 = (bf16[1536,256]{1,0:T(8,128)(2,1)S(1)}, bf16[1536,256]{1,0:T(8,128)(2,1)S(1)}, u32[]{:S(2)}, u32[]{:S(2)}) collective-permute-start(bf16[1536,256]{1,0:T(8,128)(2,1)S(1)} %constant_dynamic-update-slice_fusion.refs_0_), channel_id=1, source_target_pairs={{0,4},{1,5},{2,6},{3,7},{4,0},{5,1},{6,2},{7,3},{8,12},{9,13},{10,... | collective-permute-start | bytes 2359304 | tf_op jit(solution)/shard_map/ppermute | solution.py:23
  60.4 50.4 %collective-permute-start.3 = (bf16[1536,256]{1,0:T(8,128)(2,1)S(1)}, bf16[1536,256]{1,0:T(8,128)(2,1)S(1)}, u32[]{:S(2)}, u32[]{:S(2)}) collective-permute-start(bf16[1536,256]{1,0:T(8,128)(2,1)S(1)} %constant_dynamic-update-slice_fusion.refs_0_), channel_id=1, source_target_pairs={{0,6},{1,3},{2,0},{3,5},{4,2},{5,7},{6,4},{7,1},{8,14},{9,11},{10,... | collective-permute-start | bytes 2359304 | tf_op jit(solution)/shard_map/ppermute | solution.py:23
  62.3 48.5 %collective-permute-start.2 = (bf16[1536,256]{1,0:T(8,128)(2,1)S(1)}, bf16[1536,256]{1,0:T(8,128)(2,1)S(1)}, u32[]{:S(2)}, u32[]{:S(2)}) collective-permute-start(bf16[1536,256]{1,0:T(8,128)(2,1)S(1)} %constant_dynamic-update-slice_fusion.refs_0_), channel_id=1, source_target_pairs={{0,2},{1,7},{2,4},{3,1},{4,6},{5,3},{6,0},{7,5},{8,10},{9,15},{10,... | collective-permute-start | bytes 2359304 | tf_op jit(solution)/shard_map/ppermute | solution.py:23
  67.5 34.0 %collective-permute-start.8 = (bf16[512,256]{1,0:T(8,128)(2,1)S(1)}, bf16[512,256]{1,0:T(8,128)(2,1)}, u32[]{:S(2)}, u32[]{:S(2)}) collective-permute-start(bf16[512,256]{1,0:T(8,128)(2,1)S(1)} %collective-permute-done.5.refs_4_), channel_id=1, source_target_pairs={{0,4},{1,5},{2,6},{3,7},{4,0},{5,1},{6,2},{7,3},{8,12},{9,13},{10,... | collective-permute-start | bytes 786440 | tf_op jit(solution)/shard_map/ppermute | solution.py:23
  70.5 36.5 %collective-permute-start.7 = (bf16[512,256]{1,0:T(8,128)(2,1)S(1)}, bf16[512,256]{1,0:T(8,128)(2,1)}, u32[]{:S(2)}, u32[]{:S(2)}) collective-permute-start(bf16[512,256]{1,0:T(8,128)(2,1)S(1)} %collective-permute-done.5.refs_4_), channel_id=1, source_target_pairs={{0,6},{1,3},{2,0},{3,5},{4,2},{5,7},{6,4},{7,1},{8,14},{9,11},{10,... | collective-permute-start | bytes 786440 | tf_op jit(solution)/shard_map/ppermute | solution.py:23
  101.5 9.3 %collective-permute-start.6 = (bf16[512,256]{1,0:T(8,128)(2,1)S(1)}, bf16[512,256]{1,0:T(8,128)(2,1)}, u32[]{:S(2)}, u32[]{:S(2)}) collective-permute-start(bf16[512,256]{1,0:T(8,128)(2,1)S(1)} %collective-permute-done.5.refs_4_), channel_id=1, source_target_pairs={{0,2},{1,7},{2,4},{3,1},{4,6},{5,3},{6,0},{7,5},{8,10},{9,15},{10,... | collective-permute-start | bytes 786440 | tf_op jit(solution)/shard_map/ppermute | solution.py:23
  110.8 1.0 copy-start
  116.4 6.1 %collective-permute-start.9 = (f32[256,2048]{1,0:T(8,128)S(1)}, f32[256,2048]{1,0:T(8,128)S(1)}, u32[]{:S(2)}, u32[]{:S(2)}) collective-permute-start(f32[256,2048]{1,0:T(8,128)S(1)} %get-tuple-element.16), channel_id=1, source_target_pairs={{0,1},{1,0},{2,3},{3,2},{4,5},{5,4},{6,7},{7,6},{8,9},{9,8},{10,11... | collective-permute-start | bytes 6291464 | tf_op jit(solution)/shard_map/ppermute | solution.py:189

commit v6 on v5

--- a/solution.py
+++ b/solution.py
@@ -25,10 +25,11 @@
 
 def split_kernel(place, source, *outs):
     row, core = place[0], place[1]
-    width = outs[0].shape[1]
+    width = outs[0].shape[-1]
     for out, step in zip(outs, (0, 1 + 2 * core, 3 + 2 * core, 2)):
         start = lax.rem(row + step, ROW) * width
-        out[...] = source[:, pl.ds(pl.multiple_of(start, width), width)]
+        part = source[:, pl.ds(pl.multiple_of(start, width), width)]
+        out[...] = jnp.broadcast_to(part, out.shape)
 
 
 STEPS = (1, 3, 2)
@@ -39,7 +40,8 @@
     width = cells // ROW
     return pl.pallas_call(
         split_kernel,
-        out_shape=[jax.ShapeDtypeStruct((held, width), snapshots.dtype)] * ROW,
+        out_shape=[jax.ShapeDtypeStruct((X, held, width), snapshots.dtype)]
+        + [jax.ShapeDtypeStruct((held, width), snapshots.dtype)] * (ROW - 1),
         in_specs=[SCALARS, FULL],
         out_specs=[FULL] * ROW,
         compiler_params=params(),
@@ -160,8 +162,9 @@
 
 
 def share(value):
-    copies = jnp.broadcast_to(value[None], (X,) + value.shape)
-    return lax.all_to_all(copies, "x", 0, 0, tiled=False)
+    if value.ndim == 2:
+        value = jnp.broadcast_to(value[None], (X,) + value.shape)
+    return lax.all_to_all(value, "x", 0, 0, tiled=False)
 
 
 def local(snapshots, snapshot_order):
@@ -181,10 +184,10 @@
     wanted = jnp.where(core == 0, mine[::-1], mine).reshape(total // X, 1)
     own, *sent = split(place, snapshots)
     near_a, near_b, opposite = [both_ways(value, "row", by) for value, by in zip(sent, STEPS)]
-    group = jnp.concatenate([own, near_a, near_b], axis=0)
-    group = [group] + [both_ways(group, "x", by) for by in STEPS]
-    arrays = group + [opposite] + [both_ways(opposite, "x", by) for by in STEPS]
-    sources = [(None, (0, 1, 2, 3), m * held) for m in range(3)] + [(None, (4, 5, 6, 7), 0)]
+    arrays = [share(own), share(near_a)]
+    for value in (near_b, opposite):
+        arrays += [value] + [both_ways(value, "x", by) for by in STEPS]
+    sources = [("by_x", 0, 0), ("by_x", 1, 0), (None, (2, 3, 4, 5), 0), (None, (6, 7, 8, 9), 0)]
     far, near = panels(place, wanted, held, sources, arrays)
     near = near + lax.ppermute(far, "core", [(0, 1), (1, 0)])
     value = lax.all_to_all(near.reshape(Y, -1, total), "y", 0, 0, tiled=False)

time: 194 us -> 176 us (0.907)
  waiting for transfers between devices: 63.3 us -> 7.48 us
  starting transfers between devices: 47.8 us -> 76.3 us
  blocking collectives: 66.3 us -> 73.6 us
    ppermute x9, waiting for transfers between devices: 61.6 us -> 5.76 us  [both_ways(): return lax.ppermute(value, (axis, 'core'), pairs)]
    ppermute x9, starting transfers between devices: 45.9 us -> 60.3 us  [both_ways(): return lax.ppermute(value, (axis, 'core'), pairs)]
    all_to_all x0 -> x2, starting transfers between devices: none -> 14.1 us  [share(): return lax.all_to_all(value, 'x', 0, 0, tiled=False)]
    all_to_all x1, blocking collectives: 35.4 us -> 42.7 us  [local(): value = lax.all_to_all(value, ('row', 'zl'), 0, 0, tiled=False)]
  transfers between devices with their start and end apart: 10 -> 12, of which waited for: 4 -> 4; matrix products, arithmetic and copies ran while one was open for 1% -> 1% of each run, Pallas kernels for 1% -> 1%
where the time goes in v6:
time: 176 us; the launch traced here: 174 us
  starting transfers between devices  76.3 us (43%)
  blocking collectives  73.6 us (42%)
  Pallas kernels  10.6 us (6%)
  waiting for transfers between devices  7.48 us (4%)
  local copies, waits for them, and re-layouts  4.33 us (2%)
    ppermute x9, starting transfers between devices, both_ways(): return lax.ppermute(value, (axis, 'core'), pairs)  60.3 us
    all_to_all x1, blocking collectives, local(): value = lax.all_to_all(value, ('row', 'zl'), 0, 0, tiled=False)  42.7 us
    all_to_all x1, blocking collectives, local(): value = lax.all_to_all(near.reshape(Y, -1, total), 'y', 0, 0, tiled=False)  30.9 us
    all_to_all x2, starting transfers between devices, share(): return lax.all_to_all(value, 'x', 0, 0, tiled=False)  14.1 us
    ppermute x9, waiting for transfers between devices, both_ways(): return lax.ppermute(value, (axis, 'core'), pairs)  5.76 us
    pallas_call x1, Pallas kernels, panels(): pl.pallas_call(functools.partial(far_kernel, sources, held), out_shape=[p...  4.59 us
  transfers between devices with their start and end apart: 12, of which 4 were waited for; matrix products, arithmetic and copies ran while one was open for 1% of the time, Pallas kernels for 1%

profile of v6, /device:TPU:6, one launch (start us, length us, event | category | flops | bytes accessed | tf_op | source)
XLA Modules:
  0.0 173.7 jit_solution(11101179191064716542)
XLA Ops:
  0.1 1.2 copy-done.1
  1.3 1.8 %split_cells.1 = (bf16[4,512,256]{2,1,0:T(8,128)(2,1)}, bf16[512,256]{1,0:T(8,128)(2,1)S(1)}, bf16[512,256]{1,0:T(8,128)(2,1)S(1)}, bf16[512,256]{1,0:T(8,128)(2,1)}) custom-call(s32[3]{0:T(128)S(1)} %pad_add_fusion.place, bf16[512,1024]{1,0:T(8,128)(2,1)S(1)} %copy-done.1), custom_call_target="tpu_custom_call" | custom-call | tf_op jit(solution)/shard_map/split_cells/pallas_call | solution.py:41
  3.1 9.3 %all-to-all-start = ((bf16[4,512,256]{2,1,0:T(8,128)(2,1)}), bf16[4,512,256]{2,1,0:T(8,128)(2,1)S(1)}, u32[]{:S(2)}, u32[]{:S(2)}) async-start(bf16[4,512,256]{2,1,0:T(8,128)(2,1)} %get-tuple-element.11), calls=%async_computation | async-start | bytes 2097152 | tf_op jit(solution)/shard_map/all_to_all | solution.py:167
  12.4 4.6 %collective-permute-start = (bf16[512,256]{1,0:T(8,128)(2,1)S(1)}, bf16[512,256]{1,0:T(8,128)(2,1)S(1)}, u32[]{:S(2)}, u32[]{:S(2)}) collective-permute-start(bf16[512,256]{1,0:T(8,128)(2,1)S(1)} %get-tuple-element.12), channel_id=1, source_target_pairs={{0,8},{1,25},{8,16},{9,1},{16,24},{17,9},{24,0},{25,17},{2,10},{3,... | collective-permute-start | bytes 786440 | tf_op jit(solution)/shard_map/ppermute | solution.py:23
  17.1 5.6 %collective-permute-start.1 = (bf16[512,256]{1,0:T(8,128)(2,1)S(1)}, bf16[512,256]{1,0:T(8,128)(2,1)S(1)}, u32[]{:S(2)}, u32[]{:S(2)}) collective-permute-start(bf16[512,256]{1,0:T(8,128)(2,1)S(1)} %get-tuple-element.13), channel_id=1, source_target_pairs={{0,24},{1,9},{8,0},{9,17},{16,8},{17,25},{24,16},{25,1},{2,26},{3,... | collective-permute-start | bytes 786440 | tf_op jit(solution)/shard_map/ppermute | solution.py:23
  22.6 2.7 %collective-permute-done = bf16[512,256]{1,0:T(8,128)(2,1)S(1)} collective-permute-done((bf16[512,256]{1,0:T(8,128)(2,1)S(1)}, bf16[512,256]{1,0:T(8,128)(2,1)S(1)}, u32[]{:S(2)}, u32[]{:S(2)}) %collective-permute-start) | collective-permute-done | bytes 262176 | tf_op jit(solution)/shard_map/ppermute | solution.py:23
  25.3 1.0 broadcast_in_dim.9
  26.4 4.8 %all-to-all-start.1 = ((bf16[4,512,256]{2,1,0:T(8,128)(2,1)}), bf16[4,512,256]{2,1,0:T(8,128)(2,1)S(1)}, u32[]{:S(2)}, u32[]{:S(2)}) async-start(bf16[4,512,256]{2,1,0:T(8,128)(2,1)} %broadcast_in_dim.9), calls=%async_computation.1 | async-start | bytes 2097152 | tf_op jit(solution)/shard_map/all_to_all | solution.py:167
  31.2 29.8 %collective-permute-start.5 = (bf16[512,256]{1,0:T(8,128)(2,1)}, bf16[512,256]{1,0:T(8,128)(2,1)S(1)}, u32[]{:S(2)}, u32[]{:S(2)}) collective-permute-start(bf16[512,256]{1,0:T(8,128)(2,1)} %get-tuple-element.14), channel_id=1, source_target_pairs={{0,16},{1,17},{8,24},{9,25},{16,0},{17,1},{24,8},{25,9},{2,18},{3,... | collective-permute-start | bytes 786440 | tf_op jit(solution)/shard_map/ppermute | solution.py:23
  61.0 3.4 %collective-permute-start.4 = (bf16[512,256]{1,0:T(8,128)(2,1)S(1)}, bf16[512,256]{1,0:T(8,128)(2,1)S(1)}, u32[]{:S(2)}, u32[]{:S(2)}) collective-permute-start(bf16[512,256]{1,0:T(8,128)(2,1)S(1)} %collective-permute-done.1.refs_2_), channel_id=1, source_target_pairs={{0,4},{1,5},{2,6},{3,7},{4,0},{5,1},{6,2},{7,3},{8,12},{9,13},{10,... | collective-permute-start | bytes 786440 | tf_op jit(solution)/shard_map/ppermute | solution.py:23
  64.6 1.9 %collective-permute-start.3 = (bf16[512,256]{1,0:T(8,128)(2,1)S(1)}, bf16[512,256]{1,0:T(8,128)(2,1)S(1)}, u32[]{:S(2)}, u32[]{:S(2)}) collective-permute-start(bf16[512,256]{1,0:T(8,128)(2,1)S(1)} %collective-permute-done.1.refs_2_), channel_id=1, source_target_pairs={{0,6},{1,3},{2,0},{3,5},{4,2},{5,7},{6,4},{7,1},{8,14},{9,11},{10,... | collective-permute-start | bytes 786440 | tf_op jit(solution)/shard_map/ppermute | solution.py:23
  66.5 5.1 %collective-permute-start.2 = (bf16[512,256]{1,0:T(8,128)(2,1)S(1)}, bf16[512,256]{1,0:T(8,128)(2,1)S(1)}, u32[]{:S(2)}, u32[]{:S(2)}) collective-permute-start(bf16[512,256]{1,0:T(8,128)(2,1)S(1)} %collective-permute-done.1.refs_2_), channel_id=1, source_target_pairs={{0,2},{1,7},{2,4},{3,1},{4,6},{5,3},{6,0},{7,5},{8,10},{9,15},{10,... | collective-permute-start | bytes 786440 | tf_op jit(solution)/shard_map/ppermute | solution.py:23
  71.7 2.8 %collective-permute-start.8 = (bf16[512,256]{1,0:T(8,128)(2,1)S(1)}, bf16[512,256]{1,0:T(8,128)(2,1)}, u32[]{:S(2)}, u32[]{:S(2)}) collective-permute-start(bf16[512,256]{1,0:T(8,128)(2,1)S(1)} %collective-permute-done.5.refs_6_), channel_id=1, source_target_pairs={{0,4},{1,5},{2,6},{3,7},{4,0},{5,1},{6,2},{7,3},{8,12},{9,13},{10,... | collective-permute-start | bytes 786440 | tf_op jit(solution)/shard_map/ppermute | solution.py:23
  74.4 2.8 %collective-permute-start.7 = (bf16[512,256]{1,0:T(8,128)(2,1)S(1)}, bf16[512,256]{1,0:T(8,128)(2,1)}, u32[]{:S(2)}, u32[]{:S(2)}) collective-permute-start(bf16[512,256]{1,0:T(8,128)(2,1)S(1)} %collective-permute-done.5.refs_6_), channel_id=1, source_target_pairs={{0,6},{1,3},{2,0},{3,5},{4,2},{5,7},{6,4},{7,1},{8,14},{9,11},{10,... | collective-permute-start | bytes 786440 | tf_op jit(solution)/shard_map/ppermute | solution.py:23
  77.2 4.3 %collective-permute-start.6 = (bf16[512,256]{1,0:T(8,128)(2,1)S(1)}, bf16[512,256]{1,0:T(8,128)(2,1)}, u32[]{:S(2)}, u32[]{:S(2)}) collective-permute-start(bf16[512,256]{1,0:T(8,128)(2,1)S(1)} %collective-permute-done.5.refs_6_), channel_id=1, source_target_pairs={{0,2},{1,7},{2,4},{3,1},{4,6},{5,3},{6,0},{7,5},{8,10},{9,15},{10,... | collective-permute-start | bytes 786440 | tf_op jit(solution)/shard_map/ppermute | solution.py:23
  82.6 2.9 %collective-permute-done.7.refs_8_ = bf16[512,256]{1,0:T(8,128)(2,1)} collective-permute-done((bf16[512,256]{1,0:T(8,128)(2,1)S(1)}, bf16[512,256]{1,0:T(8,128)(2,1)}, u32[]{:S(2)}, u32[]{:S(2)}) %collective-permute-start.7) | collective-permute-done | bytes 262176 | tf_op jit(solution)/shard_map/ppermute | solution.py:23
  85.6 0.9 copy-done
  86.6 4.6 %far_panel.1 = (f32[256,2048]{1,0:T(8,128)S(1)}, bf16[256,1024]{1,0:T(8,128)(2,1)S(1)}) custom-call(s32[3]{0:T(128)S(1)} %pad_add_fusion.place, s32[512,1]{1,0:T(8,128)S(1)} %copy-done, bf16[4,512,256]{2,1,0:T(8,128)(2,1)S(1)} %all-to-all-done.refs_0_, bf16[4,512,256]{2,1,0:T(8,128)(2,1)S(1)} %all-to-all-done.1.refs_1_, ...), custom_call_target="tpu_custom_call" | custom-call | flops 1073741824 | bytes 6291456 | tf_op jit(solution)/shard_map/far_panel/pallas_call | solution.py:108
  91.2 1.9 %collective-permute-start.9 = (f32[256,2048]{1,0:T(8,128)S(1)}, f32[256,2048]{1,0:T(8,128)S(1)}, u32[]{:S(2)}, u32[]{:S(2)}) collective-permute-start(f32[256,2048]{1,0:T(8,128)S(1)} %get-tuple-element.16), channel_id=1, source_target_pairs={{0,1},{1,0},{2,3},{3,2},{4,5},{5,4},{6,7},{7,6},{8,9},{9,8},{10,11... | collective-permute-start | bytes 6291464 | tf_op jit(solution)/shard_map/ppermute | solution.py:192
  93.1 2.4 %near_panel.1 = f32[256,2048]{1,0:T(8,128)S(1)} custom-call(s32[3]{0:T(128)S(1)} %pad_add_fusion.place, bf16[256,1024]{1,0:T(8,128)(2,1)S(1)} %get-tuple-element.15.chosen, bf16[4,512,256]{2,1,0:T(8,128)(2,1)S(1)} %all-to-all-done.refs_0_, bf16[4,512,256]{2,1,0:T(8,128)(2,1)S(1)} %all-to-all-done.1.refs_1_, ...), custom_call_target="tpu_custom_call" | custom-call | flops 1073741824 | bytes 6291456 | tf_op jit(solution)/shard_map/near_panel/pallas_call | solution.py:117
  95.5 1.7 collective-permute-done.9
  97.5 30.9 %all_to_all.20.value = f32[4,64,2048]{2,1,0:T(8,128)S(1)} all-to-all(f32[4,64,2048]{2,1,0:T(8,128)S(1)} %bitcast.14), channel_id=1, replica_groups=mesh['y'=4,'zl'=4,'row'=4,'x'=4,'core'=2] {'y'}, dimensions={0} | all-to-all | bytes 4194304 | tf_op jit(solution)/shard_map/all_to_all | solution.py:193
  128.4 1.8 %arrange_rows.1 = f32[16,16,512]{2,1,0:T(8,128)S(1)} custom-call(s32[1,2048]{1,0:T(1,128)S(1)} %bitcast.13, f32[4,64,2048]{2,1,0:T(8,128)S(1)} %all_to_all.20.value), custom_call_target="tpu_custom_call" | custom-call | flops 1610612736 | bytes 2621440 | tf_op jit(solution)/shard_map/arrange_rows/pallas_call | solution.py:151
  130.3 42.7 %all_to_all.21 = f32[16,16,512]{2,1,0:T(8,128)S(1)} all-to-all(f32[16,16,512]{2,1,0:T(8,128)S(1)} %arrange_rows.1), channel_id=1, replica_groups=mesh['y'=4,'zl'=4,'row'=4,'x'=4,'core'=2] {'row','zl'}, dimensions={0} | all-to-all | bytes 1048576 | tf_op jit(solution)/shard_map/all_to_all | solution.py:195
  (24 shorter events, 2.4 us)
Async XLA Ops:
  0.1 1.2 copy-start.1
  3.1 22.3 %all-to-all-start = ((bf16[4,512,256]{2,1,0:T(8,128)(2,1)}), bf16[4,512,256]{2,1,0:T(8,128)(2,1)S(1)}, u32[]{:S(2)}, u32[]{:S(2)}) async-start(bf16[4,512,256]{2,1,0:T(8,128)(2,1)} %get-tuple-element.11), calls=%async_computation | async-start | bytes 2097152 | tf_op jit(solution)/shard_map/all_to_all | solution.py:167
  12.4 52.0 %copy-start.2 = (s32[2048]{0:T(1024)S(1)}, s32[2048]{0:T(1024)}, u32[]{:S(2)}) copy-start(s32[2048]{0:T(1024)} %param.3) | copy-start | bytes 24580
  12.4 12.9 %collective-permute-start = (bf16[512,256]{1,0:T(8,128)(2,1)S(1)}, bf16[512,256]{1,0:T(8,128)(2,1)S(1)}, u32[]{:S(2)}, u32[]{:S(2)}) collective-permute-start(bf16[512,256]{1,0:T(8,128)(2,1)S(1)} %get-tuple-element.12), channel_id=1, source_target_pairs={{0,8},{1,25},{8,16},{9,1},{16,24},{17,9},{24,0},{25,17},{2,10},{3,... | collective-permute-start | bytes 786440 | tf_op jit(solution)/shard_map/ppermute | solution.py:23
  17.1 44.0 %collective-permute-start.1 = (bf16[512,256]{1,0:T(8,128)(2,1)S(1)}, bf16[512,256]{1,0:T(8,128)(2,1)S(1)}, u32[]{:S(2)}, u32[]{:S(2)}) collective-permute-start(bf16[512,256]{1,0:T(8,128)(2,1)S(1)} %get-tuple-element.13), channel_id=1, source_target_pairs={{0,24},{1,9},{8,0},{9,17},{16,8},{17,25},{24,16},{25,1},{2,26},{3,... | collective-permute-start | bytes 786440 | tf_op jit(solution)/shard_map/ppermute | solution.py:23
  26.4 59.2 %all-to-all-start.1 = ((bf16[4,512,256]{2,1,0:T(8,128)(2,1)}), bf16[4,512,256]{2,1,0:T(8,128)(2,1)S(1)}, u32[]{:S(2)}, u32[]{:S(2)}) async-start(bf16[4,512,256]{2,1,0:T(8,128)(2,1)} %broadcast_in_dim.9), calls=%async_computation.1 | async-start | bytes 2097152 | tf_op jit(solution)/shard_map/all_to_all | solution.py:167
  31.2 40.5 %collective-permute-start.5 = (bf16[512,256]{1,0:T(8,128)(2,1)}, bf16[512,256]{1,0:T(8,128)(2,1)S(1)}, u32[]{:S(2)}, u32[]{:S(2)}) collective-permute-start(bf16[512,256]{1,0:T(8,128)(2,1)} %get-tuple-element.14), channel_id=1, source_target_pairs={{0,16},{1,17},{8,24},{9,25},{16,0},{17,1},{24,8},{25,9},{2,18},{3,... | collective-permute-start | bytes 786440 | tf_op jit(solution)/shard_map/ppermute | solution.py:23
  61.0 16.2 %collective-permute-start.4 = (bf16[512,256]{1,0:T(8,128)(2,1)S(1)}, bf16[512,256]{1,0:T(8,128)(2,1)S(1)}, u32[]{:S(2)}, u32[]{:S(2)}) collective-permute-start(bf16[512,256]{1,0:T(8,128)(2,1)S(1)} %collective-permute-done.1.refs_2_), channel_id=1, source_target_pairs={{0,4},{1,5},{2,6},{3,7},{4,0},{5,1},{6,2},{7,3},{8,12},{9,13},{10,... | collective-permute-start | bytes 786440 | tf_op jit(solution)/shard_map/ppermute | solution.py:23
  64.6 18.0 %collective-permute-start.3 = (bf16[512,256]{1,0:T(8,128)(2,1)S(1)}, bf16[512,256]{1,0:T(8,128)(2,1)S(1)}, u32[]{:S(2)}, u32[]{:S(2)}) collective-permute-start(bf16[512,256]{1,0:T(8,128)(2,1)S(1)} %collective-permute-done.1.refs_2_), channel_id=1, source_target_pairs={{0,6},{1,3},{2,0},{3,5},{4,2},{5,7},{6,4},{7,1},{8,14},{9,11},{10,... | collective-permute-start | bytes 786440 | tf_op jit(solution)/shard_map/ppermute | solution.py:23
  66.5 16.0 %collective-permute-start.2 = (bf16[512,256]{1,0:T(8,128)(2,1)S(1)}, bf16[512,256]{1,0:T(8,128)(2,1)S(1)}, u32[]{:S(2)}, u32[]{:S(2)}) collective-permute-start(bf16[512,256]{1,0:T(8,128)(2,1)S(1)} %collective-permute-done.1.refs_2_), channel_id=1, source_target_pairs={{0,2},{1,7},{2,4},{3,1},{4,6},{5,3},{6,0},{7,5},{8,10},{9,15},{10,... | collective-permute-start | bytes 786440 | tf_op jit(solution)/shard_map/ppermute | solution.py:23
  71.7 10.9 %collective-permute-start.8 = (bf16[512,256]{1,0:T(8,128)(2,1)S(1)}, bf16[512,256]{1,0:T(8,128)(2,1)}, u32[]{:S(2)}, u32[]{:S(2)}) collective-permute-start(bf16[512,256]{1,0:T(8,128)(2,1)S(1)} %collective-permute-done.5.refs_6_), channel_id=1, source_target_pairs={{0,4},{1,5},{2,6},{3,7},{4,0},{5,1},{6,2},{7,3},{8,12},{9,13},{10,... | collective-permute-start | bytes 786440 | tf_op jit(solution)/shard_map/ppermute | solution.py:23
  74.4 11.0 %collective-permute-start.7 = (bf16[512,256]{1,0:T(8,128)(2,1)S(1)}, bf16[512,256]{1,0:T(8,128)(2,1)}, u32[]{:S(2)}, u32[]{:S(2)}) collective-permute-start(bf16[512,256]{1,0:T(8,128)(2,1)S(1)} %collective-permute-done.5.refs_6_), channel_id=1, source_target_pairs={{0,6},{1,3},{2,0},{3,5},{4,2},{5,7},{6,4},{7,1},{8,14},{9,11},{10,... | collective-permute-start | bytes 786440 | tf_op jit(solution)/shard_map/ppermute | solution.py:23
  77.2 8.4 %collective-permute-start.6 = (bf16[512,256]{1,0:T(8,128)(2,1)S(1)}, bf16[512,256]{1,0:T(8,128)(2,1)}, u32[]{:S(2)}, u32[]{:S(2)}) collective-permute-start(bf16[512,256]{1,0:T(8,128)(2,1)S(1)} %collective-permute-done.5.refs_6_), channel_id=1, source_target_pairs={{0,2},{1,7},{2,4},{3,1},{4,6},{5,3},{6,0},{7,5},{8,10},{9,15},{10,... | collective-permute-start | bytes 786440 | tf_op jit(solution)/shard_map/ppermute | solution.py:23
  85.6 1.0 copy-start
  91.2 6.1 %collective-permute-start.9 = (f32[256,2048]{1,0:T(8,128)S(1)}, f32[256,2048]{1,0:T(8,128)S(1)}, u32[]{:S(2)}, u32[]{:S(2)}) collective-permute-start(f32[256,2048]{1,0:T(8,128)S(1)} %get-tuple-element.16), channel_id=1, source_target_pairs={{0,1},{1,0},{2,3},{3,2},{4,5},{5,4},{6,7},{7,6},{8,9},{9,8},{10,11... | collective-permute-start | bytes 6291464 | tf_op jit(solution)/shard_map/ppermute | solution.py:192

commit v7 on v6

--- a/solution.py
+++ b/solution.py
@@ -76,15 +76,15 @@
             )
 
 
-def far_kernel(sources, held, place, wanted, *refs):
+def far_kernel(sources, held, place, far_wanted, near_wanted, *refs):
     arrays, (far, chosen) = refs[:-2], refs[-2:]
     order = slots(place)
     values = []
-    for at in range(0, wanted.shape[0], BLOCK):
+    for wanted in (far_wanted, near_wanted):
         parts = [None] * X
         for m, source in enumerate(sources):
-            number = lax.broadcasted_iota(jnp.int32, (BLOCK, held), 1) + m * held
-            pick = jnp.where(wanted[at : at + BLOCK, :] == number, 1.0, 0.0).astype(jnp.bfloat16)
+            number = lax.broadcasted_iota(jnp.int32, (wanted.shape[0], held), 1) + m * held
+            pick = jnp.where(wanted[...] == number, 1.0, 0.0).astype(jnp.bfloat16)
             for s, rows in enumerate(rows_of(source, 0, held, order, arrays)):
                 term = jnp.dot(pick, rows, preferred_element_type=jnp.float32)
                 parts[s] = term if parts[s] is None else parts[s] + term
@@ -100,7 +100,7 @@
 
 def panels(place, wanted, held, sources, arrays):
     width = arrays[0].shape[-1]
-    total, depth, half = held * ROW, width * X, wanted.shape[0] // CORE
+    total, depth, half = held * ROW, width * X, wanted[0].shape[0]
     panel = jax.ShapeDtypeStruct((half, total), jnp.float32)
     cost = pl.CostEstimate(
         flops=2 * half * total * depth, bytes_accessed=2 * total * depth + 4 * half * total, transcendentals=0
@@ -108,12 +108,12 @@
     far, chosen = pl.pallas_call(
         functools.partial(far_kernel, sources, held),
         out_shape=[panel, jax.ShapeDtypeStruct((half, depth), arrays[0].dtype)],
-        in_specs=[SCALARS] + [FULL] * (1 + len(arrays)),
+        in_specs=[SCALARS] + [FULL] * (2 + len(arrays)),
         out_specs=[FULL] * 2,
         compiler_params=params(),
         cost_estimate=cost,
         name="far_panel",
-    )(place, wanted, *arrays)
+    )(place, *wanted, *arrays)
     near = pl.pallas_call(
         functools.partial(near_kernel, sources, held),
         out_shape=panel,
@@ -181,13 +181,18 @@
     mine = index.reshape(Y, ZL, X, CORE, -1)
     mine = lax.dynamic_index_in_dim(mine, lax.axis_index("x"), 2, keepdims=False)
     mine = mine.transpose(2, 0, 1, 3)
-    wanted = jnp.where(core == 0, mine[::-1], mine).reshape(total // X, 1)
+    wanted = [
+        jnp.where(core == 0, mine[1], mine[0]).reshape(-1, 1),
+        jnp.where(core == 0, mine[0], mine[1]).reshape(-1, 1),
+    ]
     own, *sent = split(place, snapshots)
-    near_a, near_b, opposite = [both_ways(value, "row", by) for value, by in zip(sent, STEPS)]
-    arrays = [share(own), share(near_a)]
-    for value in (near_b, opposite):
+    near_a, near_b = [both_ways(value, "row", by) for value, by in zip(sent[:2], STEPS)]
+    far_sent, near_b = lax.optimization_barrier((sent[2], near_b))
+    opposite = both_ways(far_sent, "row", 2)
+    arrays = [share(own)]
+    for value in (near_a, near_b, opposite):
         arrays += [value] + [both_ways(value, "x", by) for by in STEPS]
-    sources = [("by_x", 0, 0), ("by_x", 1, 0), (None, (2, 3, 4, 5), 0), (None, (6, 7, 8, 9), 0)]
+    sources = [("by_x", 0, 0)] + [(None, tuple(range(1 + X * m, 1 + X * m + X)), 0) for m in range(3)]
     far, near = panels(place, wanted, held, sources, arrays)
     near = near + lax.ppermute(far, "core", [(0, 1), (1, 0)])
     value = lax.all_to_all(near.reshape(Y, -1, total), "y", 0, 0, tiled=False)

time: 176 us -> 175 us (level)
  waiting for transfers between devices: 7.48 us -> 28.2 us
  blocking collectives: 73.6 us -> 62.5 us
  starting transfers between devices: 76.3 us -> 65.9 us
    ppermute x9 -> x12, waiting for transfers between devices: 5.76 us -> 26.6 us  [both_ways(): return lax.ppermute(value, (axis, 'core'), pairs)]
    all_to_all x1, blocking collectives: 42.7 us -> 31.6 us  [local(): value = lax.all_to_all(value, ('row', 'zl'), 0, 0, tiled=False)]
    all_to_all x2 -> x1, starting transfers between devices: 14.1 us -> 4.78 us  [share(): return lax.all_to_all(value, 'x', 0, 0, tiled=False)]
    select_n x1 -> x2, local copies, waits for them, and re-layouts: 0.01 us -> 2.26 us  [the longest x1 1.46 us: local(): jnp.where(core == 0, mine[1], mine[0]).reshape(-1, 1)]
    ppermute x9 -> x12, starting transfers between devices: 60.3 us -> 59.1 us  [both_ways(): return lax.ppermute(value, (axis, 'core'), pairs)]
  transfers between devices with their start and end apart: 12 -> 14, of which waited for: 4 -> 5; matrix products, arithmetic and copies ran while one was open for 1% -> 2% of each run, Pallas kernels for 1% -> 1%
where the time goes in v7:
time: 175 us; the launch traced here: 174 us
  starting transfers between devices  65.9 us (38%)
  blocking collectives  62.5 us (36%)
  waiting for transfers between devices  28.2 us (16%)
  Pallas kernels  10.6 us (6%)
  local copies, waits for them, and re-layouts  4.54 us (3%)
    ppermute x12, starting transfers between devices, both_ways(): return lax.ppermute(value, (axis, 'core'), pairs)  59.1 us
    all_to_all x1, blocking collectives, local(): value = lax.all_to_all(value, ('row', 'zl'), 0, 0, tiled=False)  31.6 us
    all_to_all x1, blocking collectives, local(): value = lax.all_to_all(near.reshape(Y, -1, total), 'y', 0, 0, tiled=False)  30.9 us
    ppermute x12, waiting for transfers between devices, both_ways(): return lax.ppermute(value, (axis, 'core'), pairs)  26.6 us
    all_to_all x1, starting transfers between devices, share(): return lax.all_to_all(value, 'x', 0, 0, tiled=False)  4.78 us
    pallas_call x1, Pallas kernels, panels(): pl.pallas_call(functools.partial(far_kernel, sources, held), out_shape=[p...  4.59 us
  transfers between devices with their start and end apart: 14, of which 5 were waited for; matrix products, arithmetic and copies ran while one was open for 2% of the time, Pallas kernels for 1%

profile of v7, /device:TPU:6, one launch (start us, length us, event | category | flops | bytes accessed | tf_op | source)
XLA Modules:
  0.0 173.7 jit_solution(11069689483226169036)
XLA Ops:
  1.3 1.8 %split_cells.1 = (bf16[4,512,256]{2,1,0:T(8,128)(2,1)}, bf16[512,256]{1,0:T(8,128)(2,1)S(1)}, bf16[512,256]{1,0:T(8,128)(2,1)S(1)}, bf16[512,256]{1,0:T(8,128)(2,1)}) custom-call(s32[3]{0:T(128)S(1)} %pad_add_fusion.place, bf16[512,1024]{1,0:T(8,128)(2,1)S(1)} %copy-done), custom_call_target="tpu_custom_call" | custom-call | tf_op jit(solution)/shard_map/split_cells/pallas_call | solution.py:41
  3.1 9.1 %collective-permute-start = (bf16[512,256]{1,0:T(8,128)(2,1)S(1)}, bf16[512,256]{1,0:T(8,128)(2,1)S(1)}, u32[]{:S(2)}, u32[]{:S(2)}) collective-permute-start(bf16[512,256]{1,0:T(8,128)(2,1)S(1)} %get-tuple-element.14), channel_id=1, source_target_pairs={{0,8},{1,25},{8,16},{9,1},{16,24},{17,9},{24,0},{25,17},{2,10},{3,... | collective-permute-start | bytes 786440 | tf_op jit(solution)/shard_map/ppermute | solution.py:23
  12.2 5.6 %collective-permute-start.4 = (bf16[512,256]{1,0:T(8,128)(2,1)S(1)}, bf16[512,256]{1,0:T(8,128)(2,1)S(1)}, u32[]{:S(2)}, u32[]{:S(2)}) collective-permute-start(bf16[512,256]{1,0:T(8,128)(2,1)S(1)} %get-tuple-element.16), channel_id=1, source_target_pairs={{0,24},{1,9},{8,0},{9,17},{16,8},{17,25},{24,16},{25,1},{2,26},{3,... | collective-permute-start | bytes 786440 | tf_op jit(solution)/shard_map/ppermute | solution.py:23
  17.7 4.8 %all-to-all-start = ((bf16[4,512,256]{2,1,0:T(8,128)(2,1)}), bf16[4,512,256]{2,1,0:T(8,128)(2,1)S(1)}, u32[]{:S(2)}, u32[]{:S(2)}) async-start(bf16[4,512,256]{2,1,0:T(8,128)(2,1)} %get-tuple-element.13), calls=%async_computation | async-start | bytes 2097152 | tf_op jit(solution)/shard_map/all_to_all | solution.py:167
  22.5 3.4 %collective-permute-start.3 = (bf16[512,256]{1,0:T(8,128)(2,1)S(1)}, bf16[512,256]{1,0:T(8,128)(2,1)S(1)}, u32[]{:S(2)}, u32[]{:S(2)}) collective-permute-start(bf16[512,256]{1,0:T(8,128)(2,1)S(1)} %collective-permute-done.refs_1_), channel_id=1, source_target_pairs={{0,4},{1,5},{2,6},{3,7},{4,0},{5,1},{6,2},{7,3},{8,12},{9,13},{10,... | collective-permute-start | bytes 786440 | tf_op jit(solution)/shard_map/ppermute | solution.py:23
  25.9 12.4 %collective-permute-done.4.refs_5_ = bf16[512,256]{1,0:T(8,128)(2,1)S(1)} collective-permute-done((bf16[512,256]{1,0:T(8,128)(2,1)S(1)}, bf16[512,256]{1,0:T(8,128)(2,1)S(1)}, u32[]{:S(2)}, u32[]{:S(2)}) %collective-permute-start.4) | collective-permute-done | bytes 262176 | tf_op jit(solution)/shard_map/ppermute | solution.py:23
  38.3 2.7 %collective-permute-start.2 = (bf16[512,256]{1,0:T(8,128)(2,1)S(1)}, bf16[512,256]{1,0:T(8,128)(2,1)S(1)}, u32[]{:S(2)}, u32[]{:S(2)}) collective-permute-start(bf16[512,256]{1,0:T(8,128)(2,1)S(1)} %collective-permute-done.refs_1_), channel_id=1, source_target_pairs={{0,6},{1,3},{2,0},{3,5},{4,2},{5,7},{6,4},{7,1},{8,14},{9,11},{10,... | collective-permute-start | bytes 786440 | tf_op jit(solution)/shard_map/ppermute | solution.py:23
  41.0 14.4 %collective-permute-start.8 = (bf16[512,256]{1,0:T(8,128)(2,1)}, bf16[512,256]{1,0:T(8,128)(2,1)S(1)}, u32[]{:S(2)}, u32[]{:S(2)}) collective-permute-start(bf16[512,256]{1,0:T(8,128)(2,1)} %get-tuple-element.18), channel_id=1, source_target_pairs={{0,16},{1,17},{8,24},{9,25},{16,0},{17,1},{24,8},{25,9},{2,18},{3,... | collective-permute-start | bytes 786440 | tf_op jit(solution)/shard_map/ppermute | solution.py:23
  55.4 5.1 %collective-permute-start.1 = (bf16[512,256]{1,0:T(8,128)(2,1)S(1)}, bf16[512,256]{1,0:T(8,128)(2,1)S(1)}, u32[]{:S(2)}, u32[]{:S(2)}) collective-permute-start(bf16[512,256]{1,0:T(8,128)(2,1)S(1)} %collective-permute-done.refs_1_), channel_id=1, source_target_pairs={{0,2},{1,7},{2,4},{3,1},{4,6},{5,3},{6,0},{7,5},{8,10},{9,15},{10,... | collective-permute-start | bytes 786440 | tf_op jit(solution)/shard_map/ppermute | solution.py:23
  60.6 2.8 %collective-permute-start.7 = (bf16[512,256]{1,0:T(8,128)(2,1)S(1)}, bf16[512,256]{1,0:T(8,128)(2,1)S(1)}, u32[]{:S(2)}, u32[]{:S(2)}) collective-permute-start(bf16[512,256]{1,0:T(8,128)(2,1)S(1)} %collective-permute-done.4.refs_5_), channel_id=1, source_target_pairs={{0,4},{1,5},{2,6},{3,7},{4,0},{5,1},{6,2},{7,3},{8,12},{9,13},{10,... | collective-permute-start | bytes 786440 | tf_op jit(solution)/shard_map/ppermute | solution.py:23
  63.4 2.7 %collective-permute-start.6 = (bf16[512,256]{1,0:T(8,128)(2,1)S(1)}, bf16[512,256]{1,0:T(8,128)(2,1)S(1)}, u32[]{:S(2)}, u32[]{:S(2)}) collective-permute-start(bf16[512,256]{1,0:T(8,128)(2,1)S(1)} %collective-permute-done.4.refs_5_), channel_id=1, source_target_pairs={{0,6},{1,3},{2,0},{3,5},{4,2},{5,7},{6,4},{7,1},{8,14},{9,11},{10,... | collective-permute-start | bytes 786440 | tf_op jit(solution)/shard_map/ppermute | solution.py:23
  66.2 4.3 %collective-permute-start.5 = (bf16[512,256]{1,0:T(8,128)(2,1)S(1)}, bf16[512,256]{1,0:T(8,128)(2,1)S(1)}, u32[]{:S(2)}, u32[]{:S(2)}) collective-permute-start(bf16[512,256]{1,0:T(8,128)(2,1)S(1)} %collective-permute-done.4.refs_5_), channel_id=1, source_target_pairs={{0,2},{1,7},{2,4},{3,1},{4,6},{5,3},{6,0},{7,5},{8,10},{9,15},{10,... | collective-permute-start | bytes 786440 | tf_op jit(solution)/shard_map/ppermute | solution.py:23
  70.5 8.6 %collective-permute-done.8.refs_9_ = bf16[512,256]{1,0:T(8,128)(2,1)S(1)} collective-permute-done((bf16[512,256]{1,0:T(8,128)(2,1)}, bf16[512,256]{1,0:T(8,128)(2,1)S(1)}, u32[]{:S(2)}, u32[]{:S(2)}) %collective-permute-start.8) | collective-permute-done | bytes 262176 | tf_op jit(solution)/shard_map/ppermute | solution.py:23
  79.1 1.9 %collective-permute-start.11 = (bf16[512,256]{1,0:T(8,128)(2,1)S(1)}, bf16[512,256]{1,0:T(8,128)(2,1)}, u32[]{:S(2)}, u32[]{:S(2)}) collective-permute-start(bf16[512,256]{1,0:T(8,128)(2,1)S(1)} %collective-permute-done.8.refs_9_), channel_id=1, source_target_pairs={{0,4},{1,5},{2,6},{3,7},{4,0},{5,1},{6,2},{7,3},{8,12},{9,13},{10,... | collective-permute-start | bytes 786440 | tf_op jit(solution)/shard_map/ppermute | solution.py:23
  81.0 4.6 %collective-permute-start.10 = (bf16[512,256]{1,0:T(8,128)(2,1)S(1)}, bf16[512,256]{1,0:T(8,128)(2,1)}, u32[]{:S(2)}, u32[]{:S(2)}) collective-permute-start(bf16[512,256]{1,0:T(8,128)(2,1)S(1)} %collective-permute-done.8.refs_9_), channel_id=1, source_target_pairs={{0,6},{1,3},{2,0},{3,5},{4,2},{5,7},{6,4},{7,1},{8,14},{9,11},{10,... | collective-permute-start | bytes 786440 | tf_op jit(solution)/shard_map/ppermute | solution.py:23
  85.6 2.5 %collective-permute-start.9 = (bf16[512,256]{1,0:T(8,128)(2,1)S(1)}, bf16[512,256]{1,0:T(8,128)(2,1)}, u32[]{:S(2)}, u32[]{:S(2)}) collective-permute-start(bf16[512,256]{1,0:T(8,128)(2,1)S(1)} %collective-permute-done.8.refs_9_), channel_id=1, source_target_pairs={{0,2},{1,7},{2,4},{3,1},{4,6},{5,3},{6,0},{7,5},{8,10},{9,15},{10,... | collective-permute-start | bytes 786440 | tf_op jit(solution)/shard_map/ppermute | solution.py:23
  91.6 5.2 %collective-permute-done.10.refs_11_ = bf16[512,256]{1,0:T(8,128)(2,1)} collective-permute-done((bf16[512,256]{1,0:T(8,128)(2,1)S(1)}, bf16[512,256]{1,0:T(8,128)(2,1)}, u32[]{:S(2)}, u32[]{:S(2)}) %collective-permute-start.10) | collective-permute-done | bytes 262176 | tf_op jit(solution)/shard_map/ppermute | solution.py:23
  97.7 4.6 %far_panel.1 = (f32[256,2048]{1,0:T(8,128)S(1)}, bf16[256,1024]{1,0:T(8,128)(2,1)S(1)}) custom-call(s32[3]{0:T(128)S(1)} %pad_add_fusion.place, s32[256,1]{1,0:T(8,128)S(1)} %copy-done.1, s32[256,1]{1,0:T(8,128)S(1)} %select_n.76.near_wanted, bf16[4,512,256]{2,1,0:T(8,128)(2,1)S(1)} %all-to-all-done.refs_0_, ...), custom_call_target="tpu_custom_call" | custom-call | flops 1073741824 | bytes 6291456 | tf_op jit(solution)/shard_map/far_panel/pallas_call | solution.py:108
  102.3 2.0 %collective-permute-start.12 = (f32[256,2048]{1,0:T(8,128)S(1)}, f32[256,2048]{1,0:T(8,128)S(1)}, u32[]{:S(2)}, u32[]{:S(2)}) collective-permute-start(f32[256,2048]{1,0:T(8,128)S(1)} %get-tuple-element.20), channel_id=1, source_target_pairs={{0,1},{1,0},{2,3},{3,2},{4,5},{5,4},{6,7},{7,6},{8,9},{9,8},{10,11... | collective-permute-start | bytes 6291464 | tf_op jit(solution)/shard_map/ppermute | solution.py:197
  104.3 2.4 %near_panel.1 = f32[256,2048]{1,0:T(8,128)S(1)} custom-call(s32[3]{0:T(128)S(1)} %pad_add_fusion.place, bf16[256,1024]{1,0:T(8,128)(2,1)S(1)} %get-tuple-element.19.chosen, bf16[4,512,256]{2,1,0:T(8,128)(2,1)S(1)} %all-to-all-done.refs_0_, bf16[512,256]{1,0:T(8,128)(2,1)S(1)} %collective-permute-done.refs_1_, ...), custom_call_target="tpu_custom_call" | custom-call | flops 1073741824 | bytes 6291456 | tf_op jit(solution)/shard_map/near_panel/pallas_call | solution.py:117
  106.7 1.6 collective-permute-done.12
  108.7 30.9 %all_to_all.15.value = f32[4,64,2048]{2,1,0:T(8,128)S(1)} all-to-all(f32[4,64,2048]{2,1,0:T(8,128)S(1)} %bitcast.12), channel_id=1, replica_groups=mesh['y'=4,'zl'=4,'row'=4,'x'=4,'core'=2] {'y'}, dimensions={0} | all-to-all | bytes 4194304 | tf_op jit(solution)/shard_map/all_to_all | solution.py:198
  139.6 1.8 %arrange_rows.1 = f32[16,16,512]{2,1,0:T(8,128)S(1)} custom-call(s32[1,2048]{1,0:T(1,128)S(1)} %bitcast.11, f32[4,64,2048]{2,1,0:T(8,128)S(1)} %all_to_all.15.value), custom_call_target="tpu_custom_call" | custom-call | flops 1610612736 | bytes 2621440 | tf_op jit(solution)/shard_map/arrange_rows/pallas_call | solution.py:151
  141.4 31.6 %all_to_all.16 = f32[16,16,512]{2,1,0:T(8,128)S(1)} all-to-all(f32[16,16,512]{2,1,0:T(8,128)S(1)} %arrange_rows.1), channel_id=1, replica_groups=mesh['y'=4,'zl'=4,'row'=4,'x'=4,'core'=2] {'row','zl'}, dimensions={0} | all-to-all | bytes 1048576 | tf_op jit(solution)/shard_map/all_to_all | solution.py:200
  (26 shorter events, 6.6 us)
Async XLA Ops:
  0.0 88.1 %copy-start.2 = (s32[2048]{0:T(1024)S(1)}, s32[2048]{0:T(1024)}, u32[]{:S(2)}) copy-start(s32[2048]{0:T(1024)} %param.3) | copy-start | bytes 24580
  0.1 1.2 copy-start
  3.1 19.4 %collective-permute-start = (bf16[512,256]{1,0:T(8,128)(2,1)S(1)}, bf16[512,256]{1,0:T(8,128)(2,1)S(1)}, u32[]{:S(2)}, u32[]{:S(2)}) collective-permute-start(bf16[512,256]{1,0:T(8,128)(2,1)S(1)} %get-tuple-element.14), channel_id=1, source_target_pairs={{0,8},{1,25},{8,16},{9,1},{16,24},{17,9},{24,0},{25,17},{2,10},{3,... | collective-permute-start | bytes 786440 | tf_op jit(solution)/shard_map/ppermute | solution.py:23
  12.2 26.1 %collective-permute-start.4 = (bf16[512,256]{1,0:T(8,128)(2,1)S(1)}, bf16[512,256]{1,0:T(8,128)(2,1)S(1)}, u32[]{:S(2)}, u32[]{:S(2)}) collective-permute-start(bf16[512,256]{1,0:T(8,128)(2,1)S(1)} %get-tuple-element.16), channel_id=1, source_target_pairs={{0,24},{1,9},{8,0},{9,17},{16,8},{17,25},{24,16},{25,1},{2,26},{3,... | collective-permute-start | bytes 786440 | tf_op jit(solution)/shard_map/ppermute | solution.py:23
  17.7 79.0 %all-to-all-start = ((bf16[4,512,256]{2,1,0:T(8,128)(2,1)}), bf16[4,512,256]{2,1,0:T(8,128)(2,1)S(1)}, u32[]{:S(2)}, u32[]{:S(2)}) async-start(bf16[4,512,256]{2,1,0:T(8,128)(2,1)} %get-tuple-element.13), calls=%async_computation | async-start | bytes 2097152 | tf_op jit(solution)/shard_map/all_to_all | solution.py:167
  22.5 40.9 %collective-permute-start.3 = (bf16[512,256]{1,0:T(8,128)(2,1)S(1)}, bf16[512,256]{1,0:T(8,128)(2,1)S(1)}, u32[]{:S(2)}, u32[]{:S(2)}) collective-permute-start(bf16[512,256]{1,0:T(8,128)(2,1)S(1)} %collective-permute-done.refs_1_), channel_id=1, source_target_pairs={{0,4},{1,5},{2,6},{3,7},{4,0},{5,1},{6,2},{7,3},{8,12},{9,13},{10,... | collective-permute-start | bytes 786440 | tf_op jit(solution)/shard_map/ppermute | solution.py:23
  38.3 27.9 %collective-permute-start.2 = (bf16[512,256]{1,0:T(8,128)(2,1)S(1)}, bf16[512,256]{1,0:T(8,128)(2,1)S(1)}, u32[]{:S(2)}, u32[]{:S(2)}) collective-permute-start(bf16[512,256]{1,0:T(8,128)(2,1)S(1)} %collective-permute-done.refs_1_), channel_id=1, source_target_pairs={{0,6},{1,3},{2,0},{3,5},{4,2},{5,7},{6,4},{7,1},{8,14},{9,11},{10,... | collective-permute-start | bytes 786440 | tf_op jit(solution)/shard_map/ppermute | solution.py:23
  41.0 38.1 %collective-permute-start.8 = (bf16[512,256]{1,0:T(8,128)(2,1)}, bf16[512,256]{1,0:T(8,128)(2,1)S(1)}, u32[]{:S(2)}, u32[]{:S(2)}) collective-permute-start(bf16[512,256]{1,0:T(8,128)(2,1)} %get-tuple-element.18), channel_id=1, source_target_pairs={{0,16},{1,17},{8,24},{9,25},{16,0},{17,1},{24,8},{25,9},{2,18},{3,... | collective-permute-start | bytes 786440 | tf_op jit(solution)/shard_map/ppermute | solution.py:23
  55.4 25.6 %collective-permute-start.1 = (bf16[512,256]{1,0:T(8,128)(2,1)S(1)}, bf16[512,256]{1,0:T(8,128)(2,1)S(1)}, u32[]{:S(2)}, u32[]{:S(2)}) collective-permute-start(bf16[512,256]{1,0:T(8,128)(2,1)S(1)} %collective-permute-done.refs_1_), channel_id=1, source_target_pairs={{0,2},{1,7},{2,4},{3,1},{4,6},{5,3},{6,0},{7,5},{8,10},{9,15},{10,... | collective-permute-start | bytes 786440 | tf_op jit(solution)/shard_map/ppermute | solution.py:23
  60.6 25.1 %collective-permute-start.7 = (bf16[512,256]{1,0:T(8,128)(2,1)S(1)}, bf16[512,256]{1,0:T(8,128)(2,1)S(1)}, u32[]{:S(2)}, u32[]{:S(2)}) collective-permute-start(bf16[512,256]{1,0:T(8,128)(2,1)S(1)} %collective-permute-done.4.refs_5_), channel_id=1, source_target_pairs={{0,4},{1,5},{2,6},{3,7},{4,0},{5,1},{6,2},{7,3},{8,12},{9,13},{10,... | collective-permute-start | bytes 786440 | tf_op jit(solution)/shard_map/ppermute | solution.py:23
  63.4 27.8 %collective-permute-start.6 = (bf16[512,256]{1,0:T(8,128)(2,1)S(1)}, bf16[512,256]{1,0:T(8,128)(2,1)S(1)}, u32[]{:S(2)}, u32[]{:S(2)}) collective-permute-start(bf16[512,256]{1,0:T(8,128)(2,1)S(1)} %collective-permute-done.4.refs_5_), channel_id=1, source_target_pairs={{0,6},{1,3},{2,0},{3,5},{4,2},{5,7},{6,4},{7,1},{8,14},{9,11},{10,... | collective-permute-start | bytes 786440 | tf_op jit(solution)/shard_map/ppermute | solution.py:23
  66.2 25.1 %collective-permute-start.5 = (bf16[512,256]{1,0:T(8,128)(2,1)S(1)}, bf16[512,256]{1,0:T(8,128)(2,1)S(1)}, u32[]{:S(2)}, u32[]{:S(2)}) collective-permute-start(bf16[512,256]{1,0:T(8,128)(2,1)S(1)} %collective-permute-done.4.refs_5_), channel_id=1, source_target_pairs={{0,2},{1,7},{2,4},{3,1},{4,6},{5,3},{6,0},{7,5},{8,10},{9,15},{10,... | collective-permute-start | bytes 786440 | tf_op jit(solution)/shard_map/ppermute | solution.py:23
  79.1 12.4 %collective-permute-start.11 = (bf16[512,256]{1,0:T(8,128)(2,1)S(1)}, bf16[512,256]{1,0:T(8,128)(2,1)}, u32[]{:S(2)}, u32[]{:S(2)}) collective-permute-start(bf16[512,256]{1,0:T(8,128)(2,1)S(1)} %collective-permute-done.8.refs_9_), channel_id=1, source_target_pairs={{0,4},{1,5},{2,6},{3,7},{4,0},{5,1},{6,2},{7,3},{8,12},{9,13},{10,... | collective-permute-start | bytes 786440 | tf_op jit(solution)/shard_map/ppermute | solution.py:23
  81.0 15.7 %collective-permute-start.10 = (bf16[512,256]{1,0:T(8,128)(2,1)S(1)}, bf16[512,256]{1,0:T(8,128)(2,1)}, u32[]{:S(2)}, u32[]{:S(2)}) collective-permute-start(bf16[512,256]{1,0:T(8,128)(2,1)S(1)} %collective-permute-done.8.refs_9_), channel_id=1, source_target_pairs={{0,6},{1,3},{2,0},{3,5},{4,2},{5,7},{6,4},{7,1},{8,14},{9,11},{10,... | collective-permute-start | bytes 786440 | tf_op jit(solution)/shard_map/ppermute | solution.py:23
  85.6 11.1 %collective-permute-start.9 = (bf16[512,256]{1,0:T(8,128)(2,1)S(1)}, bf16[512,256]{1,0:T(8,128)(2,1)}, u32[]{:S(2)}, u32[]{:S(2)}) collective-permute-start(bf16[512,256]{1,0:T(8,128)(2,1)S(1)} %collective-permute-done.8.refs_9_), channel_id=1, source_target_pairs={{0,2},{1,7},{2,4},{3,1},{4,6},{5,3},{6,0},{7,5},{8,10},{9,15},{10,... | collective-permute-start | bytes 786440 | tf_op jit(solution)/shard_map/ppermute | solution.py:23
  96.8 0.9 copy-start.1
  102.3 6.1 %collective-permute-start.12 = (f32[256,2048]{1,0:T(8,128)S(1)}, f32[256,2048]{1,0:T(8,128)S(1)}, u32[]{:S(2)}, u32[]{:S(2)}) collective-permute-start(f32[256,2048]{1,0:T(8,128)S(1)} %get-tuple-element.20), channel_id=1, source_target_pairs={{0,1},{1,0},{2,3},{3,2},{4,5},{5,4},{6,7},{7,6},{8,9},{9,8},{10,11... | collective-permute-start | bytes 6291464 | tf_op jit(solution)/shard_map/ppermute | solution.py:197

commit v8 on v7

--- a/solution.py
+++ b/solution.py
@@ -76,26 +76,22 @@
             )
 
 
-def far_kernel(sources, held, place, far_wanted, near_wanted, *refs):
-    arrays, (far, chosen) = refs[:-2], refs[-2:]
-    order = slots(place)
-    values = []
-    for wanted in (far_wanted, near_wanted):
-        parts = [None] * X
-        for m, source in enumerate(sources):
-            number = lax.broadcasted_iota(jnp.int32, (wanted.shape[0], held), 1) + m * held
-            pick = jnp.where(wanted[...] == number, 1.0, 0.0).astype(jnp.bfloat16)
-            for s, rows in enumerate(rows_of(source, 0, held, order, arrays)):
-                term = jnp.dot(pick, rows, preferred_element_type=jnp.float32)
-                parts[s] = term if parts[s] is None else parts[s] + term
-        values.append(jnp.concatenate(parts, axis=1).astype(jnp.bfloat16))
-    chosen[...] = values[1]
-    multiply(values[0], far, [sources[m] for m in (0, 2, 1, 3)], held, order, arrays)
+def pick_columns(wanted, sources, held, order, arrays):
+    parts = [None] * X
+    for m, source in enumerate(sources):
+        number = lax.broadcasted_iota(jnp.int32, (wanted.shape[0], held), 1) + m * held
+        pick = jnp.where(wanted[...] == number, 1.0, 0.0).astype(jnp.bfloat16)
+        for s, rows in enumerate(rows_of(source, 0, held, order, arrays)):
+            term = jnp.dot(pick, rows, preferred_element_type=jnp.float32)
+            parts[s] = term if parts[s] is None else parts[s] + term
+    return jnp.concatenate(parts, axis=1).astype(jnp.bfloat16)
 
 
-def near_kernel(sources, held, place, chosen, *refs):
-    arrays, near = refs[:-1], refs[-1]
-    multiply(chosen[...], near, sources, held, slots(place), arrays)
+def panel_kernel(sources, lanes_of, held, place, wanted, *refs):
+    arrays, out = refs[:-1], refs[-1]
+    order = slots(place)
+    chosen = pick_columns(wanted, sources, held, order, arrays)
+    multiply(chosen, out, [sources[m] for m in lanes_of], held, order, arrays)
 
 
 def panels(place, wanted, held, sources, arrays):
@@ -105,25 +101,18 @@
     cost = pl.CostEstimate(
         flops=2 * half * total * depth, bytes_accessed=2 * total * depth + 4 * half * total, transcendentals=0
     )
-    far, chosen = pl.pallas_call(
-        functools.partial(far_kernel, sources, held),
-        out_shape=[panel, jax.ShapeDtypeStruct((half, depth), arrays[0].dtype)],
-        in_specs=[SCALARS] + [FULL] * (2 + len(arrays)),
-        out_specs=[FULL] * 2,
-        compiler_params=params(),
-        cost_estimate=cost,
-        name="far_panel",
-    )(place, *wanted, *arrays)
-    near = pl.pallas_call(
-        functools.partial(near_kernel, sources, held),
-        out_shape=panel,
-        in_specs=[SCALARS] + [FULL] * (1 + len(arrays)),
-        out_specs=FULL,
-        compiler_params=params(),
-        cost_estimate=cost,
-        name="near_panel",
-    )(place, chosen, *arrays)
-    return far, near
+    def call(columns, lanes_of, name):
+        return pl.pallas_call(
+            functools.partial(panel_kernel, sources, lanes_of, held),
+            out_shape=panel,
+            in_specs=[SCALARS] + [FULL] * (1 + len(arrays)),
+            out_specs=FULL,
+            compiler_params=params(),
+            cost_estimate=cost,
+            name=name,
+        )(place, columns, *arrays)
+
+    return call(wanted[0], (0, 2, 1, 3), "far_panel"), call(wanted[1], (0, 1, 2, 3), "near_panel")
 
 
 def arrange_kernel(order, value, out):

time: 175 us -> 197 us (1.13)
  local copies, waits for them, and re-layouts: 4.54 us -> 30.2 us
  waiting for transfers between devices: 28.2 us -> 22.8 us
    unnamed x6 -> x70, local copies, waits for them, and re-layouts: 2.13 us -> 29.1 us
    ppermute x12, waiting for transfers between devices: 26.6 us -> 22.8 us  [both_ways(): return lax.ppermute(value, (axis, 'core'), pairs)]
  transfers between devices with their start and end apart: 14 -> 14, of which waited for: 5 -> 3; matrix products, arithmetic and copies ran while one was open for 2% -> 1% of each run, Pallas kernels for 1% -> 2%
where the time goes in v8:
time: 197 us; the launch traced here: 196 us
  starting transfers between devices  65.7 us (33%)
  blocking collectives  63.8 us (32%)
  local copies, waits for them, and re-layouts  30.2 us (15%)
  waiting for transfers between devices  22.8 us (12%)
  Pallas kernels  9.38 us (5%)
  other arithmetic  3.33 us (2%)
    ppermute x12, starting transfers between devices, both_ways(): return lax.ppermute(value, (axis, 'core'), pairs)  59 us
    all_to_all x1, blocking collectives, local(): value = lax.all_to_all(value, ('row', 'zl'), 0, 0, tiled=False)  32.5 us
    all_to_all x1, blocking collectives, local(): value = lax.all_to_all(near.reshape(Y, -1, total), 'y', 0, 0, tiled=False)  31.3 us
    unnamed x70, local copies, waits for them, and re-layouts  29.1 us
    ppermute x12, waiting for transfers between devices, both_ways(): return lax.ppermute(value, (axis, 'core'), pairs)  22.8 us
    pallas_call x2, Pallas kernels, call(): pl.pallas_call(functools.partial(panel_kernel, sources, lanes_of, held),...  5.88 us
    all_to_all x1, starting transfers between devices, share(): return lax.all_to_all(value, 'x', 0, 0, tiled=False)  4.78 us
  transfers between devices with their start and end apart: 14, of which 3 were waited for; matrix products, arithmetic and copies ran while one was open for 1% of the time, Pallas kernels for 2%

profile of v8, /device:TPU:6, one launch (start us, length us, event | category | flops | bytes accessed | tf_op | source)
XLA Modules:
  0.0 195.5 jit_solution(14845914093115689837)
XLA Ops:
  1.3 1.7 split_cells.1
  3.0 9.1 %collective-permute-start = (bf16[512,256]{1,0:T(8,128)(2,1)S(1)}, bf16[512,256]{1,0:T(8,128)(2,1)S(1)}, u32[]{:S(2)}, u32[]{:S(2)}) collective-permute-start(bf16[512,256]{1,0:T(8,128)(2,1)S(1)} %get-tuple-element.12), channel_id=1, source_target_pairs={{0,8},{1,25},{8,16},{9,1},{16,24},{17,9},{24,0},{25,17},{2,10},{3,... | collective-permute-start | bytes 786440 | tf_op jit(solution)/shard_map/ppermute | solution.py:23
  12.1 5.6 %collective-permute-start.4 = (bf16[512,256]{1,0:T(8,128)(2,1)S(1)}, bf16[512,256]{1,0:T(8,128)(2,1)S(1)}, u32[]{:S(2)}, u32[]{:S(2)}) collective-permute-start(bf16[512,256]{1,0:T(8,128)(2,1)S(1)} %get-tuple-element.14), channel_id=1, source_target_pairs={{0,24},{1,9},{8,0},{9,17},{16,8},{17,25},{24,16},{25,1},{2,26},{3,... | collective-permute-start | bytes 786440 | tf_op jit(solution)/shard_map/ppermute | solution.py:23
  17.6 4.8 %all-to-all-start = ((bf16[4,512,256]{2,1,0:T(8,128)(2,1)}), bf16[4,512,256]{2,1,0:T(8,128)(2,1)S(1)}, u32[]{:S(2)}, u32[]{:S(2)}) async-start(bf16[4,512,256]{2,1,0:T(8,128)(2,1)} %get-tuple-element.11), calls=%async_computation | async-start | bytes 2097152 | tf_op jit(solution)/shard_map/all_to_all | solution.py:156
  22.4 3.4 %collective-permute-start.3 = (bf16[512,256]{1,0:T(8,128)(2,1)S(1)}, bf16[512,256]{1,0:T(8,128)(2,1)S(1)}, u32[]{:S(2)}, u32[]{:S(2)}) collective-permute-start(bf16[512,256]{1,0:T(8,128)(2,1)S(1)} %collective-permute-done.refs_1_), channel_id=1, source_target_pairs={{0,4},{1,5},{2,6},{3,7},{4,0},{5,1},{6,2},{7,3},{8,12},{9,13},{10,... | collective-permute-start | bytes 786440 | tf_op jit(solution)/shard_map/ppermute | solution.py:23
  25.8 12.4 %collective-permute-done.4.refs_5_ = bf16[512,256]{1,0:T(8,128)(2,1)S(1)} collective-permute-done((bf16[512,256]{1,0:T(8,128)(2,1)S(1)}, bf16[512,256]{1,0:T(8,128)(2,1)S(1)}, u32[]{:S(2)}, u32[]{:S(2)}) %collective-permute-start.4) | collective-permute-done | bytes 262176 | tf_op jit(solution)/shard_map/ppermute | solution.py:23
  38.2 2.7 %collective-permute-start.2 = (bf16[512,256]{1,0:T(8,128)(2,1)S(1)}, bf16[512,256]{1,0:T(8,128)(2,1)S(1)}, u32[]{:S(2)}, u32[]{:S(2)}) collective-permute-start(bf16[512,256]{1,0:T(8,128)(2,1)S(1)} %collective-permute-done.refs_1_), channel_id=1, source_target_pairs={{0,6},{1,3},{2,0},{3,5},{4,2},{5,7},{6,4},{7,1},{8,14},{9,11},{10,... | collective-permute-start | bytes 786440 | tf_op jit(solution)/shard_map/ppermute | solution.py:23
  40.9 14.4 %collective-permute-start.8 = (bf16[512,256]{1,0:T(8,128)(2,1)S(1)}, bf16[512,256]{1,0:T(8,128)(2,1)S(1)}, u32[]{:S(2)}, u32[]{:S(2)}) collective-permute-start(bf16[512,256]{1,0:T(8,128)(2,1)S(1)} %get-tuple-element.16), channel_id=1, source_target_pairs={{0,16},{1,17},{8,24},{9,25},{16,0},{17,1},{24,8},{25,9},{2,18},{3,... | collective-permute-start | bytes 786440 | tf_op jit(solution)/shard_map/ppermute | solution.py:23
  55.3 5.1 %collective-permute-start.1 = (bf16[512,256]{1,0:T(8,128)(2,1)S(1)}, bf16[512,256]{1,0:T(8,128)(2,1)S(1)}, u32[]{:S(2)}, u32[]{:S(2)}) collective-permute-start(bf16[512,256]{1,0:T(8,128)(2,1)S(1)} %collective-permute-done.refs_1_), channel_id=1, source_target_pairs={{0,2},{1,7},{2,4},{3,1},{4,6},{5,3},{6,0},{7,5},{8,10},{9,15},{10,... | collective-permute-start | bytes 786440 | tf_op jit(solution)/shard_map/ppermute | solution.py:23
  60.5 2.8 %collective-permute-start.7 = (bf16[512,256]{1,0:T(8,128)(2,1)S(1)}, bf16[512,256]{1,0:T(8,128)(2,1)S(1)}, u32[]{:S(2)}, u32[]{:S(2)}) collective-permute-start(bf16[512,256]{1,0:T(8,128)(2,1)S(1)} %collective-permute-done.4.refs_5_), channel_id=1, source_target_pairs={{0,4},{1,5},{2,6},{3,7},{4,0},{5,1},{6,2},{7,3},{8,12},{9,13},{10,... | collective-permute-start | bytes 786440 | tf_op jit(solution)/shard_map/ppermute | solution.py:23
  64.0 2.7 %collective-permute-start.6 = (bf16[512,256]{1,0:T(8,128)(2,1)S(1)}, bf16[512,256]{1,0:T(8,128)(2,1)S(1)}, u32[]{:S(2)}, u32[]{:S(2)}) collective-permute-start(bf16[512,256]{1,0:T(8,128)(2,1)S(1)} %collective-permute-done.4.refs_5_), channel_id=1, source_target_pairs={{0,6},{1,3},{2,0},{3,5},{4,2},{5,7},{6,4},{7,1},{8,14},{9,11},{10,... | collective-permute-start | bytes 786440 | tf_op jit(solution)/shard_map/ppermute | solution.py:23
  67.5 4.3 %collective-permute-start.5 = (bf16[512,256]{1,0:T(8,128)(2,1)S(1)}, bf16[512,256]{1,0:T(8,128)(2,1)S(1)}, u32[]{:S(2)}, u32[]{:S(2)}) collective-permute-start(bf16[512,256]{1,0:T(8,128)(2,1)S(1)} %collective-permute-done.4.refs_5_), channel_id=1, source_target_pairs={{0,2},{1,7},{2,4},{3,1},{4,6},{5,3},{6,0},{7,5},{8,10},{9,15},{10,... | collective-permute-start | bytes 786440 | tf_op jit(solution)/shard_map/ppermute | solution.py:23
  71.8 7.0 %collective-permute-done.8.refs_9_ = bf16[512,256]{1,0:T(8,128)(2,1)S(1)} collective-permute-done((bf16[512,256]{1,0:T(8,128)(2,1)S(1)}, bf16[512,256]{1,0:T(8,128)(2,1)S(1)}, u32[]{:S(2)}, u32[]{:S(2)}) %collective-permute-start.8) | collective-permute-done | bytes 262176 | tf_op jit(solution)/shard_map/ppermute | solution.py:23
  78.8 1.9 collective-permute-start.11
  81.4 4.6 %collective-permute-start.10 = (bf16[512,256]{1,0:T(8,128)(2,1)S(1)}, bf16[512,256]{1,0:T(8,128)(2,1)S(1)}, u32[]{:S(2)}, u32[]{:S(2)}) collective-permute-start(bf16[512,256]{1,0:T(8,128)(2,1)S(1)} %collective-permute-done.8.refs_9_), channel_id=1, source_target_pairs={{0,6},{1,3},{2,0},{3,5},{4,2},{5,7},{6,4},{7,1},{8,14},{9,11},{10,... | collective-permute-start | bytes 786440 | tf_op jit(solution)/shard_map/ppermute | solution.py:23
  86.8 2.5 %collective-permute-start.9 = (bf16[512,256]{1,0:T(8,128)(2,1)S(1)}, bf16[512,256]{1,0:T(8,128)(2,1)S(1)}, u32[]{:S(2)}, u32[]{:S(2)}) collective-permute-start(bf16[512,256]{1,0:T(8,128)(2,1)S(1)} %collective-permute-done.8.refs_9_), channel_id=1, source_target_pairs={{0,2},{1,7},{2,4},{3,1},{4,6},{5,3},{6,0},{7,5},{8,10},{9,15},{10,... | collective-permute-start | bytes 786440 | tf_op jit(solution)/shard_map/ppermute | solution.py:23
  93.0 3.3 %collective-permute-done.10.refs_11_ = bf16[512,256]{1,0:T(8,128)(2,1)S(1)} collective-permute-done((bf16[512,256]{1,0:T(8,128)(2,1)S(1)}, bf16[512,256]{1,0:T(8,128)(2,1)S(1)}, u32[]{:S(2)}, u32[]{:S(2)}) %collective-permute-start.10) | collective-permute-done | bytes 262176 | tf_op jit(solution)/shard_map/ppermute | solution.py:23
  108.2 2.9 %far_panel.1 = f32[256,2048]{1,0:T(8,128)S(1)} custom-call(s32[3]{0:T(128)S(1)} %pad_add_fusion.place, s32[256,1]{1,0:T(8,128)S(1)} %select_n.76.wanted, bf16[4,512,256]{2,1,0:T(8,128)(2,1)S(1)} %all-to-all-done.refs_0_, bf16[512,256]{1,0:T(8,128)(2,1)S(1)} %collective-permute-done.refs_1_, bf16[512,256]{1,0:T(8,128)(2,1)S(1)} %copy-done.13, ...), custom_call_target="tpu_custom_call" | custom-call | flops 1073741824 | bytes 6291456 | tf_op jit(solution)/shard_map/far_panel/pallas_call | solution.py:105
  111.2 1.9 collective-permute-start.12
  124.4 2.9 %near_panel.1 = f32[256,2048]{1,0:T(8,128)S(1)} custom-call(s32[3]{0:T(128)S(1)} %pad_add_fusion.place, s32[256,1]{1,0:T(8,128)S(1)} %select_n.75.wanted, bf16[4,512,256]{2,1,0:T(8,128)(2,1)S(1)} %all-to-all-done.refs_0_, bf16[512,256]{1,0:T(8,128)(2,1)S(1)} %collective-permute-done.refs_1_, bf16[512,256]{1,0:T(8,128)(2,1)S(1)} %copy-done.14, ...), custom_call_target="tpu_custom_call" | custom-call | flops 1073741824 | bytes 6291456 | tf_op jit(solution)/shard_map/near_panel/pallas_call | solution.py:105
  127.3 1.9 add.24
  129.2 31.3 %all_to_all.15.value = f32[4,64,2048]{2,1,0:T(8,128)S(1)} all-to-all(f32[4,64,2048]{2,1,0:T(8,128)S(1)} %bitcast.12), channel_id=1, replica_groups=mesh['y'=4,'zl'=4,'row'=4,'x'=4,'core'=2] {'y'}, dimensions={0} | all-to-all | bytes 4194304 | tf_op jit(solution)/shard_map/all_to_all | solution.py:187
  160.5 1.8 arrange_rows.1
  162.3 32.5 %all_to_all.16 = f32[16,16,512]{2,1,0:T(8,128)S(1)} all-to-all(f32[16,16,512]{2,1,0:T(8,128)S(1)} %arrange_rows.1), channel_id=1, replica_groups=mesh['y'=4,'zl'=4,'row'=4,'x'=4,'core'=2] {'row','zl'}, dimensions={0} | all-to-all | bytes 1048576 | tf_op jit(solution)/shard_map/all_to_all | solution.py:189
  (90 shorter events, 31.6 us)
Async XLA Ops:
  0.0 89.9 %copy-start.34 = (s32[2048]{0:T(1024)S(1)}, s32[2048]{0:T(1024)}, u32[]{:S(2)}) copy-start(s32[2048]{0:T(1024)} %param.3) | copy-start | bytes 24580
  0.1 1.2 copy-start.33
  3.0 19.4 %collective-permute-start = (bf16[512,256]{1,0:T(8,128)(2,1)S(1)}, bf16[512,256]{1,0:T(8,128)(2,1)S(1)}, u32[]{:S(2)}, u32[]{:S(2)}) collective-permute-start(bf16[512,256]{1,0:T(8,128)(2,1)S(1)} %get-tuple-element.12), channel_id=1, source_target_pairs={{0,8},{1,25},{8,16},{9,1},{16,24},{17,9},{24,0},{25,17},{2,10},{3,... | collective-permute-start | bytes 786440 | tf_op jit(solution)/shard_map/ppermute | solution.py:23
  12.1 26.1 %collective-permute-start.4 = (bf16[512,256]{1,0:T(8,128)(2,1)S(1)}, bf16[512,256]{1,0:T(8,128)(2,1)S(1)}, u32[]{:S(2)}, u32[]{:S(2)}) collective-permute-start(bf16[512,256]{1,0:T(8,128)(2,1)S(1)} %get-tuple-element.14), channel_id=1, source_target_pairs={{0,24},{1,9},{8,0},{9,17},{16,8},{17,25},{24,16},{25,1},{2,26},{3,... | collective-permute-start | bytes 786440 | tf_op jit(solution)/shard_map/ppermute | solution.py:23
  17.6 80.1 %all-to-all-start = ((bf16[4,512,256]{2,1,0:T(8,128)(2,1)}), bf16[4,512,256]{2,1,0:T(8,128)(2,1)S(1)}, u32[]{:S(2)}, u32[]{:S(2)}) async-start(bf16[4,512,256]{2,1,0:T(8,128)(2,1)} %get-tuple-element.11), calls=%async_computation | async-start | bytes 2097152 | tf_op jit(solution)/shard_map/all_to_all | solution.py:156
  22.4 40.9 %collective-permute-start.3 = (bf16[512,256]{1,0:T(8,128)(2,1)S(1)}, bf16[512,256]{1,0:T(8,128)(2,1)S(1)}, u32[]{:S(2)}, u32[]{:S(2)}) collective-permute-start(bf16[512,256]{1,0:T(8,128)(2,1)S(1)} %collective-permute-done.refs_1_), channel_id=1, source_target_pairs={{0,4},{1,5},{2,6},{3,7},{4,0},{5,1},{6,2},{7,3},{8,12},{9,13},{10,... | collective-permute-start | bytes 786440 | tf_op jit(solution)/shard_map/ppermute | solution.py:23
  38.2 58.9 %copy-start = (bf16[512,256]{1,0:T(8,128)(2,1)}, bf16[512,256]{1,0:T(8,128)(2,1)S(1)}, u32[]{:S(2)}) copy-start(bf16[512,256]{1,0:T(8,128)(2,1)S(1)} %collective-permute-done.4.refs_5_) | copy-start | bytes 786436
  38.2 28.6 %collective-permute-start.2 = (bf16[512,256]{1,0:T(8,128)(2,1)S(1)}, bf16[512,256]{1,0:T(8,128)(2,1)S(1)}, u32[]{:S(2)}, u32[]{:S(2)}) collective-permute-start(bf16[512,256]{1,0:T(8,128)(2,1)S(1)} %collective-permute-done.refs_1_), channel_id=1, source_target_pairs={{0,6},{1,3},{2,0},{3,5},{4,2},{5,7},{6,4},{7,1},{8,14},{9,11},{10,... | collective-permute-start | bytes 786440 | tf_op jit(solution)/shard_map/ppermute | solution.py:23
  40.9 37.9 %collective-permute-start.8 = (bf16[512,256]{1,0:T(8,128)(2,1)S(1)}, bf16[512,256]{1,0:T(8,128)(2,1)S(1)}, u32[]{:S(2)}, u32[]{:S(2)}) collective-permute-start(bf16[512,256]{1,0:T(8,128)(2,1)S(1)} %get-tuple-element.16), channel_id=1, source_target_pairs={{0,16},{1,17},{8,24},{9,25},{16,0},{17,1},{24,8},{25,9},{2,18},{3,... | collective-permute-start | bytes 786440 | tf_op jit(solution)/shard_map/ppermute | solution.py:23
  55.3 25.4 %collective-permute-start.1 = (bf16[512,256]{1,0:T(8,128)(2,1)S(1)}, bf16[512,256]{1,0:T(8,128)(2,1)S(1)}, u32[]{:S(2)}, u32[]{:S(2)}) collective-permute-start(bf16[512,256]{1,0:T(8,128)(2,1)S(1)} %collective-permute-done.refs_1_), channel_id=1, source_target_pairs={{0,2},{1,7},{2,4},{3,1},{4,6},{5,3},{6,0},{7,5},{8,10},{9,15},{10,... | collective-permute-start | bytes 786440 | tf_op jit(solution)/shard_map/ppermute | solution.py:23
  60.5 25.6 %collective-permute-start.7 = (bf16[512,256]{1,0:T(8,128)(2,1)S(1)}, bf16[512,256]{1,0:T(8,128)(2,1)S(1)}, u32[]{:S(2)}, u32[]{:S(2)}) collective-permute-start(bf16[512,256]{1,0:T(8,128)(2,1)S(1)} %collective-permute-done.4.refs_5_), channel_id=1, source_target_pairs={{0,4},{1,5},{2,6},{3,7},{4,0},{5,1},{6,2},{7,3},{8,12},{9,13},{10,... | collective-permute-start | bytes 786440 | tf_op jit(solution)/shard_map/ppermute | solution.py:23
  64.0 26.9 %collective-permute-start.6 = (bf16[512,256]{1,0:T(8,128)(2,1)S(1)}, bf16[512,256]{1,0:T(8,128)(2,1)S(1)}, u32[]{:S(2)}, u32[]{:S(2)}) collective-permute-start(bf16[512,256]{1,0:T(8,128)(2,1)S(1)} %collective-permute-done.4.refs_5_), channel_id=1, source_target_pairs={{0,6},{1,3},{2,0},{3,5},{4,2},{5,7},{6,4},{7,1},{8,14},{9,11},{10,... | collective-permute-start | bytes 786440 | tf_op jit(solution)/shard_map/ppermute | solution.py:23
  67.5 24.1 %collective-permute-start.5 = (bf16[512,256]{1,0:T(8,128)(2,1)S(1)}, bf16[512,256]{1,0:T(8,128)(2,1)S(1)}, u32[]{:S(2)}, u32[]{:S(2)}) collective-permute-start(bf16[512,256]{1,0:T(8,128)(2,1)S(1)} %collective-permute-done.4.refs_5_), channel_id=1, source_target_pairs={{0,2},{1,7},{2,4},{3,1},{4,6},{5,3},{6,0},{7,5},{8,10},{9,15},{10,... | collective-permute-start | bytes 786440 | tf_op jit(solution)/shard_map/ppermute | solution.py:23
  78.8 13.5 %collective-permute-start.11 = (bf16[512,256]{1,0:T(8,128)(2,1)S(1)}, bf16[512,256]{1,0:T(8,128)(2,1)S(1)}, u32[]{:S(2)}, u32[]{:S(2)}) collective-permute-start(bf16[512,256]{1,0:T(8,128)(2,1)S(1)} %collective-permute-done.8.refs_9_), channel_id=1, source_target_pairs={{0,4},{1,5},{2,6},{3,7},{4,0},{5,1},{6,2},{7,3},{8,12},{9,13},{10,... | collective-permute-start | bytes 786440 | tf_op jit(solution)/shard_map/ppermute | solution.py:23
  81.4 14.9 %collective-permute-start.10 = (bf16[512,256]{1,0:T(8,128)(2,1)S(1)}, bf16[512,256]{1,0:T(8,128)(2,1)S(1)}, u32[]{:S(2)}, u32[]{:S(2)}) collective-permute-start(bf16[512,256]{1,0:T(8,128)(2,1)S(1)} %collective-permute-done.8.refs_9_), channel_id=1, source_target_pairs={{0,6},{1,3},{2,0},{3,5},{4,2},{5,7},{6,4},{7,1},{8,14},{9,11},{10,... | collective-permute-start | bytes 786440 | tf_op jit(solution)/shard_map/ppermute | solution.py:23
  86.8 10.3 %collective-permute-start.9 = (bf16[512,256]{1,0:T(8,128)(2,1)S(1)}, bf16[512,256]{1,0:T(8,128)(2,1)S(1)}, u32[]{:S(2)}, u32[]{:S(2)}) collective-permute-start(bf16[512,256]{1,0:T(8,128)(2,1)S(1)} %collective-permute-done.8.refs_9_), channel_id=1, source_target_pairs={{0,2},{1,7},{2,4},{3,1},{4,6},{5,3},{6,0},{7,5},{8,10},{9,15},{10,... | collective-permute-start | bytes 786440 | tf_op jit(solution)/shard_map/ppermute | solution.py:23
  97.8 1.0 copy-start.1
  98.7 0.9 copy-start.4
  99.7 0.9 copy-start.7
  100.6 0.9 copy-start.10
  101.6 0.9 copy-start.13
  102.5 0.9 copy-start.16
  111.2 16.1 %collective-permute-start.12 = (f32[256,2048]{1,0:T(8,128)S(1)}, f32[256,2048]{1,0:T(8,128)}, u32[]{:S(2)}, u32[]{:S(2)}) collective-permute-start(f32[256,2048]{1,0:T(8,128)S(1)} %far_panel.1), channel_id=1, source_target_pairs={{0,1},{1,0},{2,3},{3,2},{4,5},{5,4},{6,7},{7,6},{8,9},{9,8},{10,11... | collective-permute-start | bytes 6291464 | tf_op jit(solution)/shard_map/ppermute | solution.py:186
  113.9 1.0 copy-start.2
  (25 other events, 21.3 us)
